TPU v7x, 512 devices: a whole 4x8x8 slice. The times are simulated.
512 devices in a mesh: outer: 8 (over z_hi, x), inner: 64 (over y, z_lo, core).
Axes of the slice: x: 4, y: 8, z: 8 (z_hi: 2, z_lo: 4; z = z_hi * 4 + z_lo), core: 2. Of those that a mesh axis runs over, the one named last changes fastest.
Arguments:
- positions: float32 [3, 262144], P(None, ('outer', 'inner')), may hold values from 0 to 3.4
- species: int32 [262144], P(('outer', 'inner')), may hold values from 0 to 6
- send_lists: int32 [8, 90112], P(None, ('outer', 'inner')), may hold values from 0 to 511, as said below
- centers: int32 [393216], P(('outer', 'inner')), may hold values from 0 to 511
- neighbours: int32 [393216], P(('outer', 'inner')), may hold values from 0 to 1919, as said below
- live_blocks: int32 [512], P(('outer', 'inner')), may hold values from 1 to 6
- w_rad: float32 [8, 128], replicated, may hold values from -2 to 2
- emb_center: bfloat16 [7, 128], replicated, may hold values from -5 to 5
- emb_neigh: bfloat16 [7, 128], replicated, may hold values from -5 to 5
- w_env: bfloat16 [128, 192], replicated, may hold values from -0.5 to 0.5
- w_lat: bfloat16 [320, 128], replicated, may hold values from -0.3125 to 0.3125
- w_out: bfloat16 [128], replicated, may hold values from -0.5 to 0.5
Outputs:
- forces: float32 [3, 262144], P(None, ('outer', 'inner'))
- atom_energy: float32 [262144], P(('outer', 'inner'))
Inputs may be any that keep to these rules, and one draw needn't show every extreme that they name: `neighbours`: within the 768 pair slots of one domain no two share a neighbour index; values below 512 are local atoms, value 512 + k * 176 + s is entry s of ghost direction k. `send_lists`: each send list of one domain and one direction names 176 distinct local atoms.
All inputs are finite; a program needn't handle non-finite values.
Results may differ from a plain program's by a relative error of at most 0.013.
Values sent between devices are 32-bit elements; how exact they have to be, the bound alone decides.
No kernel may reach another device: no remote copies, remote signals or barrier semaphores. Data moves between devices by JAX's collectives and lax.ppermute only.
A program may use at most 64 MiB of HBM per device.

v0:
```python
import math

import jax
import jax.numpy as jnp
from jax import lax
from jax.sharding import PartitionSpec as P

DIRS = ((-1, -1), (-1, 0), (-1, 1), (0, -1), (0, 1), (1, -1), (1, 0), (1, 1))
CUTOFF = 6.0
TP_SCALE = 2.0
ROOT3 = math.sqrt(3.0)
ROOT5 = math.sqrt(5.0)
ROOT15 = math.sqrt(15.0)


def from_behind(block, axis, distance):
    devices = range(lax.axis_size(axis))
    route = [((i - distance) % len(devices), i) for i in devices]
    return lax.ppermute(block, axis, route)


def harmonics(unit_vec):
    comp_x, comp_y, comp_z = (unit_vec[0], unit_vec[1], unit_vec[2])
    length_sq = comp_x * comp_x + comp_y * comp_y + comp_z * comp_z
    return jnp.stack(
        [
            jnp.ones_like(comp_x),
            ROOT3 * comp_x,
            ROOT3 * comp_y,
            ROOT3 * comp_z,
            ROOT15 * comp_x * comp_y,
            ROOT15 * comp_y * comp_z,
            0.5 * ROOT5 * (3.0 * comp_z * comp_z - length_sq),
            ROOT15 * comp_x * comp_z,
            0.5 * ROOT15 * (comp_x * comp_x - comp_y * comp_y),
        ],
        0,
    )


def pair_front(
    displace, onehot_center, onehot_neigh, live_mask, w_rad, emb_center, emb_neigh, w_env
):
    squared = jnp.sum(displace * displace, axis=0) + 1.0
    distance = jnp.sqrt(squared)
    unit_vec = displace / distance
    envelope = (1.0 - squared / (CUTOFF * CUTOFF)) ** 2
    orders = jnp.arange(1, w_rad.shape[0] + 1).astype(jnp.float32)
    basis = jnp.sin(orders[:, None] * distance[None, :] * (math.pi / CUTOFF)) / distance * envelope
    preact = jnp.dot(basis.T, w_rad, precision=lax.Precision.HIGHEST)
    preact = preact + jnp.dot(onehot_center, emb_center, preferred_element_type=jnp.float32)
    preact = preact + jnp.dot(onehot_neigh, emb_neigh, preferred_element_type=jnp.float32)
    latent = jax.nn.silu(preact)
    latent_half = latent.astype(jnp.bfloat16)
    scaled = envelope * live_mask
    env_weight = jnp.dot(latent_half, w_env, preferred_element_type=jnp.float32) * scaled[:, None]
    return (latent, latent_half, env_weight, harmonics(unit_vec), scaled)


def spread(env_weight, harmonic):
    feat = env_weight.shape[1] // 3
    rows = harmonic.T
    pieces = [
        env_weight[:, 0:feat][:, None, :] * rows[:, 0:1, None],
        env_weight[:, feat : 2 * feat][:, None, :] * rows[:, 1:4, None],
        env_weight[:, 2 * feat :][:, None, :] * rows[:, 4:9, None],
    ]
    return jnp.concatenate(pieces, axis=1).reshape(rows.shape[0], 9 * feat)


def pair_energy(
    displace,
    gathered,
    onehot_center,
    onehot_neigh,
    live_mask,
    w_rad,
    emb_center,
    emb_neigh,
    w_env,
    w_lat,
    w_out,
):
    latent, latent_half, env_weight, harmonic, scaled = pair_front(
        displace, onehot_center, onehot_neigh, live_mask, w_rad, emb_center, emb_neigh, w_env
    )
    feat = env_weight.shape[1] // 3
    rows = harmonic.T
    mixed = gathered.reshape(rows.shape[0], 9, feat) * rows[:, :, None]
    invariant = (
        jnp.concatenate(
            [
                jnp.sum(mixed[:, 0:1], axis=1),
                jnp.sum(mixed[:, 1:4], axis=1),
                jnp.sum(mixed[:, 4:9], axis=1),
            ],
            axis=1,
        )
        * env_weight
        * TP_SCALE
    )
    joined = jnp.concatenate([latent_half, invariant.astype(jnp.bfloat16)], axis=1)
    update = jax.nn.silu(jnp.dot(joined, w_lat, preferred_element_type=jnp.float32))
    refined = (latent + update).astype(jnp.bfloat16)
    return scaled * jnp.dot(refined, w_out, preferred_element_type=jnp.float32)


def send_outer(stacked, offset):
    return from_behind(stacked, "outer", offset)


def send_inner(stacked, offset):
    return from_behind(stacked, "inner", offset)


def return_outer(stacked, offset):
    return from_behind(stacked, "outer", offset)


def return_inner(stacked, offset):
    return from_behind(stacked, "inner", offset)


def outer_slot(leading, trailing):
    return DIRS.index((leading, trailing))


def route_forward(outgoing, lead_shift, trail_shift, slot_of):
    landed = {}
    passed = {}
    for leading in (1, -1):
        stacked = jnp.stack([outgoing[slot_of(leading, trailing)] for trailing in (-1, 0, 1)])
        arrived = lead_shift(stacked, leading)
        landed[slot_of(leading, 0)] = arrived[1]
        passed[leading, -1] = arrived[0]
        passed[leading, 1] = arrived[2]
    for trailing in (1, -1):
        stacked = jnp.stack(
            [outgoing[slot_of(0, trailing)], passed[1, trailing], passed[-1, trailing]]
        )
        arrived = trail_shift(stacked, trailing)
        landed[slot_of(0, trailing)] = arrived[0]
        landed[slot_of(1, trailing)] = arrived[1]
        landed[slot_of(-1, trailing)] = arrived[2]
    return jnp.concatenate([landed[listed] for listed in range(8)], axis=1)


def route_back(ghost_terms, send_len, lead_shift, trail_shift, slot_of):
    pieces = [ghost_terms[:, listed * send_len : (listed + 1) * send_len] for listed in range(8)]
    returned = {}
    carried = {}
    for trailing in (1, -1):
        stacked = jnp.stack(
            [
                pieces[slot_of(0, trailing)],
                pieces[slot_of(1, trailing)],
                pieces[slot_of(-1, trailing)],
            ]
        )
        arrived = trail_shift(stacked, -trailing)
        returned[slot_of(0, trailing)] = arrived[0]
        carried[1, trailing] = arrived[1]
        carried[-1, trailing] = arrived[2]
    for leading in (1, -1):
        stacked = jnp.stack(
            [carried[leading, -1], pieces[slot_of(leading, 0)], carried[leading, 1]]
        )
        arrived = lead_shift(stacked, -leading)
        returned[slot_of(leading, -1)] = arrived[0]
        returned[slot_of(leading, 0)] = arrived[1]
        returned[slot_of(leading, 1)] = arrived[2]
    return jnp.concatenate([returned[listed] for listed in range(8)], axis=1)


def device_terms(
    comb_pos,
    comb_spec,
    center_ids,
    neighbour_ids,
    live_mask,
    atom_count,
    w_rad,
    emb_center,
    emb_neigh,
    w_env,
    w_lat,
    w_out,
):
    pair_len = center_ids.shape[0]
    block_len = math.gcd(pair_len, 1024)
    blocks = pair_len // block_len
    spec_count = emb_center.shape[0]
    width = 3 * w_env.shape[1]
    kinds = jnp.arange(spec_count).astype(jnp.float32)
    onehot_center = (comb_spec[center_ids][:, None] == kinds[None, :]).astype(jnp.bfloat16)
    onehot_neigh = (comb_spec[neighbour_ids][:, None] == kinds[None, :]).astype(jnp.bfloat16)
    displace = comb_pos[:, neighbour_ids] - comb_pos[:, center_ids]
    items = (
        jnp.transpose(displace.reshape(3, blocks, block_len), (1, 0, 2)),
        center_ids.reshape(blocks, block_len),
        onehot_center.reshape(blocks, block_len, spec_count),
        onehot_neigh.reshape(blocks, block_len, spec_count),
        live_mask.reshape(blocks, block_len),
    )

    def contrib(moved, block_center, block_neigh, block_live):
        _, _, env_weight, harmonic, _ = pair_front(
            moved, block_center, block_neigh, block_live, w_rad, emb_center, emb_neigh, w_env
        )
        return spread(env_weight, harmonic)

    def accumulate(env_sum, item):
        moved, block_ids, block_center, block_neigh, block_live = item
        return (
            env_sum.at[block_ids].add(contrib(moved, block_center, block_neigh, block_live)),
            None,
        )

    env_sum, _ = lax.scan(accumulate, jnp.zeros((atom_count, width), jnp.float32), items)

    def energy_pass(d_env, item):
        moved, block_ids, block_center, block_neigh, block_live = item

        def energy_of(shifted, gathered):
            return pair_energy(
                shifted,
                gathered,
                block_center,
                block_neigh,
                block_live,
                w_rad,
                emb_center,
                emb_neigh,
                w_env,
                w_lat,
                w_out,
            )

        pair_vals, pull_back = jax.vjp(energy_of, moved, env_sum[block_ids])
        d_first, d_gather = pull_back(jnp.ones_like(pair_vals))
        return (d_env.at[block_ids].add(d_gather), (pair_vals, d_first))

    d_env, (pair_vals, d_firsts) = lax.scan(
        energy_pass, jnp.zeros((atom_count, width), jnp.float32), items
    )

    def geometry_pass(unused, item):
        moved, block_ids, block_center, block_neigh, block_live = item

        def local_contrib(shifted):
            return contrib(shifted, block_center, block_neigh, block_live)

        _, pull_back = jax.vjp(local_contrib, moved)
        return (unused, pull_back(d_env[block_ids])[0])

    _, d_seconds = lax.scan(geometry_pass, jnp.zeros((), jnp.float32), items)
    d_displace = jnp.transpose(d_firsts + d_seconds, (1, 0, 2)).reshape(3, pair_len)
    energies = pair_vals.reshape(pair_len)
    slots_total = comb_pos.shape[1]
    gradient = (
        jnp.zeros((3, slots_total), jnp.float32)
        .at[:, neighbour_ids]
        .add(d_displace)
        .at[:, center_ids]
        .add(-d_displace)
    )
    shares = (
        jnp.zeros((slots_total,), jnp.float32)
        .at[neighbour_ids]
        .add(0.5 * energies)
        .at[center_ids]
        .add(0.5 * energies)
    )
    return jnp.concatenate([-gradient, shares[None, :]], axis=0)


def on_device(
    positions,
    species,
    send_lists,
    centers,
    neighbours,
    live_blocks,
    w_rad,
    emb_center,
    emb_neigh,
    w_env,
    w_lat,
    w_out,
):
    atom_count = positions.shape[1]
    send_len = send_lists.shape[1]
    pair_len = centers.shape[0]
    packed = jnp.concatenate([positions, species.astype(jnp.float32)[None, :]], axis=0)
    outgoing = jnp.transpose(jnp.take(packed, send_lists, axis=1), (1, 0, 2))
    ghosts = route_forward(outgoing, send_outer, send_inner, outer_slot)
    combined = jnp.concatenate([packed, ghosts], axis=1)
    live_mask = (jnp.arange(pair_len) // 128 < live_blocks[0]).astype(jnp.float32)
    terms = device_terms(
        combined[0:3],
        combined[3],
        centers,
        neighbours,
        live_mask,
        atom_count,
        w_rad,
        emb_center,
        emb_neigh,
        w_env,
        w_lat,
        w_out,
    )
    arrivals = route_back(terms[:, atom_count:], send_len, return_outer, return_inner, outer_slot)
    local_terms = terms[:, :atom_count].at[:, send_lists.reshape(-1)].add(arrivals)
    return (local_terms[0:3], local_terms[3])


def solution(mesh):
    return jax.shard_map(
        on_device,
        mesh=mesh,
        in_specs=(
            P(None, ("outer", "inner")),
            P(("outer", "inner")),
            P(None, ("outer", "inner")),
            P(("outer", "inner")),
            P(("outer", "inner")),
            P(("outer", "inner")),
            P(),
            P(),
            P(),
            P(),
            P(),
            P(),
        ),
        out_specs=(P(None, ("outer", "inner")), P(("outer", "inner"))),
        check_vma=False,
    )
```

profile of v0, /device:TPU:6, one launch (start us, length us, event | category | flops | bytes accessed | tf_op | source)
XLA Modules:
  0.0 182.2 jit_solution(10028950065046412630)
XLA Ops:
  3.8 2.7 %gather_fusion.2 = f32[1408,4]{1,0:T(8,128)S(1)} fusion(f32[4,512]{0,1:T(8,128)S(1)} %copy.83, s32[2048]{0:T(1024)S(1)} %pad_clamp_fusion.2), kind=kCustom, calls=%fused_computation.2 | custom fusion | bytes 50688 | tf_op jit(solution)/shard_map/jit(_take)/gather | solution.py:295
  6.8 10.8 %collective-permute-start = (f32[3,4,176]{2,1,0:T(4,128)S(1)}, f32[3,4,176]{2,1,0:T(4,128)S(1)}, u32[]{:S(2)}, u32[]{:S(2)}) collective-permute-start(f32[3,4,176]{2,1,0:T(4,128)S(1)} %get-tuple-element.390), channel_id=1, source_target_pairs={{448,0},{0,64},{64,128},{128,192},{192,256},{256,320},{320,384},{3... | collective-permute-start | bytes 25352 | tf_op jit(solution)/shard_map/ppermute | solution.py:19
  17.7 1.9 %collective-permute-start.1 = (f32[3,4,176]{2,1,0:T(4,128)S(1)}, f32[3,4,176]{2,1,0:T(4,128)S(1)}, u32[]{:S(2)}, u32[]{:S(2)}) collective-permute-start(f32[3,4,176]{2,1,0:T(4,128)S(1)} %get-tuple-element.391), channel_id=1, source_target_pairs={{64,0},{128,64},{192,128},{256,192},{320,256},{384,320},{448,384},... | collective-permute-start | bytes 25352 | tf_op jit(solution)/shard_map/ppermute | solution.py:19
  20.5 8.8 %collective-permute-done.1 = f32[3,4,176]{2,1,0:T(4,128)S(1)} collective-permute-done((f32[3,4,176]{2,1,0:T(4,128)S(1)}, f32[3,4,176]{2,1,0:T(4,128)S(1)}, u32[]{:S(2)}, u32[]{:S(2)}) %collective-permute-start.1) | collective-permute-done | bytes 8480 | tf_op jit(solution)/shard_map/ppermute | solution.py:19
  29.3 6.1 %collective-permute-start.2 = (f32[3,4,176]{2,1,0:T(4,128)S(1)}, f32[3,4,176]{2,1,0:T(4,128)S(1)}, u32[]{:S(2)}, u32[]{:S(2)}) collective-permute-start(f32[3,4,176]{2,1,0:T(4,128)S(1)} %pad_maximum_fusion.2), channel_id=1, source_target_pairs={{1,0},{2,1},{3,2},{4,3},{5,4},{6,5},{7,6},{8,7},{9,8},{10,9},{11,1... | collective-permute-start | bytes 25352 | tf_op jit(solution)/shard_map/ppermute | solution.py:19
  35.4 1.9 %collective-permute-start.3 = (f32[3,4,176]{2,1,0:T(4,128)S(1)}, f32[3,4,176]{2,1,0:T(4,128)S(1)}, u32[]{:S(2)}, u32[]{:S(2)}) collective-permute-start(f32[3,4,176]{2,1,0:T(4,128)S(1)} %pad_maximum_fusion.3), channel_id=1, source_target_pairs={{63,0},{0,1},{1,2},{2,3},{3,4},{4,5},{5,6},{6,7},{7,8},{8,9},{9,10... | collective-permute-start | bytes 25352 | tf_op jit(solution)/shard_map/ppermute | solution.py:19
  37.4 7.0 %collective-permute-done.3 = f32[3,4,176]{2,1,0:T(4,128)S(1)} collective-permute-done((f32[3,4,176]{2,1,0:T(4,128)S(1)}, f32[3,4,176]{2,1,0:T(4,128)S(1)}, u32[]{:S(2)}, u32[]{:S(2)}) %collective-permute-start.3) | collective-permute-done | bytes 8480 | tf_op jit(solution)/shard_map/ppermute | solution.py:19
  44.5 4.5 %gather_fusion.6 = f32[768]{0:T(1024)S(1)} fusion(f32[1920]{0:T(1024)S(1)} %slice_reduce_fusion.3, s32[1024]{0:T(1024)S(1)} %pad_clamp_fusion.4), kind=kCustom, calls=%fused_computation.6 | custom fusion | bytes 9216 | tf_op jit(solution)/shard_map/gather | solution.py:196
  49.0 4.5 %gather_fusion.5 = f32[768]{0:T(1024)S(1)} fusion(f32[1920]{0:T(1024)S(1)} %slice_reduce_fusion.3, s32[1024]{0:T(1024)S(1)} %pad_clamp_fusion.3), kind=kCustom, calls=%fused_computation.5 | custom fusion | bytes 9216 | tf_op jit(solution)/shard_map/gather | solution.py:195
  53.8 1.6 gather_fusion.4
  55.4 1.6 gather_fusion.3
  57.8 13.5 %while.34 = (s32[]{:T(128)}, f32[512,576]{1,0:T(8,128)S(1)}, s32[3,256]{1,0:T(4,128)S(1)}, f32[3,3,256]{2,1,0:T(4,128)S(1)}, f32[8,128]{1,0:T(8,128)S(1)}, /*ind...) while((s32[]{:T(128)}, f32[512,576]{1,0:T(8,128)S(1)}, ...), condition=%wide.region_3.4_spmd, body=%wide.region_0.3_spmd.sunk | while | flops 17531664 | bytes 6046945 | solution.py:219
  59.6 2.7 %scatter_fusion = f32[512,576]{1,0:T(8,128)S(1)} fusion(f32[512,576]{1,0:T(8,128)S(1)} %get-tuple-element.811, s32[256]{0:T(256)S(1)} %bitcast.355, f32[256,576]{1,0:T(8,128)S(1)} %copy.100), kind=kCustom, calls=%fused_computation.7.clone.1 | custom fusion | flops 147456 | bytes 1770496 | tf_op jit(solution)/shard_map/while/body/eval_jaxpr/scatter-add | solution.py:215
  64.0 2.7 %scatter_fusion = f32[512,576]{1,0:T(8,128)S(1)} fusion(f32[512,576]{1,0:T(8,128)S(1)} %get-tuple-element.811, s32[256]{0:T(256)S(1)} %bitcast.355, f32[256,576]{1,0:T(8,128)S(1)} %copy.100), kind=kCustom, calls=%fused_computation.7.clone.1 | custom fusion | flops 147456 | bytes 1770496 | tf_op jit(solution)/shard_map/while/body/eval_jaxpr/scatter-add | solution.py:215
  68.5 2.7 %scatter_fusion = f32[512,576]{1,0:T(8,128)S(1)} fusion(f32[512,576]{1,0:T(8,128)S(1)} %get-tuple-element.811, s32[256]{0:T(256)S(1)} %bitcast.355, f32[256,576]{1,0:T(8,128)S(1)} %copy.100), kind=kCustom, calls=%fused_computation.7.clone.1 | custom fusion | flops 147456 | bytes 1770496 | tf_op jit(solution)/shard_map/while/body/eval_jaxpr/scatter-add | solution.py:215
  72.2 39.1 %while.35 = (s32[]{:T(128)}, f32[512,576]{1,0:T(8,128)S(1)}, f32[3,256]{1,0:T(4,128)S(1)}, f32[3,3,256]{2,1,0:T(4,128)S(1)}, s32[3,256]{1,0:T(4,128)S(1)}, /*ind...) while((s32[]{:T(128)}, f32[512,576]{1,0:T(8,128)S(1)}, ...), condition=%wide.region_15.16_spmd, body=%wide.region_4.15_spmd.sunk | while | flops 78497448 | bytes 14634577 | solution.py:243
  74.9 1.9 %gather_fusion = f32[256,576]{1,0:T(8,128)} fusion(f32[512,576]{1,0:T(8,128)S(1)} %get-tuple-element.887, s32[1024]{0:T(1024)S(1)} %pad_clamp_fusion.7), kind=kCustom, calls=%fused_computation.clone.1 | custom fusion | bytes 1180672 | tf_op jit(solution)/shard_map/while/body/eval_jaxpr/gather | solution.py:239
  76.8 1.3 copy.101
  80.1 0.9 multiply_reduce_fusion.21
  81.2 1.3 copy.102
  82.5 2.7 %scatter_fusion.1 = f32[512,576]{1,0:T(8,128)S(1)} fusion(f32[512,576]{1,0:T(8,128)S(1)} %get-tuple-element.856, s32[256]{0:T(256)S(1)} %bitcast.347, f32[256,576]{1,0:T(8,128)S(1)} %copy.102), kind=kCustom, calls=%fused_computation.8.clone.1 | custom fusion | flops 147456 | bytes 1770496 | tf_op jit(solution)/shard_map/while/body/eval_jaxpr/scatter-add | solution.py:241
  87.1 0.9 fusion.276
  87.9 1.9 %gather_fusion = f32[256,576]{1,0:T(8,128)} fusion(f32[512,576]{1,0:T(8,128)S(1)} %get-tuple-element.887, s32[1024]{0:T(1024)S(1)} %pad_clamp_fusion.7), kind=kCustom, calls=%fused_computation.clone.1 | custom fusion | bytes 1180672 | tf_op jit(solution)/shard_map/while/body/eval_jaxpr/gather | solution.py:239
  89.8 1.3 copy.101
  93.2 0.9 multiply_reduce_fusion.21
  94.2 1.3 copy.102
  95.5 2.7 %scatter_fusion.1 = f32[512,576]{1,0:T(8,128)S(1)} fusion(f32[512,576]{1,0:T(8,128)S(1)} %get-tuple-element.856, s32[256]{0:T(256)S(1)} %bitcast.347, f32[256,576]{1,0:T(8,128)S(1)} %copy.102), kind=kCustom, calls=%fused_computation.8.clone.1 | custom fusion | flops 147456 | bytes 1770496 | tf_op jit(solution)/shard_map/while/body/eval_jaxpr/scatter-add | solution.py:241
  100.1 0.9 fusion.276
  101.0 1.9 %gather_fusion = f32[256,576]{1,0:T(8,128)} fusion(f32[512,576]{1,0:T(8,128)S(1)} %get-tuple-element.887, s32[1024]{0:T(1024)S(1)} %pad_clamp_fusion.7), kind=kCustom, calls=%fused_computation.clone.1 | custom fusion | bytes 1180672 | tf_op jit(solution)/shard_map/while/body/eval_jaxpr/gather | solution.py:239
  102.9 1.3 copy.101
  106.2 0.9 multiply_reduce_fusion.21
  107.3 1.3 copy.102
  108.6 2.7 %scatter_fusion.1 = f32[512,576]{1,0:T(8,128)S(1)} fusion(f32[512,576]{1,0:T(8,128)S(1)} %get-tuple-element.856, s32[256]{0:T(256)S(1)} %bitcast.347, f32[256,576]{1,0:T(8,128)S(1)} %copy.102), kind=kCustom, calls=%fused_computation.8.clone.1 | custom fusion | flops 147456 | bytes 1770496 | tf_op jit(solution)/shard_map/while/body/eval_jaxpr/scatter-add | solution.py:241
  111.3 10.9 %while.36 = (s32[]{:T(128)}, f32[3,3,256]{2,1,0:T(4,128)S(1)}, f32[3,3,256]{2,1,0:T(4,128)S(1)}, f32[8,128]{1,0:T(8,128)S(1)}, bf16[3,256,7]{1,2,0:T(8,128)(2,1)...) while((s32[]{:T(128)}, f32[3,3,256]{2,1,0:T(4,128)S(1)}, ...), condition=%wide.region_28.29_spmd, body=%wide.region_16.28_spmd.sunk | while | flops 33969704 | bytes 6062417 | solution.py:256
  112.7 1.1 gather_fusion.1
  116.4 1.1 gather_fusion.1
  120.0 1.1 gather_fusion.1
  122.2 4.6 %scatter_custom_fusion.4 = f32[1920]{0:T(1024)S(1)} fusion(s32[768]{0:T(1024)S(1)} %compare_select_fusion.6, f32[768]{0:T(1024)S(1)} %reshape.448, f32[]{:T(128)} %constant.169.clone.1), kind=kCustom, calls=%fused_computation.364 | custom fusion | flops 768 | bytes 7684 | tf_op jit(solution)/shard_map/scatter-add | solution.py:270
  126.8 6.0 %scatter_fusion.3 = f32[1920]{0:T(1024)S(1)} fusion(f32[1920]{0:T(1024)S(1)} %scatter_custom_fusion.4, s32[768]{0:T(1024)S(1)} %compare_select_fusion.5, f32[768]{0:T(1024)S(1)} %reshape.448), kind=kCustom, calls=%fused_computation.12 | custom fusion | flops 768 | bytes 12288 | tf_op jit(solution)/shard_map/scatter-add | solution.py:272
  133.3 6.3 %scatter_custom_fusion.2 = f32[3,1920]{0,1:T(8,128)S(1)} fusion(s32[768]{0:T(1024)S(1)} %compare_select_fusion.6, f32[768,3]{1,0:T(8,128)S(1)} %copy.87, f32[]{:T(128)} %constant.169.clone.1), kind=kCustom, calls=%fused_computation.293 | custom fusion | flops 2304 | bytes 23044 | tf_op jit(solution)/shard_map/scatter-add | solution.py:263
  139.6 6.4 %scatter_fusion.2 = f32[3,1920]{0,1:T(8,128)S(1)} fusion(f32[3,1920]{0,1:T(8,128)S(1)} %scatter_custom_fusion.2, s32[768]{0:T(1024)S(1)} %compare_select_fusion.5, f32[768,3]{1,0:T(8,128)S(1)} %copy.88), kind=kCustom, calls=%fused_computation.10 | custom fusion | flops 2304 | bytes 30720 | tf_op jit(solution)/shard_map/scatter-add | solution.py:265
  146.5 1.9 %collective-permute-start.5 = (f32[3,4,176]{2,1,0:T(4,128)S(1)}, f32[3,4,176]{2,1,0:T(4,128)S(1)}, u32[]{:S(2)}, u32[]{:S(2)}) collective-permute-start(f32[3,4,176]{2,1,0:T(4,128)S(1)} %pad_maximum_fusion.5), channel_id=1, source_target_pairs={{1,0},{2,1},{3,2},{4,3},{5,4},{6,5},{7,6},{8,7},{9,8},{10,9},{11,1... | collective-permute-start | bytes 25352 | tf_op jit(solution)/shard_map/ppermute | solution.py:19
  148.4 2.4 %collective-permute-start.4 = (f32[3,4,176]{2,1,0:T(4,128)S(1)}, f32[3,4,176]{2,1,0:T(4,128)S(1)}, u32[]{:S(2)}, u32[]{:S(2)}) collective-permute-start(f32[3,4,176]{2,1,0:T(4,128)S(1)} %pad_maximum_fusion.4), channel_id=1, source_target_pairs={{63,0},{0,1},{1,2},{2,3},{3,4},{4,5},{5,6},{6,7},{7,8},{8,9},{9,10... | collective-permute-start | bytes 25352 | tf_op jit(solution)/shard_map/ppermute | solution.py:19
  151.0 6.4 %collective-permute-done.4 = f32[3,4,176]{2,1,0:T(4,128)S(1)} collective-permute-done((f32[3,4,176]{2,1,0:T(4,128)S(1)}, f32[3,4,176]{2,1,0:T(4,128)S(1)}, u32[]{:S(2)}, u32[]{:S(2)}) %collective-permute-start.4) | collective-permute-done | bytes 8480 | tf_op jit(solution)/shard_map/ppermute | solution.py:19
  157.5 2.0 %collective-permute-start.6 = (f32[3,4,176]{2,1,0:T(4,128)S(1)}, f32[3,4,176]{2,1,0:T(4,128)S(1)}, u32[]{:S(2)}, u32[]{:S(2)}) collective-permute-start(f32[3,4,176]{2,1,0:T(4,128)S(1)} %pad_maximum_fusion.6), channel_id=1, source_target_pairs={{448,0},{0,64},{64,128},{128,192},{192,256},{256,320},{320,384},{3... | collective-permute-start | bytes 25352 | tf_op jit(solution)/shard_map/ppermute | solution.py:19
  159.5 3.9 %collective-permute-start.7 = (f32[3,4,176]{2,1,0:T(4,128)S(1)}, f32[3,4,176]{2,1,0:T(4,128)S(1)}, u32[]{:S(2)}, u32[]{:S(2)}) collective-permute-start(f32[3,4,176]{2,1,0:T(4,128)S(1)} %pad_maximum_fusion.7), channel_id=1, source_target_pairs={{64,0},{128,64},{192,128},{256,192},{320,256},{384,320},{448,384},... | collective-permute-start | bytes 25352 | tf_op jit(solution)/shard_map/ppermute | solution.py:19
  163.4 7.7 %collective-permute-done.7 = f32[3,4,176]{2,1,0:T(4,128)S(1)} collective-permute-done((f32[3,4,176]{2,1,0:T(4,128)S(1)}, f32[3,4,176]{2,1,0:T(4,128)S(1)}, u32[]{:S(2)}, u32[]{:S(2)}) %collective-permute-start.7) | collective-permute-done | bytes 8480 | tf_op jit(solution)/shard_map/ppermute | solution.py:19
  171.5 9.1 %scatter_fusion.4 = f32[4,512]{0,1:T(8,128)S(1)} fusion(f32[4,512]{0,1:T(8,128)S(1)} %copy.90, s32[1408]{0:T(1024)S(1)} %fusion.150, f32[1408,4]{1,0:T(8,128)S(1)} %copy.91), kind=kCustom, calls=%fused_computation.13 | custom fusion | flops 5632 | bytes 73216 | tf_op jit(solution)/shard_map/scatter-add | solution.py:314
  (362 shorter events, 33.1 us)
Async XLA Ops:
  0.6 19.0 %copy-start.3 = (s32[8,176]{1,0:T(8,128)S(1)}, s32[8,176]{1,0:T(8,128)}, u32[]{:S(2)}) copy-start(s32[8,176]{1,0:T(8,128)} %param.20) | copy-start | bytes 16900
  0.6 19.7 %copy-start.6 = (s32[768]{0:T(1024)S(1)}, s32[768]{0:T(1024)}, u32[]{:S(2)}) copy-start(s32[768]{0:T(1024)} %param.22) | copy-start | bytes 9220
  0.7 19.8 %copy-start.5 = (s32[768]{0:T(1024)S(1)}, s32[768]{0:T(1024)}, u32[]{:S(2)}) copy-start(s32[768]{0:T(1024)} %param.21) | copy-start | bytes 9220
  6.8 13.7 %collective-permute-start = (f32[3,4,176]{2,1,0:T(4,128)S(1)}, f32[3,4,176]{2,1,0:T(4,128)S(1)}, u32[]{:S(2)}, u32[]{:S(2)}) collective-permute-start(f32[3,4,176]{2,1,0:T(4,128)S(1)} %get-tuple-element.390), channel_id=1, source_target_pairs={{448,0},{0,64},{64,128},{128,192},{192,256},{256,320},{320,384},{3... | collective-permute-start | bytes 25352 | tf_op jit(solution)/shard_map/ppermute | solution.py:19
  17.7 11.6 %collective-permute-start.1 = (f32[3,4,176]{2,1,0:T(4,128)S(1)}, f32[3,4,176]{2,1,0:T(4,128)S(1)}, u32[]{:S(2)}, u32[]{:S(2)}) collective-permute-start(f32[3,4,176]{2,1,0:T(4,128)S(1)} %get-tuple-element.391), channel_id=1, source_target_pairs={{64,0},{128,64},{192,128},{256,192},{320,256},{384,320},{448,384},... | collective-permute-start | bytes 25352 | tf_op jit(solution)/shard_map/ppermute | solution.py:19
  29.3 8.1 %collective-permute-start.2 = (f32[3,4,176]{2,1,0:T(4,128)S(1)}, f32[3,4,176]{2,1,0:T(4,128)S(1)}, u32[]{:S(2)}, u32[]{:S(2)}) collective-permute-start(f32[3,4,176]{2,1,0:T(4,128)S(1)} %pad_maximum_fusion.2), channel_id=1, source_target_pairs={{1,0},{2,1},{3,2},{4,3},{5,4},{6,5},{7,6},{8,7},{9,8},{10,9},{11,1... | collective-permute-start | bytes 25352 | tf_op jit(solution)/shard_map/ppermute | solution.py:19
  35.4 8.9 %collective-permute-start.3 = (f32[3,4,176]{2,1,0:T(4,128)S(1)}, f32[3,4,176]{2,1,0:T(4,128)S(1)}, u32[]{:S(2)}, u32[]{:S(2)}) collective-permute-start(f32[3,4,176]{2,1,0:T(4,128)S(1)} %pad_maximum_fusion.3), channel_id=1, source_target_pairs={{63,0},{0,1},{1,2},{2,3},{3,4},{4,5},{5,6},{6,7},{7,8},{8,9},{9,10... | collective-permute-start | bytes 25352 | tf_op jit(solution)/shard_map/ppermute | solution.py:19
  57.0 0.8 copy-start
  57.0 0.8 copy-start.1
  57.0 0.8 copy-start.2
  57.0 0.8 copy-start.4
  71.3 0.9 copy-start.7
  71.3 0.9 copy-start.8
  78.1 0.9 copy-start.11
  78.2 1.0 copy-start.9
  79.2 0.6 copy-start.10
  91.1 0.9 copy-start.11
  91.2 1.0 copy-start.9
  92.2 0.6 copy-start.10
  104.2 0.9 copy-start.11
  104.3 1.0 copy-start.9
  105.3 0.6 copy-start.10
  146.5 4.5 %collective-permute-start.5 = (f32[3,4,176]{2,1,0:T(4,128)S(1)}, f32[3,4,176]{2,1,0:T(4,128)S(1)}, u32[]{:S(2)}, u32[]{:S(2)}) collective-permute-start(f32[3,4,176]{2,1,0:T(4,128)S(1)} %pad_maximum_fusion.5), channel_id=1, source_target_pairs={{1,0},{2,1},{3,2},{4,3},{5,4},{6,5},{7,6},{8,7},{9,8},{10,9},{11,1... | collective-permute-start | bytes 25352 | tf_op jit(solution)/shard_map/ppermute | solution.py:19
  148.4 9.0 %collective-permute-start.4 = (f32[3,4,176]{2,1,0:T(4,128)S(1)}, f32[3,4,176]{2,1,0:T(4,128)S(1)}, u32[]{:S(2)}, u32[]{:S(2)}) collective-permute-start(f32[3,4,176]{2,1,0:T(4,128)S(1)} %pad_maximum_fusion.4), channel_id=1, source_target_pairs={{63,0},{0,1},{1,2},{2,3},{3,4},{4,5},{5,6},{6,7},{7,8},{8,9},{9,10... | collective-permute-start | bytes 25352 | tf_op jit(solution)/shard_map/ppermute | solution.py:19
  157.5 5.9 %collective-permute-start.6 = (f32[3,4,176]{2,1,0:T(4,128)S(1)}, f32[3,4,176]{2,1,0:T(4,128)S(1)}, u32[]{:S(2)}, u32[]{:S(2)}) collective-permute-start(f32[3,4,176]{2,1,0:T(4,128)S(1)} %pad_maximum_fusion.6), channel_id=1, source_target_pairs={{448,0},{0,64},{64,128},{128,192},{192,256},{256,320},{320,384},{3... | collective-permute-start | bytes 25352 | tf_op jit(solution)/shard_map/ppermute | solution.py:19
  159.5 11.6 %collective-permute-start.7 = (f32[3,4,176]{2,1,0:T(4,128)S(1)}, f32[3,4,176]{2,1,0:T(4,128)S(1)}, u32[]{:S(2)}, u32[]{:S(2)}) collective-permute-start(f32[3,4,176]{2,1,0:T(4,128)S(1)} %pad_maximum_fusion.7), channel_id=1, source_target_pairs={{64,0},{128,64},{192,128},{256,192},{320,256},{384,320},{448,384},... | collective-permute-start | bytes 25352 | tf_op jit(solution)/shard_map/ppermute | solution.py:19
where the time goes:
time: 183 us; the launch traced here: 182 us
  other arithmetic  60.6 us (33%)
  local copies, waits for them, and re-layouts  40.4 us (22%)
  starting transfers between devices  30.9 us (17%)
  waiting for transfers between devices  29.9 us (16%)
  matrix products  16.9 us (9%)
  between operations  1.9 us (1%)
    ppermute x8, starting transfers between devices, from_behind(): return lax.ppermute(block, axis, route)  30.9 us
    ppermute x8, waiting for transfers between devices, from_behind(): return lax.ppermute(block, axis, route)  29.9 us
    scatter-add x2, other arithmetic, device_terms(): gradient = jnp.zeros((3, slots_total), jnp.float32).at[:, neighbour_ids]....  12.7 us
    scatter-add x2, other arithmetic, device_terms(): shares = jnp.zeros((slots_total,), jnp.float32).at[neighbour_ids].add(0.5...  10.7 us
    gather x6, local copies, waits for them, and re-layouts, energy_pass(): pair_vals, pull_back = jax.vjp(energy_of, moved, env_sum[block_ids])  9.64 us
    scatter-add x1, other arithmetic, on_device(): terms[:, :atom_count].at[:, send_lists.reshape(-1)].add(arrivals)  9.14 us
    scatter-add x3, other arithmetic, energy_pass(): return (d_env.at[block_ids].add(d_gather), (pair_vals, d_first))  8.16 us
    scatter-add x3, other arithmetic, accumulate(): env_sum.at[block_ids]  8.16 us
  transfers between devices with their start and end apart: 8, of which 4 were waited for; matrix products, arithmetic and copies ran while one was open for 0% of the time, Pallas kernels for 0%

commit v1 on v0

v1 whole, which is shorter than its diff:
```python
import math

import jax
import jax.numpy as jnp
from jax import lax
from jax.experimental import pallas as pl
from jax.experimental.pallas import tpu as pltpu
from jax.sharding import PartitionSpec as P

AXES = ("outer", "inner")
CUTOFF = 6.0
ROOT3 = math.sqrt(3.0)
ROOT5 = math.sqrt(5.0)
ROOT15 = math.sqrt(15.0)
LANES = 128
F32 = jnp.float32
BF16 = jnp.bfloat16
ORDER_OF = (0, 1, 1, 1, 2, 2, 2, 2, 2)


def exchange(block, along, parity):
    outer_len = lax.axis_size("outer")
    inner_len = lax.axis_size("inner")
    route = []
    for o in range(outer_len):
        for n in range(inner_len):
            if along == "outer":
                partner = ((o + 1 if o % 2 == parity else o - 1) % outer_len, n)
            else:
                partner = (o, (n + 1 if n % 2 == parity else n - 1) % inner_len)
            route.append((o * inner_len + n, partner[0] * inner_len + partner[1]))
    return lax.ppermute(block, AXES, route)


def dot(lhs, rhs):
    return jnp.dot(lhs, rhs, preferred_element_type=F32)


def dot_lanes(lhs, rhs):
    return lax.dot_general(lhs, rhs, (((1,), (1,)), ((), ())), preferred_element_type=F32)


def dot_rows(lhs, rhs):
    return lax.dot_general(lhs, rhs, (((0,), (0,)), ((), ())), preferred_element_type=F32)


def parts(value, count):
    out = []
    for _ in range(count):
        piece = value.astype(BF16)
        out.append(piece)
        value = value - piece.astype(F32)
    return out


def onehot_low(low_row):
    rows = lax.broadcasted_iota(jnp.int32, (LANES, low_row.shape[1]), 0)
    return jnp.where(rows == low_row, 1.0, 0.0).astype(BF16)


def high_mask(high_row, group):
    rows = lax.broadcasted_iota(jnp.int32, (8, high_row.shape[1]), 0)
    return high_row == 2 * group + jnp.where(rows >= 4, 1, 0)


def gather(table, low_hot, high_row):
    size = table.shape[0]
    found = dot(jnp.concatenate(parts(table, 3), 0), low_hot)
    found = found[0:size] + found[size : 2 * size] + found[2 * size :]
    total = None
    for group in range(size // 8):
        term = jnp.where(high_mask(high_row, group), found[8 * group : 8 * group + 8], 0.0)
        total = term if total is None else total + term
    return total + pltpu.roll(total, 4, 0)


def scatter(values, low_hot, high_row, groups):
    spread = [jnp.where(high_mask(high_row, group), values, 0.0) for group in range(groups)]
    spread = jnp.concatenate(spread, 0)
    size = 8 * groups
    summed = dot_lanes(jnp.concatenate(parts(spread, 3), 0), low_hot)
    return summed[0:size] + summed[size : 2 * size] + summed[2 * size :]


def local_table(pos_ref, spec_ref):
    packed = jnp.concatenate([pos_ref[...], spec_ref[...].astype(F32)], 0)
    return jnp.concatenate([packed[:, j * LANES : (j + 1) * LANES] for j in range(4)], 0)


def padded_lists(lists_ref, wide_ref):
    wide_ref[...] = jnp.zeros_like(wide_ref)
    wide_ref[:, 0 : lists_ref.shape[1]] = lists_ref[...]
    return wide_ref[...]


def send_kernel(pos_ref, spec_ref, lists_ref, first_ref, second_ref, mid_ref, table_ref, wide_ref):
    table = local_table(pos_ref, spec_ref)
    table_ref[...] = table
    lists = padded_lists(lists_ref, wide_ref)
    tiles = []
    rows = lax.broadcasted_iota(jnp.int32, (8, LANES), 0)
    for k in range(8):
        ids = lists[k : k + 1]
        taken = gather(table, onehot_low(ids & 127), ids >> 7)
        tiles.append(jnp.where(rows < 4, taken[:, 0:LANES], taken[:, LANES:]))
    even = lax.axis_index("outer") % 2 == 0
    for j in range(3):
        at = slice(8 * j, 8 * j + 8)
        first_ref[at] = jnp.where(even, tiles[5 + j], tiles[j])
        second_ref[at] = jnp.where(even, tiles[j], tiles[5 + j])
    mid_ref[0:8] = tiles[3]
    mid_ref[8:16] = tiles[4]


def silu_parts(pre):
    sig = 1.0 / (1.0 + jnp.exp(-pre))
    act = pre * sig
    return act, sig + act * (1.0 - sig)


def pair_kernel(
    feat,
    table_ref,
    first_ref,
    second_ref,
    low_ref,
    up_ref,
    centers_ref,
    neigh_ref,
    live_ref,
    w_rad_ref,
    emb_center_ref,
    emb_neigh_ref,
    w_env_ref,
    w_lat_ref,
    w_out_ref,
    local_ref,
    out_a_ref,
    out_b_ref,
    edge_a_ref,
    edge_b_ref,
    same_ref,
    contrib_ref,
    gath_ref,
):
    pair_len = centers_ref.shape[1]
    lat = w_lat_ref.shape[1]
    even_o = lax.axis_index("outer") % 2 == 0
    even_n = lax.axis_index("inner") % 2 == 0

    centers = centers_ref[...]
    for i in range(pair_len // LANES):
        own = centers[:, i * LANES : (i + 1) * LANES].astype(F32)
        down = jnp.broadcast_to(own, (LANES, LANES)).T
        for j in range(pair_len // LANES):
            across = centers[:, j * LANES : (j + 1) * LANES].astype(F32)
            same_ref[i * LANES : (i + 1) * LANES, j * LANES : (j + 1) * LANES] = jnp.where(
                down == across, 1.0, 0.0
            ).astype(BF16)

    first = first_ref[...]
    second = second_ref[...]
    low = low_ref[...]
    up = up_ref[...]
    by_minus = jnp.where(even_n, low, up)
    by_plus = jnp.where(even_n, up, low)
    lead = [
        jnp.where(even_o, first[8:16], second[8:16]),
        jnp.where(even_o, second[8:16], first[8:16]),
    ]
    diag = []
    for arrived in (by_minus, by_plus):
        diag.append(
            (
                jnp.where(even_o, arrived[8:16], arrived[16:24]),
                jnp.where(even_o, arrived[16:24], arrived[8:16]),
            )
        )
    table = jnp.concatenate(
        [
            table_ref[...],
            diag[0][0],
            lead[0],
            diag[1][0],
            by_minus[0:8],
            by_plus[0:8],
            diag[0][1],
            lead[1],
            diag[1][1],
        ],
        0,
    )

    neigh = neigh_ref[...]
    ghost = neigh - 512
    listed = (ghost * 745) >> 17
    entry = ghost - 176 * listed
    is_local = neigh < 512
    neigh_low = jnp.where(is_local, neigh & 127, entry & 127)
    neigh_high = jnp.where(is_local, neigh >> 7, 4 + 2 * listed + (entry >> 7))
    neigh_hot = onehot_low(neigh_low)
    center_hot = onehot_low(centers & 127)
    center_high = centers >> 7
    at_neigh = gather(table, neigh_hot, neigh_high)
    at_center = gather(table_ref[...], center_hot, center_high)
    moved = at_neigh - at_center

    block = lax.broadcasted_iota(jnp.int32, (1, pair_len), 1) // 128
    mask = jnp.where(block < live_ref[0], 1.0, 0.0)

    rx, ry, rz = moved[0:1], moved[1:2], moved[2:3]
    squared = rx * rx + ry * ry + rz * rz + 1.0
    dist = jnp.sqrt(squared)
    inv = 1.0 / dist
    ux, uy, uz = rx * inv, ry * inv, rz * inv
    slack = 1.0 - squared * (1.0 / (CUTOFF * CUTOFF))
    env = slack * slack
    scaled = env * mask
    ns = (lax.broadcasted_iota(jnp.int32, (8, pair_len), 0) + 1).astype(F32)
    turns = ns * (dist * (1.0 / CUTOFF))
    whole = jnp.floor(turns + 0.5)
    rest = (turns - whole) * math.pi
    odd = whole - 2.0 * jnp.floor(whole * 0.5)
    sign = 1.0 - 2.0 * odd
    r2 = rest * rest
    sine = sign * rest * (
        1.0
        + r2 * (-1.0 / 6 + r2 * (1.0 / 120 + r2 * (-1.0 / 5040 + r2 * (1.0 / 362880 - r2 / 39916800.0))))
    )
    cosine = sign * (
        1.0
        + r2
        * (
            -0.5
            + r2
            * (
                1.0 / 24
                + r2 * (-1.0 / 720 + r2 * (1.0 / 40320 + r2 * (-1.0 / 3628800 + r2 / 479001600.0)))
            )
        )
    )
    scale = inv * env
    basis = sine * scale
    w_rad = w_rad_ref[...]
    kinds = lax.broadcasted_iota(jnp.int32, (8, pair_len), 0).astype(F32)
    hot_center = jnp.where(at_center[3:4] == kinds, 1.0, 0.0).astype(BF16)
    hot_neigh = jnp.where(at_neigh[3:4] == kinds, 1.0, 0.0).astype(BF16)
    b1, b2, b3 = parts(basis, 3)
    w1, w2, w3 = parts(w_rad, 3)
    stacked = jnp.concatenate([b1, b1, b2, b1, b2, b3, hot_center, hot_neigh], 0)
    none = jnp.zeros((1, lat), BF16)
    weights = jnp.concatenate(
        [w1, w2, w1, w3, w2, w1, emb_center_ref[...], none, emb_neigh_ref[...], none], 0
    )
    pre = dot_rows(weights, stacked)
    latent, slope = silu_parts(pre)
    half = latent.astype(BF16)
    raw = dot_rows(w_env_ref[...], half)
    weight = raw * scaled
    shape = [
        None,
        ROOT3 * ux,
        ROOT3 * uy,
        ROOT3 * uz,
        ROOT15 * ux * uy,
        ROOT15 * uy * uz,
        0.5 * ROOT5 * (2.0 * uz * uz - ux * ux - uy * uy),
        ROOT15 * ux * uz,
        0.5 * ROOT15 * (ux * ux - uy * uy),
    ]

    def times(value, k):
        return value if k == 0 else value * shape[k]

    def of_order(value, k):
        return value[ORDER_OF[k] * feat : (ORDER_OF[k] + 1) * feat]

    for k in range(9):
        contrib_ref[k * feat : (k + 1) * feat] = times(of_order(weight, k), k).astype(BF16)
    gath_ref[...] = dot(contrib_ref[...], same_ref[...])
    sums = [None, None, None]
    for k in range(9):
        term = times(gath_ref[k * feat : (k + 1) * feat], k)
        order = ORDER_OF[k]
        sums[order] = term if sums[order] is None else sums[order] + term
    sums = jnp.concatenate(sums, 0)
    invariant = (2.0 * weight * sums).astype(BF16)
    w_lat = w_lat_ref[...]
    joined = jnp.concatenate([half, invariant], 0)
    update, slope2 = silu_parts(dot_rows(w_lat, joined))
    refined = (latent + update).astype(BF16)
    w_out = w_out_ref[...].astype(F32)
    raw_energy = jnp.sum(refined.astype(F32) * w_out, axis=0, keepdims=True)
    energy = scaled * raw_energy

    d_refined = scaled * w_out
    d_joined = dot(w_lat, (d_refined * slope2).astype(BF16))
    d_inv2 = 2.0 * d_joined[lat:]
    d_weight = d_inv2 * sums
    d_sums = d_inv2 * weight
    for k in range(9):
        contrib_ref[k * feat : (k + 1) * feat] = times(of_order(d_sums, k), k).astype(BF16)
    back = dot(contrib_ref[...], same_ref[...])
    d_shape = [None] * 9
    d_order = [None, None, None]
    for k in range(9):
        here = back[k * feat : (k + 1) * feat]
        order = ORDER_OF[k]
        term = times(here, k)
        d_order[order] = term if d_order[order] is None else d_order[order] + term
        if k:
            both = of_order(d_sums, k) * gath_ref[k * feat : (k + 1) * feat] + of_order(weight, k) * here
            d_shape[k] = jnp.sum(both, axis=0, keepdims=True)
    d_weight = d_weight + jnp.concatenate(d_order, 0)
    d_scaled = raw_energy + jnp.sum(d_weight * raw, axis=0, keepdims=True)
    d_latent = d_refined + d_joined[:lat] + dot(w_env_ref[...], (d_weight * scaled).astype(BF16))
    d_pre = d_latent * slope
    p1, p2 = parts(d_pre, 2)
    near = dot(jnp.concatenate([w1, w2], 0), p1)
    d_basis = near[0:8] + near[8:16] + dot(w1, p2)

    along = jnp.sum(d_basis * sine, axis=0, keepdims=True)
    turned = jnp.sum(d_basis * cosine * ns, axis=0, keepdims=True)
    d_env = along * inv + mask * d_scaled
    dx = (
        ROOT3 * d_shape[1]
        + ROOT15 * (uy * d_shape[4] + uz * d_shape[7] + ux * d_shape[8])
        - ROOT5 * ux * d_shape[6]
    )
    dy = (
        ROOT3 * d_shape[2]
        + ROOT15 * (ux * d_shape[4] + uz * d_shape[5] - uy * d_shape[8])
        - ROOT5 * uy * d_shape[6]
    )
    dz = (
        ROOT3 * d_shape[3]
        + ROOT15 * (uy * d_shape[5] + ux * d_shape[7])
        + 2.0 * ROOT5 * uz * d_shape[6]
    )
    d_inv = along * env + dx * rx + dy * ry + dz * rz
    d_dist = turned * (math.pi / CUTOFF) * scale - d_inv * inv * inv
    d_squared = 0.5 * inv * d_dist - (2.0 / (CUTOFF * CUTOFF)) * slack * d_env
    gx = dx * inv + 2.0 * rx * d_squared
    gy = dy * inv + 2.0 * ry * d_squared
    gz = dz * inv + 2.0 * rz * d_squared
    half_energy = 0.5 * energy
    rows4 = [gx, gy, gz, half_energy]
    values = jnp.concatenate(rows4 + rows4, 0)
    rows = lax.broadcasted_iota(jnp.int32, (8, pair_len), 0)
    flipped = jnp.where((rows & 3) == 3, values, -values)
    at_neigh = scatter(flipped, neigh_hot, neigh_high, table.shape[0] // 8)
    at_center = scatter(values, center_hot, center_high, 2)
    local_ref[...] = at_neigh[0:16] + at_center

    tile = [at_neigh[16 + 8 * k : 24 + 8 * k] for k in range(8)]
    back_minus = [tile[3], jnp.where(even_o, tile[0], tile[5]), jnp.where(even_o, tile[5], tile[0])]
    back_plus = [tile[4], jnp.where(even_o, tile[2], tile[7]), jnp.where(even_o, tile[7], tile[2])]
    for j in range(3):
        at = slice(8 * j, 8 * j + 8)
        out_a_ref[at] = jnp.where(even_n, back_minus[j], back_plus[j])
        out_b_ref[at] = jnp.where(even_n, back_plus[j], back_minus[j])
    edge_a_ref[...] = jnp.where(even_o, tile[1], tile[6])
    edge_b_ref[...] = jnp.where(even_o, tile[6], tile[1])


def collect_kernel(
    local_ref, lists_ref, first_ref, second_ref, low_ref, up_ref, forces_ref, energy_ref, wide_ref
):
    even_o = lax.axis_index("outer") % 2 == 0
    even_n = lax.axis_index("inner") % 2 == 0
    first = first_ref[...]
    second = second_ref[...]
    plus = jnp.where(even_o, first, second)
    minus = jnp.where(even_o, second, first)
    up = jnp.where(even_n, low_ref[0:8], up_ref[0:8])
    down = jnp.where(even_n, up_ref[0:8], low_ref[0:8])
    tiles = [minus[0:8], minus[8:16], minus[16:24], down, up, plus[0:8], plus[8:16], plus[16:24]]
    lists = padded_lists(lists_ref, wide_ref)
    rows = lax.broadcasted_iota(jnp.int32, (8, LANES), 0)
    total = local_ref[...]
    for k in range(8):
        turned = pltpu.roll(tiles[k], 4, 0)
        values = jnp.concatenate(
            [jnp.where(rows < 4, tiles[k], turned), jnp.where(rows < 4, turned, tiles[k])], 1
        )
        ids = lists[k : k + 1]
        total = total + scatter(values, onehot_low(ids & 127), ids >> 7, 2)
    for j in range(4):
        forces_ref[:, j * LANES : (j + 1) * LANES] = total[4 * j : 4 * j + 3]
        energy_ref[:, j * LANES : (j + 1) * LANES] = total[4 * j + 3 : 4 * j + 4]


def on_device(
    positions,
    species,
    send_lists,
    centers,
    neighbours,
    live_blocks,
    w_rad,
    emb_center,
    emb_neigh,
    w_env,
    w_lat,
    w_out,
):
    pair_len = centers.shape[0]
    atom_count = positions.shape[1]
    feat = w_env.shape[1] // 3
    width = 3 * w_env.shape[1]
    group = jax.ShapeDtypeStruct((24, LANES), F32)
    tile = jax.ShapeDtypeStruct((8, LANES), F32)
    wide = pltpu.VMEM((8, 2 * LANES), jnp.int32)
    first, second, mid, table = pl.pallas_call(
        send_kernel,
        out_shape=[
            group,
            group,
            jax.ShapeDtypeStruct((16, LANES), F32),
            jax.ShapeDtypeStruct((16, LANES), F32),
        ],
        scratch_shapes=[wide],
        name="gather_sends",
    )(positions, species.reshape(1, atom_count), send_lists)

    even_o = lax.axis_index("outer") % 2 == 0
    even_n = lax.axis_index("inner") % 2 == 0
    second = exchange(second, "outer", 1)
    first = exchange(first, "outer", 0)
    by_plus = jnp.concatenate([mid[8:16], first[16:24], second[16:24]], 0)
    by_minus = jnp.concatenate([mid[0:8], first[0:8], second[0:8]], 0)
    up = exchange(jnp.where(even_n, by_minus, by_plus), "inner", 1)
    low = exchange(jnp.where(even_n, by_plus, by_minus), "inner", 0)

    whole = pl.BlockSpec(memory_space=pltpu.VMEM)
    scalar = pl.BlockSpec(memory_space=pltpu.SMEM)
    local, out_a, out_b, edge_a, edge_b = pl.pallas_call(
        lambda *refs: pair_kernel(feat, *refs),
        out_shape=[jax.ShapeDtypeStruct((16, LANES), F32), group, group, tile, tile],
        in_specs=[whole] * 7 + [scalar] + [whole] * 6,
        scratch_shapes=[
            pltpu.VMEM((pair_len, pair_len), BF16),
            pltpu.VMEM((width, pair_len), BF16),
            pltpu.VMEM((width, pair_len), F32),
        ],
        compiler_params=pltpu.CompilerParams(vmem_limit_bytes=48 * 1024 * 1024),
        name="pair_terms",
    )(
        table,
        first,
        second,
        low,
        up,
        centers.reshape(1, pair_len),
        neighbours.reshape(1, pair_len),
        live_blocks,
        w_rad,
        emb_center,
        emb_neigh,
        w_env,
        w_lat,
        w_out.reshape(-1, 1),
    )

    up = exchange(out_b, "inner", 1)
    low = exchange(out_a, "inner", 0)
    by_plus = jnp.where(even_n, low, up)
    by_minus = jnp.where(even_n, up, low)
    second = exchange(
        jnp.concatenate([by_minus[16:24], edge_b, by_plus[16:24]], 0), "outer", 1
    )
    first = exchange(jnp.concatenate([by_minus[8:16], edge_a, by_plus[8:16]], 0), "outer", 0)
    forces, energy = pl.pallas_call(
        collect_kernel,
        out_shape=[
            jax.ShapeDtypeStruct((3, atom_count), F32),
            jax.ShapeDtypeStruct((1, atom_count), F32),
        ],
        scratch_shapes=[wide],
        name="collect_terms",
    )(local, send_lists, first, second, low, up)
    return forces, energy.reshape(atom_count)


def solution(mesh):
    return jax.shard_map(
        on_device,
        mesh=mesh,
        in_specs=(
            P(None, AXES),
            P(AXES),
            P(None, AXES),
            P(AXES),
            P(AXES),
            P(AXES),
            P(),
            P(),
            P(),
            P(),
            P(),
            P(),
        ),
        out_specs=(P(None, AXES), P(AXES)),
        check_vma=False,
    )
```

time: 183 us -> 59.5 us (0.33)
  the two profiles are of different devices: /device:TPU:6 before, /device:TPU:1 now
where the time goes in v1:
time: 59.5 us; the launch traced here: 58.9 us
  starting transfers between devices  45 us (76%)
  Pallas kernels  7.22 us (12%)
  local copies, waits for them, and re-layouts  2.74 us (5%)
  waiting for transfers between devices  2.42 us (4%)
  between operations  1.54 us (3%)
    ppermute x8, starting transfers between devices, exchange(): return lax.ppermute(block, AXES, route)  45 us
    pallas_call x1, Pallas kernels, on_device(): pl.pallas_call(lambda *refs: pair_kernel(feat, *refs), out_shape=[jax.Sha...  3.9 us
    ppermute x8, waiting for transfers between devices, exchange(): return lax.ppermute(block, AXES, route)  2.42 us
    unnamed x29, local copies, waits for them, and re-layouts  1.89 us
    pallas_call x1, Pallas kernels, on_device(): pl.pallas_call(collect_kernel, out_shape=[jax.ShapeDtypeStruct((3, atom_c...  1.68 us
    pallas_call x1, Pallas kernels, on_device(): pl.pallas_call(send_kernel, out_shape=[group, group, jax.ShapeDtypeStruct...  1.64 us
  transfers between devices with their start and end apart: 8, of which 3 were waited for; matrix products, arithmetic and copies ran while one was open for 2% of the time, Pallas kernels for 0%

profile of v1, /device:TPU:1, one launch (start us, length us, event | category | flops | bytes accessed | tf_op | source)
XLA Modules:
  0.0 58.9 jit_solution(12731207896995288069)
XLA Ops:
  0.6 1.6 %gather_sends.1 = (f32[24,128]{1,0:T(8,128)}, f32[24,128]{1,0:T(8,128)}, f32[16,128]{1,0:T(8,128)}, f32[16,128]{1,0:T(8,128)}) custom-call(f32[3,512]{1,0:T(4,128)} %pos_ref.1, s32[1,512]{1,0:T(1,128)} %bitcast.3, s32[8,176]{1,0:T(8,128)} %lists_ref.3), custom_call_target="tpu_custom_call" | custom-call | tf_op jit(solution)/shard_map/gather_sends/pallas_call | solution.py:414
  2.3 3.9 %collective-permute-start = (f32[24,128]{1,0:T(8,128)}, f32[24,128]{1,0:T(8,128)S(1)}, u32[]{:S(2)}, u32[]{:S(2)}) collective-permute-start(f32[24,128]{1,0:T(8,128)} %get-tuple-element.14), channel_id=1, source_target_pairs={{0,64},{1,65},{2,66},{3,67},{4,68},{5,69},{6,70},{7,71},{8,72},{9,... | collective-permute-start | bytes 36872 | tf_op jit(solution)/shard_map/ppermute | solution.py:32
  6.2 12.2 %collective-permute-start.1 = (f32[24,128]{1,0:T(8,128)}, f32[24,128]{1,0:T(8,128)S(1)}, u32[]{:S(2)}, u32[]{:S(2)}) collective-permute-start(f32[24,128]{1,0:T(8,128)} %get-tuple-element.15), channel_id=1, source_target_pairs={{0,448},{1,449},{2,450},{3,451},{4,452},{5,453},{6,454},{7,455},{8... | collective-permute-start | bytes 36872 | tf_op jit(solution)/shard_map/ppermute | solution.py:32
  18.4 0.7 %fusion.6 = (f32[8,128]{1,0:T(8,128)S(1)}, f32[8,128]{1,0:T(8,128)S(1)}) fusion(f32[16,128]{1,0:T(8,128)} %get-tuple-element.16), kind=kLoop, calls=%fused_computation.12 | loop fusion | bytes 16384 | tf_op jit(solution)/shard_map/slice | solution.py:430
  19.1 0.0 collective-permute-done.refs_1_
  19.1 0.6 collective-permute-done.1.refs_2_
  19.7 0.0 copy-start.6
  19.7 0.0 copy-start.11
  19.7 4.9 %collective-permute-start.3 = (f32[24,128]{1,0:T(8,128)S(1)}, f32[24,128]{1,0:T(8,128)S(1)}, u32[]{:S(2)}, u32[]{:S(2)}) collective-permute-start(f32[24,128]{1,0:T(8,128)S(1)} %get-tuple-element.26), channel_id=1, source_target_pairs={{0,63},{1,2},{2,1},{3,4},{4,3},{5,6},{6,5},{7,8},{8,7},{9,10},{10,... | collective-permute-start | bytes 36872 | tf_op jit(solution)/shard_map/ppermute | solution.py:32
  24.6 0.0 copy-start.12
  24.7 5.3 %collective-permute-start.2 = (f32[24,128]{1,0:T(8,128)S(1)}, f32[24,128]{1,0:T(8,128)S(1)}, u32[]{:S(2)}, u32[]{:S(2)}) collective-permute-start(f32[24,128]{1,0:T(8,128)S(1)} %get-tuple-element.27), channel_id=1, source_target_pairs={{0,1},{1,0},{2,3},{3,2},{4,5},{5,4},{6,7},{7,6},{8,9},{9,8},{10,11... | collective-permute-start | bytes 36872 | tf_op jit(solution)/shard_map/ppermute | solution.py:32
  30.0 0.0 copy-start.13
  30.7 0.0 copy-done.11
  30.7 0.0 copy-start
  30.7 0.0 copy-done.12
  30.7 0.0 copy-done.13
  30.7 0.1 copy.15.refs_13_
  30.9 0.0 copy-done.6
  30.9 0.0 copy-start.1
  30.9 0.0 copy-start.3
  30.9 0.0 copy-start.4
  30.9 0.0 copy-start.5
  30.9 0.1 copy.14.refs_11_
  31.0 0.0 collective-permute-done.3.refs_4_
  31.0 0.0 collective-permute-done.2.refs_3_
  31.0 0.5 copy-done
  31.6 0.0 copy-done.1
  31.6 0.0 copy-done.3
  31.6 0.0 copy-done.4
  31.6 0.0 copy-done.5
  31.6 3.9 %pair_terms.1 = (f32[16,128]{1,0:T(8,128)S(1)}, f32[24,128]{1,0:T(8,128)S(1)}, f32[24,128]{1,0:T(8,128)S(1)}, f32[8,128]{1,0:T(8,128)S(1)}, f32[8,128]{1,0:T(8,128)S(1)}) custom-call(f32[16,128]{1,0:T(8,128)S(1)} %copy-done.1, f32[24,128]{1,0:T(8,128)S(1)} %collective-permute-done.refs_1_, f32[24,128]{1,0:T(8,128)S(1)} %collective-permute-done.1.refs_2_, ...), custom_call_target="tpu_custom_call" | custom-call | tf_op jit(solution)/shard_map/pair_terms/pallas_call | solution.py:437
  35.5 1.9 %collective-permute-start.4 = (f32[24,128]{1,0:T(8,128)S(1)}, f32[24,128]{1,0:T(8,128)S(1)}, u32[]{:S(2)}, u32[]{:S(2)}) collective-permute-start(f32[24,128]{1,0:T(8,128)S(1)} %get-tuple-element.18), channel_id=1, source_target_pairs={{0,63},{1,2},{2,1},{3,4},{4,3},{5,6},{6,5},{7,8},{8,7},{9,10},{10,... | collective-permute-start | bytes 36872 | tf_op jit(solution)/shard_map/ppermute | solution.py:32
  37.4 5.4 %collective-permute-start.5 = (f32[24,128]{1,0:T(8,128)S(1)}, f32[24,128]{1,0:T(8,128)S(1)}, u32[]{:S(2)}, u32[]{:S(2)}) collective-permute-start(f32[24,128]{1,0:T(8,128)S(1)} %get-tuple-element.19), channel_id=1, source_target_pairs={{0,1},{1,0},{2,3},{3,2},{4,5},{5,4},{6,7},{7,6},{8,9},{9,8},{10,11... | collective-permute-start | bytes 36872 | tf_op jit(solution)/shard_map/ppermute | solution.py:32
  42.8 0.0 collective-permute-done.4.up_ref
  42.9 0.0 copy-start.7
  42.9 0.8 %collective-permute-done.5.low_ref = f32[24,128]{1,0:T(8,128)S(1)} collective-permute-done((f32[24,128]{1,0:T(8,128)S(1)}, f32[24,128]{1,0:T(8,128)S(1)}, u32[]{:S(2)}, u32[]{:S(2)}) %collective-permute-start.5) | collective-permute-done | bytes 12320 | tf_op jit(solution)/shard_map/ppermute | solution.py:32
  43.7 0.0 copy-start.8
  43.7 0.0 copy-done.2
  43.7 0.0 copy-done.7
  43.7 0.6 copy-done.8
  44.3 1.9 %collective-permute-start.6 = (f32[24,128]{1,0:T(8,128)S(1)}, f32[24,128]{1,0:T(8,128)S(1)}, u32[]{:S(2)}, u32[]{:S(2)}) collective-permute-start(f32[24,128]{1,0:T(8,128)S(1)} %pad_maximum_fusion.2), channel_id=1, source_target_pairs={{0,64},{1,65},{2,66},{3,67},{4,68},{5,69},{6,70},{7,71},{8,72},{9,... | collective-permute-start | bytes 36872 | tf_op jit(solution)/shard_map/ppermute | solution.py:32
  46.2 9.4 %collective-permute-start.7 = (f32[24,128]{1,0:T(8,128)S(1)}, f32[24,128]{1,0:T(8,128)S(1)}, u32[]{:S(2)}, u32[]{:S(2)}) collective-permute-start(f32[24,128]{1,0:T(8,128)S(1)} %pad_maximum_fusion.3), channel_id=1, source_target_pairs={{0,448},{1,449},{2,450},{3,451},{4,452},{5,453},{6,454},{7,455},{8... | collective-permute-start | bytes 36872 | tf_op jit(solution)/shard_map/ppermute | solution.py:32
  55.6 0.0 collective-permute-done.6.first_ref
  55.6 0.0 copy-start.9
  55.6 1.0 %collective-permute-done.7.second_ref = f32[24,128]{1,0:T(8,128)S(1)} collective-permute-done((f32[24,128]{1,0:T(8,128)S(1)}, f32[24,128]{1,0:T(8,128)S(1)}, u32[]{:S(2)}, u32[]{:S(2)}) %collective-permute-start.7) | collective-permute-done | bytes 12320 | tf_op jit(solution)/shard_map/ppermute | solution.py:32
  56.6 0.0 copy-done.9
  56.7 0.6 %copy-done.10 = f32[24,128]{1,0:T(8,128)} copy-done((f32[24,128]{1,0:T(8,128)}, f32[24,128]{1,0:T(8,128)S(1)}, u32[]{:S(2)}) %copy-start.10) | copy-done | bytes 12312
  57.2 1.7 %collect_terms.1 = (f32[3,512]{1,0:T(4,128)}, f32[1,512]{1,0:T(1,128)}) custom-call(f32[16,128]{1,0:T(8,128)} %copy-done.2, s32[8,176]{1,0:T(8,128)} %lists_ref.3, f32[24,128]{1,0:T(8,128)} %copy-done.9, f32[24,128]{1,0:T(8,128)} %copy-done.10, f32[24,128]{1,0:T(8,128)} %copy-done.8, f32[24,128]{1,0:T(8,128)} %copy-done.7), custom_call_target="tpu_custom_call" | custom-call | tf_op jit(solution)/shard_map/collect_terms/pallas_call | solution.py:473
  (11 shorter events, 0.0 us)
Async XLA Ops:
  2.3 16.8 %collective-permute-start = (f32[24,128]{1,0:T(8,128)}, f32[24,128]{1,0:T(8,128)S(1)}, u32[]{:S(2)}, u32[]{:S(2)}) collective-permute-start(f32[24,128]{1,0:T(8,128)} %get-tuple-element.14), channel_id=1, source_target_pairs={{0,64},{1,65},{2,66},{3,67},{4,68},{5,69},{6,70},{7,71},{8,72},{9,... | collective-permute-start | bytes 36872 | tf_op jit(solution)/shard_map/ppermute | solution.py:32
  6.2 13.5 %collective-permute-start.1 = (f32[24,128]{1,0:T(8,128)}, f32[24,128]{1,0:T(8,128)S(1)}, u32[]{:S(2)}, u32[]{:S(2)}) collective-permute-start(f32[24,128]{1,0:T(8,128)} %get-tuple-element.15), channel_id=1, source_target_pairs={{0,448},{1,449},{2,450},{3,451},{4,452},{5,453},{6,454},{7,455},{8... | collective-permute-start | bytes 36872 | tf_op jit(solution)/shard_map/ppermute | solution.py:32
  19.7 11.2 %copy-start.6 = (bf16[128,192]{0,1:T(8,128)(2,1)S(1)}, bf16[128,192]{0,1:T(8,128)(2,1)}, u32[]{:S(2)}) copy-start(bf16[128,192]{0,1:T(8,128)(2,1)} %param.21) | copy-start | bytes 147460
  19.7 11.0 %copy-start.11 = (s32[768]{0:T(1024)S(1)}, s32[768]{0:T(1024)}, u32[]{:S(2)}) copy-start(s32[768]{0:T(1024)} %param.15) | copy-start | bytes 9220
  19.7 11.3 %collective-permute-start.3 = (f32[24,128]{1,0:T(8,128)S(1)}, f32[24,128]{1,0:T(8,128)S(1)}, u32[]{:S(2)}, u32[]{:S(2)}) collective-permute-start(f32[24,128]{1,0:T(8,128)S(1)} %get-tuple-element.26), channel_id=1, source_target_pairs={{0,63},{1,2},{2,1},{3,4},{4,3},{5,6},{6,5},{7,8},{8,7},{9,10},{10,... | collective-permute-start | bytes 36872 | tf_op jit(solution)/shard_map/ppermute | solution.py:32
  24.6 6.0 %copy-start.12 = (s32[768]{0:T(1024)S(1)}, s32[768]{0:T(1024)}, u32[]{:S(2)}) copy-start(s32[768]{0:T(1024)} %param.16) | copy-start | bytes 9220
  24.7 6.4 %collective-permute-start.2 = (f32[24,128]{1,0:T(8,128)S(1)}, f32[24,128]{1,0:T(8,128)S(1)}, u32[]{:S(2)}, u32[]{:S(2)}) collective-permute-start(f32[24,128]{1,0:T(8,128)S(1)} %get-tuple-element.27), channel_id=1, source_target_pairs={{0,1},{1,0},{2,3},{3,2},{4,5},{5,4},{6,7},{7,6},{8,9},{9,8},{10,11... | collective-permute-start | bytes 36872 | tf_op jit(solution)/shard_map/ppermute | solution.py:32
  30.0 0.7 %copy-start.13 = (bf16[128]{0:T(256)(128)(2,1)S(1)}, bf16[128]{0:T(256)(128)(2,1)}, u32[]{:S(2)}) copy-start(bf16[128]{0:T(256)(128)(2,1)} %param.23) | copy-start | bytes 772
  30.7 0.9 %copy-start = (bf16[320,128]{1,0:T(8,128)(2,1)S(1)}, bf16[320,128]{1,0:T(8,128)(2,1)}, u32[]{:S(2)}) copy-start(bf16[320,128]{1,0:T(8,128)(2,1)} %refs_12_.1) | copy-start | bytes 245764
  30.9 0.7 %copy-start.1 = (f32[16,128]{1,0:T(8,128)S(1)}, f32[16,128]{1,0:T(8,128)}, u32[]{:S(2)}) copy-start(f32[16,128]{1,0:T(8,128)} %get-tuple-element.13.refs_0_) | copy-start | bytes 24580
  30.9 0.7 %copy-start.3 = (f32[8,128]{1,0:T(8,128)S(1)}, f32[8,128]{1,0:T(8,128)}, u32[]{:S(2)}) copy-start(f32[8,128]{1,0:T(8,128)} %refs_8_.1) | copy-start | bytes 12292
  30.9 0.7 %copy-start.4 = (bf16[7,128]{1,0:T(8,128)(2,1)S(1)}, bf16[7,128]{1,0:T(8,128)(2,1)}, u32[]{:S(2)}) copy-start(bf16[7,128]{1,0:T(8,128)(2,1)} %refs_9_.1) | copy-start | bytes 5380
  30.9 0.7 %copy-start.5 = (bf16[7,128]{1,0:T(8,128)(2,1)S(1)}, bf16[7,128]{1,0:T(8,128)(2,1)}, u32[]{:S(2)}) copy-start(bf16[7,128]{1,0:T(8,128)(2,1)} %refs_10_.1) | copy-start | bytes 5380
  35.5 8.2 %copy-start.2 = (f32[16,128]{1,0:T(8,128)}, f32[16,128]{1,0:T(8,128)S(1)}, u32[]{:S(2)}) copy-start(f32[16,128]{1,0:T(8,128)S(1)} %get-tuple-element.17.local_ref) | copy-start | bytes 24580
  35.5 7.3 %collective-permute-start.4 = (f32[24,128]{1,0:T(8,128)S(1)}, f32[24,128]{1,0:T(8,128)S(1)}, u32[]{:S(2)}, u32[]{:S(2)}) collective-permute-start(f32[24,128]{1,0:T(8,128)S(1)} %get-tuple-element.18), channel_id=1, source_target_pairs={{0,63},{1,2},{2,1},{3,4},{4,3},{5,6},{6,5},{7,8},{8,7},{9,10},{10,... | collective-permute-start | bytes 36872 | tf_op jit(solution)/shard_map/ppermute | solution.py:32
  37.4 6.2 %collective-permute-start.5 = (f32[24,128]{1,0:T(8,128)S(1)}, f32[24,128]{1,0:T(8,128)S(1)}, u32[]{:S(2)}, u32[]{:S(2)}) collective-permute-start(f32[24,128]{1,0:T(8,128)S(1)} %get-tuple-element.19), channel_id=1, source_target_pairs={{0,1},{1,0},{2,3},{3,2},{4,5},{5,4},{6,7},{7,6},{8,9},{9,8},{10,11... | collective-permute-start | bytes 36872 | tf_op jit(solution)/shard_map/ppermute | solution.py:32
  42.9 0.8 %copy-start.7 = (f32[24,128]{1,0:T(8,128)}, f32[24,128]{1,0:T(8,128)S(1)}, u32[]{:S(2)}) copy-start(f32[24,128]{1,0:T(8,128)S(1)} %collective-permute-done.4.up_ref) | copy-start | bytes 36868
  43.7 0.6 %copy-start.8 = (f32[24,128]{1,0:T(8,128)}, f32[24,128]{1,0:T(8,128)S(1)}, u32[]{:S(2)}) copy-start(f32[24,128]{1,0:T(8,128)S(1)} %collective-permute-done.5.low_ref) | copy-start | bytes 36868
  44.3 11.3 %collective-permute-start.6 = (f32[24,128]{1,0:T(8,128)S(1)}, f32[24,128]{1,0:T(8,128)S(1)}, u32[]{:S(2)}, u32[]{:S(2)}) collective-permute-start(f32[24,128]{1,0:T(8,128)S(1)} %pad_maximum_fusion.2), channel_id=1, source_target_pairs={{0,64},{1,65},{2,66},{3,67},{4,68},{5,69},{6,70},{7,71},{8,72},{9,... | collective-permute-start | bytes 36872 | tf_op jit(solution)/shard_map/ppermute | solution.py:32
  46.2 10.5 %collective-permute-start.7 = (f32[24,128]{1,0:T(8,128)S(1)}, f32[24,128]{1,0:T(8,128)S(1)}, u32[]{:S(2)}, u32[]{:S(2)}) collective-permute-start(f32[24,128]{1,0:T(8,128)S(1)} %pad_maximum_fusion.3), channel_id=1, source_target_pairs={{0,448},{1,449},{2,450},{3,451},{4,452},{5,453},{6,454},{7,455},{8... | collective-permute-start | bytes 36872 | tf_op jit(solution)/shard_map/ppermute | solution.py:32
  55.6 1.1 %copy-start.9 = (f32[24,128]{1,0:T(8,128)}, f32[24,128]{1,0:T(8,128)S(1)}, u32[]{:S(2)}) copy-start(f32[24,128]{1,0:T(8,128)S(1)} %collective-permute-done.6.first_ref) | copy-start | bytes 36868
  56.6 0.6 %copy-start.10 = (f32[24,128]{1,0:T(8,128)}, f32[24,128]{1,0:T(8,128)S(1)}, u32[]{:S(2)}) copy-start(f32[24,128]{1,0:T(8,128)S(1)} %collective-permute-done.7.second_ref) | copy-start | bytes 36868

commit v2 on v1

--- a/solution.py
+++ b/solution.py
@@ -15,6 +15,8 @@
 LANES = 128
 F32 = jnp.float32
 BF16 = jnp.bfloat16
+SMALL = pltpu.CompilerParams(vmem_limit_bytes=8 * 1024 * 1024)
+LARGE = pltpu.CompilerParams(vmem_limit_bytes=32 * 1024 * 1024)
 ORDER_OF = (0, 1, 1, 1, 2, 2, 2, 2, 2)
 
 
@@ -121,8 +123,8 @@
 def pair_kernel(
     feat,
     table_ref,
+    second_ref,
     first_ref,
-    second_ref,
     low_ref,
     up_ref,
     centers_ref,
@@ -364,7 +366,7 @@
 
 
 def collect_kernel(
-    local_ref, lists_ref, first_ref, second_ref, low_ref, up_ref, forces_ref, energy_ref, wide_ref
+    local_ref, lists_ref, second_ref, first_ref, low_ref, up_ref, forces_ref, energy_ref, wide_ref
 ):
     even_o = lax.axis_index("outer") % 2 == 0
     even_n = lax.axis_index("inner") % 2 == 0
@@ -420,6 +422,7 @@
             jax.ShapeDtypeStruct((16, LANES), F32),
         ],
         scratch_shapes=[wide],
+        compiler_params=SMALL,
         name="gather_sends",
     )(positions, species.reshape(1, atom_count), send_lists)
 
@@ -443,12 +446,12 @@
             pltpu.VMEM((width, pair_len), BF16),
             pltpu.VMEM((width, pair_len), F32),
         ],
-        compiler_params=pltpu.CompilerParams(vmem_limit_bytes=48 * 1024 * 1024),
+        compiler_params=LARGE,
         name="pair_terms",
     )(
         table,
+        second,
         first,
-        second,
         low,
         up,
         centers.reshape(1, pair_len),
@@ -477,8 +480,9 @@
             jax.ShapeDtypeStruct((1, atom_count), F32),
         ],
         scratch_shapes=[wide],
+        compiler_params=SMALL,
         name="collect_terms",
-    )(local, send_lists, first, second, low, up)
+    )(local, send_lists, second, first, low, up)
     return forces, energy.reshape(atom_count)
 
 

time: 59.5 us -> 57.2 us (0.961)
  starting transfers between devices: 45 us -> 41 us
  waiting for transfers between devices: 2.42 us -> 6.08 us
  Pallas kernels: 7.22 us -> 5.08 us
    ppermute x8, starting transfers between devices: 45 us -> 41 us  [exchange(): return lax.ppermute(block, AXES, route)]
    ppermute x8, waiting for transfers between devices: 2.42 us -> 6.08 us  [exchange(): return lax.ppermute(block, AXES, route)]
    pallas_call x1, Pallas kernels: 1.64 us -> 0.28 us  [on_device(): pl.pallas_call(send_kernel, out_shape=[group, group, jax.ShapeDtypeStruct...]
    unnamed x29 -> x25, local copies, waits for them, and re-layouts: 1.89 us -> 2.77 us
    pallas_call x1, Pallas kernels: 1.68 us -> 0.89 us  [on_device(): pl.pallas_call(collect_kernel, out_shape=[jax.ShapeDtypeStruct((3, atom_c...]
    slice x3, local copies, waits for them, and re-layouts: 0.71 us -> 0.01 us  [on_device(): by_plus = jnp.concatenate([mid[8:16], first[16:24], second[16:24]], 0)]
  transfers between devices with their start and end apart: 8 -> 8, of which waited for: 3 -> 4; matrix products, arithmetic and copies ran while one was open for 2% -> 0% of each run, Pallas kernels for 0% -> 0%
where the time goes in v2:
time: 57.2 us; the launch traced here: 56.6 us
  starting transfers between devices  41 us (72%)
  waiting for transfers between devices  6.08 us (11%)
  Pallas kernels  5.08 us (9%)
  local copies, waits for them, and re-layouts  2.93 us (5%)
  between operations  1.56 us (3%)
    ppermute x8, starting transfers between devices, exchange(): return lax.ppermute(block, AXES, route)  41 us
    ppermute x8, waiting for transfers between devices, exchange(): return lax.ppermute(block, AXES, route)  6.08 us
    pallas_call x1, Pallas kernels, on_device(): pl.pallas_call(lambda *refs: pair_kernel(feat, *refs), out_shape=[jax.Sha...  3.91 us
    unnamed x25, local copies, waits for them, and re-layouts  2.77 us
  transfers between devices with their start and end apart: 8, of which 4 were waited for; matrix products, arithmetic and copies ran while one was open for 0% of the time, Pallas kernels for 0%

profile of v2, /device:TPU:1, one launch (start us, length us, event | category | flops | bytes accessed | tf_op | source)
XLA Modules:
  0.0 56.6 jit_solution(1146407003385410090)
XLA Ops:
  0.6 0.0 copy-start.1
  0.6 0.7 %copy-done.1 = s32[8,176]{1,0:T(8,128)S(1)} copy-done((s32[8,176]{1,0:T(8,128)S(1)}, s32[8,176]{1,0:T(8,128)}, u32[]{:S(2)}) %copy-start.1) | copy-done | bytes 5656
  1.3 0.0 copy-start.3
  1.3 0.7 %copy-done.3 = f32[3,512]{1,0:T(4,128)S(1)} copy-done((f32[3,512]{1,0:T(4,128)S(1)}, f32[3,512]{1,0:T(4,128)}, u32[]{:S(2)}) %copy-start.3) | copy-done | bytes 6168
  2.0 0.0 copy-start.7
  2.0 0.7 %copy-done.7 = s32[512]{0:T(512)S(1)} copy-done((s32[512]{0:T(512)S(1)}, s32[512]{0:T(512)}, u32[]{:S(2)}) %copy-start.7) | copy-done | bytes 2072
  2.7 0.3 gather_sends.1
  3.0 13.7 %collective-permute-start = (f32[24,128]{1,0:T(8,128)S(1)}, f32[24,128]{1,0:T(8,128)S(1)}, u32[]{:S(2)}, u32[]{:S(2)}) collective-permute-start(f32[24,128]{1,0:T(8,128)S(1)} %get-tuple-element.14), channel_id=1, source_target_pairs={{0,448},{1,449},{2,450},{3,451},{4,452},{5,453},{6,454},{7,455},{8... | collective-permute-start | bytes 36872 | tf_op jit(solution)/shard_map/ppermute | solution.py:34
  16.7 1.9 %collective-permute-start.1 = (f32[24,128]{1,0:T(8,128)S(1)}, f32[24,128]{1,0:T(8,128)S(1)}, u32[]{:S(2)}, u32[]{:S(2)}) collective-permute-start(f32[24,128]{1,0:T(8,128)S(1)} %get-tuple-element.15), channel_id=1, source_target_pairs={{0,64},{1,65},{2,66},{3,67},{4,68},{5,69},{6,70},{7,71},{8,72},{9,... | collective-permute-start | bytes 36872 | tf_op jit(solution)/shard_map/ppermute | solution.py:34
  18.6 0.0 collective-permute-done.refs_1_
  18.6 2.5 %collective-permute-done.1.refs_2_ = f32[24,128]{1,0:T(8,128)S(1)} collective-permute-done((f32[24,128]{1,0:T(8,128)S(1)}, f32[24,128]{1,0:T(8,128)S(1)}, u32[]{:S(2)}, u32[]{:S(2)}) %collective-permute-start.1) | collective-permute-done | bytes 12320 | tf_op jit(solution)/shard_map/ppermute | solution.py:34
  21.1 0.0 copy-start.8
  21.1 0.0 copy-start.9
  21.1 5.2 %collective-permute-start.3 = (f32[24,128]{1,0:T(8,128)S(1)}, f32[24,128]{1,0:T(8,128)S(1)}, u32[]{:S(2)}, u32[]{:S(2)}) collective-permute-start(f32[24,128]{1,0:T(8,128)S(1)} %get-tuple-element.26), channel_id=1, source_target_pairs={{0,63},{1,2},{2,1},{3,4},{4,3},{5,6},{6,5},{7,8},{8,7},{9,10},{10,... | collective-permute-start | bytes 36872 | tf_op jit(solution)/shard_map/ppermute | solution.py:34
  26.4 0.0 copy-start.10
  26.4 5.0 %collective-permute-start.2 = (f32[24,128]{1,0:T(8,128)S(1)}, f32[24,128]{1,0:T(8,128)S(1)}, u32[]{:S(2)}, u32[]{:S(2)}) collective-permute-start(f32[24,128]{1,0:T(8,128)S(1)} %get-tuple-element.27), channel_id=1, source_target_pairs={{0,1},{1,0},{2,3},{3,2},{4,5},{5,4},{6,7},{7,6},{8,9},{9,8},{10,11... | collective-permute-start | bytes 36872 | tf_op jit(solution)/shard_map/ppermute | solution.py:34
  31.4 0.0 copy-start.11
  32.1 0.0 copy-done.9
  32.1 0.0 copy-start
  32.1 0.0 copy-done.10
  32.1 0.0 copy-done.11
  32.2 0.1 copy.15.refs_13_
  32.3 0.0 copy-done.8
  32.3 0.0 copy-start.4
  32.3 0.0 copy-start.5
  32.3 0.0 copy-start.6
  32.3 0.1 copy.14.refs_11_
  32.4 0.0 collective-permute-done.3.refs_4_
  32.4 0.0 collective-permute-done.2.refs_3_
  32.5 0.5 copy-done
  33.0 0.0 copy-done.4
  33.0 0.0 copy-done.5
  33.0 0.0 copy-done.6
  33.0 3.9 %pair_terms.1 = (f32[16,128]{1,0:T(8,128)S(1)}, f32[24,128]{1,0:T(8,128)S(1)}, f32[24,128]{1,0:T(8,128)S(1)}, f32[8,128]{1,0:T(8,128)S(1)}, f32[8,128]{1,0:T(8,128)S(1)}) custom-call(f32[16,128]{1,0:T(8,128)S(1)} %get-tuple-element.13.refs_0_, f32[24,128]{1,0:T(8,128)S(1)} %collective-permute-done.refs_1_, f32[24,128]{1,0:T(8,128)S(1)} %collective-permute-done.1.refs_2_, ...), custom_call_target="tpu_custom_call" | custom-call | tf_op jit(solution)/shard_map/pair_terms/pallas_call | solution.py:440
  36.9 1.9 %collective-permute-start.4 = (f32[24,128]{1,0:T(8,128)S(1)}, f32[24,128]{1,0:T(8,128)S(1)}, u32[]{:S(2)}, u32[]{:S(2)}) collective-permute-start(f32[24,128]{1,0:T(8,128)S(1)} %get-tuple-element.18), channel_id=1, source_target_pairs={{0,63},{1,2},{2,1},{3,4},{4,3},{5,6},{6,5},{7,8},{8,7},{9,10},{10,... | collective-permute-start | bytes 36872 | tf_op jit(solution)/shard_map/ppermute | solution.py:34
  38.9 5.4 %collective-permute-start.5 = (f32[24,128]{1,0:T(8,128)S(1)}, f32[24,128]{1,0:T(8,128)S(1)}, u32[]{:S(2)}, u32[]{:S(2)}) collective-permute-start(f32[24,128]{1,0:T(8,128)S(1)} %get-tuple-element.19), channel_id=1, source_target_pairs={{0,1},{1,0},{2,3},{3,2},{4,5},{5,4},{6,7},{7,6},{8,9},{9,8},{10,11... | collective-permute-start | bytes 36872 | tf_op jit(solution)/shard_map/ppermute | solution.py:34
  44.3 0.0 collective-permute-done.4.up_ref
  44.3 0.8 %collective-permute-done.5.low_ref = f32[24,128]{1,0:T(8,128)S(1)} collective-permute-done((f32[24,128]{1,0:T(8,128)S(1)}, f32[24,128]{1,0:T(8,128)S(1)}, u32[]{:S(2)}, u32[]{:S(2)}) %collective-permute-start.5) | collective-permute-done | bytes 12320 | tf_op jit(solution)/shard_map/ppermute | solution.py:34
  45.1 5.9 %collective-permute-start.6 = (f32[24,128]{1,0:T(8,128)S(1)}, f32[24,128]{1,0:T(8,128)S(1)}, u32[]{:S(2)}, u32[]{:S(2)}) collective-permute-start(f32[24,128]{1,0:T(8,128)S(1)} %pad_maximum_fusion.2), channel_id=1, source_target_pairs={{0,448},{1,449},{2,450},{3,451},{4,452},{5,453},{6,454},{7,455},{8... | collective-permute-start | bytes 36872 | tf_op jit(solution)/shard_map/ppermute | solution.py:34
  51.0 0.0 copy-start.2
  51.0 1.9 %collective-permute-start.7 = (f32[24,128]{1,0:T(8,128)S(1)}, f32[24,128]{1,0:T(8,128)S(1)}, u32[]{:S(2)}, u32[]{:S(2)}) collective-permute-start(f32[24,128]{1,0:T(8,128)S(1)} %pad_maximum_fusion.3), channel_id=1, source_target_pairs={{0,64},{1,65},{2,66},{3,67},{4,68},{5,69},{6,70},{7,71},{8,72},{9,... | collective-permute-start | bytes 36872 | tf_op jit(solution)/shard_map/ppermute | solution.py:34
  52.9 2.6 %collective-permute-done.6.second_ref = f32[24,128]{1,0:T(8,128)S(1)} collective-permute-done((f32[24,128]{1,0:T(8,128)S(1)}, f32[24,128]{1,0:T(8,128)S(1)}, u32[]{:S(2)}, u32[]{:S(2)}) %collective-permute-start.6) | collective-permute-done | bytes 12320 | tf_op jit(solution)/shard_map/ppermute | solution.py:34
  55.6 0.2 collective-permute-done.7.first_ref
  55.7 0.0 copy-done.2
  55.8 0.9 %collect_terms.1 = (f32[3,512]{1,0:T(4,128)}, f32[1,512]{1,0:T(1,128)}) custom-call(f32[16,128]{1,0:T(8,128)S(1)} %get-tuple-element.17.local_ref, s32[8,176]{1,0:T(8,128)S(1)} %copy-done.2, f32[24,128]{1,0:T(8,128)S(1)} %collective-permute-done.6.second_ref, f32[24,128]{1,0:T(8,128)S(1)} %collective-permute-done.7.first_ref, ...), custom_call_target="tpu_custom_call" | custom-call | tf_op jit(solution)/shard_map/collect_terms/pallas_call | solution.py:476
  (10 shorter events, 0.0 us)
Async XLA Ops:
  0.6 0.7 %copy-start.1 = (s32[8,176]{1,0:T(8,128)S(1)}, s32[8,176]{1,0:T(8,128)}, u32[]{:S(2)}) copy-start(s32[8,176]{1,0:T(8,128)} %lists_ref.3) | copy-start | bytes 16900
  1.3 0.7 %copy-start.3 = (f32[3,512]{1,0:T(4,128)S(1)}, f32[3,512]{1,0:T(4,128)}, u32[]{:S(2)}) copy-start(f32[3,512]{1,0:T(4,128)} %pos_ref.1) | copy-start | bytes 18436
  2.0 0.7 %copy-start.7 = (s32[512]{0:T(512)S(1)}, s32[512]{0:T(512)}, u32[]{:S(2)}) copy-start(s32[512]{0:T(512)} %param.13) | copy-start | bytes 6148
  3.0 15.6 %collective-permute-start = (f32[24,128]{1,0:T(8,128)S(1)}, f32[24,128]{1,0:T(8,128)S(1)}, u32[]{:S(2)}, u32[]{:S(2)}) collective-permute-start(f32[24,128]{1,0:T(8,128)S(1)} %get-tuple-element.14), channel_id=1, source_target_pairs={{0,448},{1,449},{2,450},{3,451},{4,452},{5,453},{6,454},{7,455},{8... | collective-permute-start | bytes 36872 | tf_op jit(solution)/shard_map/ppermute | solution.py:34
  16.7 4.4 %collective-permute-start.1 = (f32[24,128]{1,0:T(8,128)S(1)}, f32[24,128]{1,0:T(8,128)S(1)}, u32[]{:S(2)}, u32[]{:S(2)}) collective-permute-start(f32[24,128]{1,0:T(8,128)S(1)} %get-tuple-element.15), channel_id=1, source_target_pairs={{0,64},{1,65},{2,66},{3,67},{4,68},{5,69},{6,70},{7,71},{8,72},{9,... | collective-permute-start | bytes 36872 | tf_op jit(solution)/shard_map/ppermute | solution.py:34
  21.1 11.2 %copy-start.8 = (bf16[128,192]{0,1:T(8,128)(2,1)S(1)}, bf16[128,192]{0,1:T(8,128)(2,1)}, u32[]{:S(2)}) copy-start(bf16[128,192]{0,1:T(8,128)(2,1)} %param.21) | copy-start | bytes 147460
  21.1 11.0 %copy-start.9 = (s32[768]{0:T(1024)S(1)}, s32[768]{0:T(1024)}, u32[]{:S(2)}) copy-start(s32[768]{0:T(1024)} %param.15) | copy-start | bytes 9220
  21.1 11.3 %collective-permute-start.3 = (f32[24,128]{1,0:T(8,128)S(1)}, f32[24,128]{1,0:T(8,128)S(1)}, u32[]{:S(2)}, u32[]{:S(2)}) collective-permute-start(f32[24,128]{1,0:T(8,128)S(1)} %get-tuple-element.26), channel_id=1, source_target_pairs={{0,63},{1,2},{2,1},{3,4},{4,3},{5,6},{6,5},{7,8},{8,7},{9,10},{10,... | collective-permute-start | bytes 36872 | tf_op jit(solution)/shard_map/ppermute | solution.py:34
  26.4 5.8 %copy-start.10 = (s32[768]{0:T(1024)S(1)}, s32[768]{0:T(1024)}, u32[]{:S(2)}) copy-start(s32[768]{0:T(1024)} %param.16) | copy-start | bytes 9220
  26.4 6.1 %collective-permute-start.2 = (f32[24,128]{1,0:T(8,128)S(1)}, f32[24,128]{1,0:T(8,128)S(1)}, u32[]{:S(2)}, u32[]{:S(2)}) collective-permute-start(f32[24,128]{1,0:T(8,128)S(1)} %get-tuple-element.27), channel_id=1, source_target_pairs={{0,1},{1,0},{2,3},{3,2},{4,5},{5,4},{6,7},{7,6},{8,9},{9,8},{10,11... | collective-permute-start | bytes 36872 | tf_op jit(solution)/shard_map/ppermute | solution.py:34
  31.4 0.7 %copy-start.11 = (bf16[128]{0:T(256)(128)(2,1)S(1)}, bf16[128]{0:T(256)(128)(2,1)}, u32[]{:S(2)}) copy-start(bf16[128]{0:T(256)(128)(2,1)} %param.23) | copy-start | bytes 772
  32.1 0.9 %copy-start = (bf16[320,128]{1,0:T(8,128)(2,1)S(1)}, bf16[320,128]{1,0:T(8,128)(2,1)}, u32[]{:S(2)}) copy-start(bf16[320,128]{1,0:T(8,128)(2,1)} %refs_12_.1) | copy-start | bytes 245764
  32.3 0.7 %copy-start.4 = (f32[8,128]{1,0:T(8,128)S(1)}, f32[8,128]{1,0:T(8,128)}, u32[]{:S(2)}) copy-start(f32[8,128]{1,0:T(8,128)} %refs_8_.1) | copy-start | bytes 12292
  32.3 0.7 %copy-start.5 = (bf16[7,128]{1,0:T(8,128)(2,1)S(1)}, bf16[7,128]{1,0:T(8,128)(2,1)}, u32[]{:S(2)}) copy-start(bf16[7,128]{1,0:T(8,128)(2,1)} %refs_9_.1) | copy-start | bytes 5380
  32.3 0.7 %copy-start.6 = (bf16[7,128]{1,0:T(8,128)(2,1)S(1)}, bf16[7,128]{1,0:T(8,128)(2,1)}, u32[]{:S(2)}) copy-start(bf16[7,128]{1,0:T(8,128)(2,1)} %refs_10_.1) | copy-start | bytes 5380
  36.9 7.3 %collective-permute-start.4 = (f32[24,128]{1,0:T(8,128)S(1)}, f32[24,128]{1,0:T(8,128)S(1)}, u32[]{:S(2)}, u32[]{:S(2)}) collective-permute-start(f32[24,128]{1,0:T(8,128)S(1)} %get-tuple-element.18), channel_id=1, source_target_pairs={{0,63},{1,2},{2,1},{3,4},{4,3},{5,6},{6,5},{7,8},{8,7},{9,10},{10,... | collective-permute-start | bytes 36872 | tf_op jit(solution)/shard_map/ppermute | solution.py:34
  38.9 6.2 %collective-permute-start.5 = (f32[24,128]{1,0:T(8,128)S(1)}, f32[24,128]{1,0:T(8,128)S(1)}, u32[]{:S(2)}, u32[]{:S(2)}) collective-permute-start(f32[24,128]{1,0:T(8,128)S(1)} %get-tuple-element.19), channel_id=1, source_target_pairs={{0,1},{1,0},{2,3},{3,2},{4,5},{5,4},{6,7},{7,6},{8,9},{9,8},{10,11... | collective-permute-start | bytes 36872 | tf_op jit(solution)/shard_map/ppermute | solution.py:34
  45.1 10.5 %collective-permute-start.6 = (f32[24,128]{1,0:T(8,128)S(1)}, f32[24,128]{1,0:T(8,128)S(1)}, u32[]{:S(2)}, u32[]{:S(2)}) collective-permute-start(f32[24,128]{1,0:T(8,128)S(1)} %pad_maximum_fusion.2), channel_id=1, source_target_pairs={{0,448},{1,449},{2,450},{3,451},{4,452},{5,453},{6,454},{7,455},{8... | collective-permute-start | bytes 36872 | tf_op jit(solution)/shard_map/ppermute | solution.py:34
  51.0 4.8 %copy-start.2 = (s32[8,176]{1,0:T(8,128)S(1)}, s32[8,176]{1,0:T(8,128)}, u32[]{:S(2)}) copy-start(s32[8,176]{1,0:T(8,128)} %lists_ref.3) | copy-start | bytes 16900
  51.0 4.7 %collective-permute-start.7 = (f32[24,128]{1,0:T(8,128)S(1)}, f32[24,128]{1,0:T(8,128)S(1)}, u32[]{:S(2)}, u32[]{:S(2)}) collective-permute-start(f32[24,128]{1,0:T(8,128)S(1)} %pad_maximum_fusion.3), channel_id=1, source_target_pairs={{0,64},{1,65},{2,66},{3,67},{4,68},{5,69},{6,70},{7,71},{8,72},{9,... | collective-permute-start | bytes 36872 | tf_op jit(solution)/shard_map/ppermute | solution.py:34

commit v3 on v2

v3 whole, which is shorter than its diff:
```python
import math

import jax
import jax.numpy as jnp
from jax import lax
from jax.experimental import pallas as pl
from jax.experimental.pallas import tpu as pltpu
from jax.sharding import PartitionSpec as P

AXES = ("outer", "inner")
CUTOFF = 6.0
ROOT3 = math.sqrt(3.0)
ROOT5 = math.sqrt(5.0)
ROOT15 = math.sqrt(15.0)
LANES = 128
F32 = jnp.float32
BF16 = jnp.bfloat16
SMALL = pltpu.CompilerParams(vmem_limit_bytes=8 * 1024 * 1024)
LARGE = pltpu.CompilerParams(vmem_limit_bytes=32 * 1024 * 1024)
DIRS = ((-1, -1), (-1, 0), (-1, 1), (0, -1), (0, 1), (1, -1), (1, 0), (1, 1))
SPAN = (-1, 0, 1)
TABLE, LISTS, CENTERS, NEIGH, PACKED = 0, 16, 32, 40, 48
LIVE = 38
ORDER_OF = (0, 1, 1, 1, 2, 2, 2, 2, 2)


def exchange(block, along, parity):
    outer_len = lax.axis_size("outer")
    inner_len = lax.axis_size("inner")
    route = []
    for o in range(outer_len):
        for n in range(inner_len):
            if along == "outer":
                partner = ((o + 1 if o % 2 == parity else o - 1) % outer_len, n)
            else:
                partner = (o, (n + 1 if n % 2 == parity else n - 1) % inner_len)
            route.append((o * inner_len + n, partner[0] * inner_len + partner[1]))
    return lax.ppermute(block, AXES, route)


def all_rows(block):
    return lax.all_to_all(block, "outer", 0, 0)


def dot(lhs, rhs):
    return jnp.dot(lhs, rhs, preferred_element_type=F32)


def dot_lanes(lhs, rhs):
    return lax.dot_general(lhs, rhs, (((1,), (1,)), ((), ())), preferred_element_type=F32)


def dot_rows(lhs, rhs):
    return lax.dot_general(lhs, rhs, (((0,), (0,)), ((), ())), preferred_element_type=F32)


def parts(value, count):
    out = []
    for _ in range(count):
        piece = value.astype(BF16)
        out.append(piece)
        value = value - piece.astype(F32)
    return out


def onehot_low(low_row):
    rows = lax.broadcasted_iota(jnp.int32, (LANES, low_row.shape[1]), 0)
    return jnp.where(rows == low_row, 1.0, 0.0).astype(BF16)


def high_mask(high_row, group):
    rows = lax.broadcasted_iota(jnp.int32, (8, high_row.shape[1]), 0)
    return high_row == 2 * group + jnp.where(rows >= 4, 1, 0)


def gather(table, low_hot, high_row):
    size = table.shape[0]
    found = dot(jnp.concatenate(parts(table, 3), 0), low_hot)
    found = found[0:size] + found[size : 2 * size] + found[2 * size :]
    total = None
    for group in range(size // 8):
        term = jnp.where(high_mask(high_row, group), found[8 * group : 8 * group + 8], 0.0)
        total = term if total is None else total + term
    return total + pltpu.roll(total, 4, 0)


def scatter(values, low_hot, high_row, groups):
    spread = [jnp.where(high_mask(high_row, group), values, 0.0) for group in groups]
    spread = jnp.concatenate(spread, 0)
    size = 8 * len(groups)
    summed = dot_lanes(jnp.concatenate(parts(spread, 3), 0), low_hot)
    return summed[0:size] + summed[size : 2 * size] + summed[2 * size :]


def pack_kernel(
    pos_hbm,
    spec_hbm,
    lists_hbm,
    centers_hbm,
    neigh_hbm,
    live_ref,
    out_ref,
    pos,
    spec,
    lists,
    centers,
    neigh,
    sems,
):
    fetched = []
    for j, (src, dst) in enumerate(
        (
            (pos_hbm, pos),
            (spec_hbm, spec),
            (lists_hbm, lists),
            (centers_hbm, centers),
            (neigh_hbm, neigh),
        )
    ):
        copy = pltpu.make_async_copy(src, dst, sems.at[j])
        copy.start()
        fetched.append(copy)
    for copy in fetched:
        copy.wait()
    rows = []
    for j in range(4):
        at = slice(j * LANES, (j + 1) * LANES)
        rows.append(pos[:, at])
        rows.append(spec[:, at].astype(F32))
    ids = lists[...].astype(F32)
    rest = ids.shape[1] - LANES
    rows.append(ids[:, 0:LANES])
    rows.append(jnp.concatenate([ids[:, LANES:], jnp.zeros((8, LANES - rest), F32)], 1))
    rows.append(centers[...].astype(F32))
    rows.append(jnp.full((1, LANES), live_ref[0].astype(F32)))
    rows.append(jnp.zeros((1, LANES), F32))
    rows.append(neigh[...].astype(F32))
    rows.append(jnp.zeros((2, LANES), F32))
    packed = jnp.concatenate(rows, 0)
    for q in range(out_ref.shape[0]):
        out_ref[q] = packed


def row_slot(offset):
    count = lax.axis_size("outer")
    return lax.rem(lax.axis_index("outer") + offset + count, count)


def tile_of(a, dx):
    return 3 * (a + 1) + dx + 1


def sends_kernel(raw_ref, far_ref, near_ref, mid_ref):
    even_n = lax.axis_index("inner") % 2 == 0
    rows = lax.broadcasted_iota(jnp.int32, (8, LANES), 0)
    for source in range(-2, 3):
        raw = raw_ref.at[row_slot(source)]
        wanted = [
            k for k in range(8) if abs(source + DIRS[k][0]) <= 1
        ]
        low = raw[LISTS : LISTS + 8].astype(jnp.int32)
        high = raw[LISTS + 8 : LISTS + 16].astype(jnp.int32)
        ids = [part[k : k + 1] for k in wanted for part in (low, high)]
        ids = jnp.concatenate(ids, 1)
        taken = gather(raw[TABLE : TABLE + 16], onehot_low(ids & 127), ids >> 7)
        tiles = {}
        for j, k in enumerate(wanted):
            at = 2 * j * LANES
            tiles[k] = jnp.where(
                rows < 4, taken[:, at : at + LANES], taken[:, at + LANES : at + 2 * LANES]
            )
        for dx in SPAN:
            a = source + dx
            if abs(a) > 1:
                continue
            t = tile_of(a, dx)
            minus, plus = tiles[DIRS.index((dx, -1))], tiles[DIRS.index((dx, 1))]
            far_ref[8 * t : 8 * t + 8] = jnp.where(even_n, minus, plus)
            near_ref[8 * t : 8 * t + 8] = jnp.where(even_n, plus, minus)
            if dx:
                m = 2 * (a + 1) + (dx + 1) // 2
                mid_ref[8 * m : 8 * m + 8] = tiles[DIRS.index((dx, 0))]


def silu_parts(pre):
    sig = 1.0 / (1.0 + jnp.exp(-pre))
    act = pre * sig
    return act, sig + act * (1.0 - sig)


def pair_kernel(
    feat,
    pair_len,
    raw_ref,
    mid_ref,
    up_ref,
    low_ref,
    w_rad_ref,
    emb_center_ref,
    emb_neigh_ref,
    w_env_ref,
    w_lat_ref,
    w_out_ref,
    local_ref,
    own_ref,
    back_far_ref,
    back_near_ref,
    same_ref,
    contrib_ref,
    gath_ref,
):
    chunks = pair_len // LANES
    width = len(SPAN) * pair_len
    lat = w_lat_ref.shape[1]
    even_n = lax.axis_index("inner") % 2 == 0

    def as_row(tile):
        return jnp.concatenate([tile[i : i + 1] for i in range(chunks)], 1)

    found_neigh, found_center, masks = [], [], []
    neigh_hots, neigh_highs = [], []
    for d, a in enumerate(SPAN):
        raw = raw_ref.at[row_slot(a)]
        centers = raw[CENTERS : CENTERS + 8]
        for i in range(chunks):
            down = jnp.broadcast_to(centers[i : i + 1], (LANES, LANES)).T
            for j in range(chunks):
                same_ref[d, i * LANES : (i + 1) * LANES, j * LANES : (j + 1) * LANES] = jnp.where(
                    down == centers[j : j + 1], 1.0, 0.0
                ).astype(BF16)
        table = [raw[TABLE : TABLE + 16]]
        for dx, dy in DIRS:
            t = 8 * tile_of(a, dx)
            if dy == 0:
                m = 8 * (2 * (a + 1) + (dx + 1) // 2)
                table.append(mid_ref[m : m + 8])
                continue
            by_low, by_up = low_ref[t : t + 8], up_ref[t : t + 8]
            if dy < 0:
                table.append(jnp.where(even_n, by_low, by_up))
            else:
                table.append(jnp.where(even_n, by_up, by_low))
        table = jnp.concatenate(table, 0)
        neigh = raw[NEIGH : NEIGH + 8].astype(jnp.int32)
        ghost = neigh - 512
        listed = (ghost * 745) >> 17
        entry = ghost - 176 * listed
        is_local = neigh < 512
        neigh_low = as_row(jnp.where(is_local, neigh & 127, entry & 127))
        neigh_high = as_row(jnp.where(is_local, neigh >> 7, 4 + 2 * listed + (entry >> 7)))
        center_ids = as_row(centers.astype(jnp.int32))
        neigh_hot = onehot_low(neigh_low)
        center_hot = onehot_low(center_ids & 127)
        center_high = center_ids >> 7
        found_neigh.append(gather(table, neigh_hot, neigh_high))
        found_center.append(gather(table[0:16], center_hot, center_high))
        neigh_hots.append(neigh_hot)
        neigh_highs.append(neigh_high)
        if a == 0:
            own_hot, own_high = center_hot, center_high
        block = lax.broadcasted_iota(jnp.int32, (1, pair_len), 1) // 128
        masks.append(jnp.where(block.astype(F32) < raw[LIVE : LIVE + 1, 0:1], 1.0, 0.0))
    at_neigh = jnp.concatenate(found_neigh, 1)
    at_center = jnp.concatenate(found_center, 1)
    mask = jnp.concatenate(masks, 1)
    moved = at_neigh - at_center

    rx, ry, rz = moved[0:1], moved[1:2], moved[2:3]
    squared = rx * rx + ry * ry + rz * rz + 1.0
    dist = jnp.sqrt(squared)
    inv = 1.0 / dist
    ux, uy, uz = rx * inv, ry * inv, rz * inv
    slack = 1.0 - squared * (1.0 / (CUTOFF * CUTOFF))
    env = slack * slack
    scaled = env * mask
    ns = (lax.broadcasted_iota(jnp.int32, (8, width), 0) + 1).astype(F32)
    turns = ns * (dist * (1.0 / CUTOFF))
    whole = jnp.floor(turns + 0.5)
    rest = (turns - whole) * math.pi
    odd = whole - 2.0 * jnp.floor(whole * 0.5)
    sign = 1.0 - 2.0 * odd
    r2 = rest * rest
    sine = sign * rest * (
        1.0
        + r2 * (-1.0 / 6 + r2 * (1.0 / 120 + r2 * (-1.0 / 5040 + r2 * (1.0 / 362880 - r2 / 39916800.0))))
    )
    cosine = sign * (
        1.0
        + r2
        * (
            -0.5
            + r2
            * (
                1.0 / 24
                + r2 * (-1.0 / 720 + r2 * (1.0 / 40320 + r2 * (-1.0 / 3628800 + r2 / 479001600.0)))
            )
        )
    )
    scale = inv * env
    basis = sine * scale
    w_rad = w_rad_ref[...]
    kinds = lax.broadcasted_iota(jnp.int32, (8, width), 0).astype(F32)
    hot_center = jnp.where(at_center[3:4] == kinds, 1.0, 0.0).astype(BF16)
    hot_neigh = jnp.where(at_neigh[3:4] == kinds, 1.0, 0.0).astype(BF16)
    b1, b2, b3 = parts(basis, 3)
    w1, w2, w3 = parts(w_rad, 3)
    stacked = jnp.concatenate([b1, b1, b2, b1, b2, b3, hot_center, hot_neigh], 0)
    none = jnp.zeros((1, lat), BF16)
    weights = jnp.concatenate(
        [w1, w2, w1, w3, w2, w1, emb_center_ref[...], none, emb_neigh_ref[...], none], 0
    )
    pre = dot_rows(weights, stacked)
    latent, slope = silu_parts(pre)
    half = latent.astype(BF16)
    raw = dot(w_env_ref[...], half)
    weight = raw * scaled
    shape = [
        None,
        ROOT3 * ux,
        ROOT3 * uy,
        ROOT3 * uz,
        ROOT15 * ux * uy,
        ROOT15 * uy * uz,
        0.5 * ROOT5 * (2.0 * uz * uz - ux * ux - uy * uy),
        ROOT15 * ux * uz,
        0.5 * ROOT15 * (ux * ux - uy * uy),
    ]

    def times(value, k):
        return value if k == 0 else value * shape[k]

    def of_order(value, k):
        return value[ORDER_OF[k] * feat : (ORDER_OF[k] + 1) * feat]

    for k in range(9):
        contrib_ref[k * feat : (k + 1) * feat] = times(of_order(weight, k), k).astype(BF16)
    for d in range(len(SPAN)):
        at = slice(d * pair_len, (d + 1) * pair_len)
        gath_ref[:, at] = dot(contrib_ref[:, at], same_ref[d])
    sums = [None, None, None]
    for k in range(9):
        term = times(gath_ref[k * feat : (k + 1) * feat], k)
        order = ORDER_OF[k]
        sums[order] = term if sums[order] is None else sums[order] + term
    sums = jnp.concatenate(sums, 0)
    invariant = (2.0 * weight * sums).astype(BF16)
    w_lat = w_lat_ref[...]
    joined = jnp.concatenate([half, invariant], 0)
    update, slope2 = silu_parts(dot_rows(w_lat, joined))
    refined = (latent + update).astype(BF16)
    w_out = jnp.broadcast_to(w_out_ref[...].astype(F32), (8, lat)).T[:, 0:1]
    raw_energy = jnp.sum(refined.astype(F32) * w_out, axis=0, keepdims=True)
    energy = scaled * raw_energy

    d_refined = scaled * w_out
    d_joined = dot(w_lat, (d_refined * slope2).astype(BF16))
    d_inv2 = 2.0 * d_joined[lat:]
    d_weight = d_inv2 * sums
    d_sums = d_inv2 * weight
    for k in range(9):
        contrib_ref[k * feat : (k + 1) * feat] = times(of_order(d_sums, k), k).astype(BF16)
    back = jnp.concatenate(
        [
            dot(contrib_ref[:, d * pair_len : (d + 1) * pair_len], same_ref[d])
            for d in range(len(SPAN))
        ],
        1,
    )
    d_shape = [None] * 9
    d_order = [None, None, None]
    for k in range(9):
        here = back[k * feat : (k + 1) * feat]
        order = ORDER_OF[k]
        term = times(here, k)
        d_order[order] = term if d_order[order] is None else d_order[order] + term
        if k:
            both = of_order(d_sums, k) * gath_ref[k * feat : (k + 1) * feat] + of_order(weight, k) * here
            d_shape[k] = jnp.sum(both, axis=0, keepdims=True)
    d_weight = d_weight + jnp.concatenate(d_order, 0)
    d_scaled = raw_energy + jnp.sum(d_weight * raw, axis=0, keepdims=True)
    d_latent = d_refined + d_joined[:lat] + dot_rows(w_env_ref[...], (d_weight * scaled).astype(BF16))
    d_pre = d_latent * slope
    p1, p2 = parts(d_pre, 2)
    low_half = dot(jnp.concatenate([w1, w2], 0), p1)
    d_basis = low_half[0:8] + low_half[8:16] + dot(w1, p2)

    along = jnp.sum(d_basis * sine, axis=0, keepdims=True)
    turned = jnp.sum(d_basis * cosine * ns, axis=0, keepdims=True)
    d_env = along * inv + mask * d_scaled
    dx = (
        ROOT3 * d_shape[1]
        + ROOT15 * (uy * d_shape[4] + uz * d_shape[7] + ux * d_shape[8])
        - ROOT5 * ux * d_shape[6]
    )
    dy = (
        ROOT3 * d_shape[2]
        + ROOT15 * (ux * d_shape[4] + uz * d_shape[5] - uy * d_shape[8])
        - ROOT5 * uy * d_shape[6]
    )
    dz = (
        ROOT3 * d_shape[3]
        + ROOT15 * (uy * d_shape[5] + ux * d_shape[7])
        + 2.0 * ROOT5 * uz * d_shape[6]
    )
    d_inv = along * env + dx * rx + dy * ry + dz * rz
    d_dist = turned * (math.pi / CUTOFF) * scale - d_inv * inv * inv
    d_squared = 0.5 * inv * d_dist - (2.0 / (CUTOFF * CUTOFF)) * slack * d_env
    gx = dx * inv + 2.0 * rx * d_squared
    gy = dy * inv + 2.0 * ry * d_squared
    gz = dz * inv + 2.0 * rz * d_squared
    half_energy = 0.5 * energy
    rows4 = [gx, gy, gz, half_energy]
    values = jnp.concatenate(rows4 + rows4, 0)
    rows = lax.broadcasted_iota(jnp.int32, (8, width), 0)
    flipped = jnp.where((rows & 3) == 3, values, -values)
    back_minus, back_plus = [], []
    for d, a in enumerate(SPAN):
        at = slice(d * pair_len, (d + 1) * pair_len)
        groups = [2 + DIRS.index((a, -1)), 2 + DIRS.index((a, 1))]
        groups += [2 + DIRS.index((a, 0))] if a else [0, 1]
        terms = scatter(flipped[:, at], neigh_hots[d], neigh_highs[d], groups)
        back_minus.append(terms[0:8])
        back_plus.append(terms[8:16])
        if a:
            own_ref[8 * (d // 2) : 8 * (d // 2) + 8] = terms[16:24]
        else:
            local_ref[...] = terms[16:32] + scatter(values[:, at], own_hot, own_high, (0, 1))
    for d in range(len(SPAN)):
        at = slice(8 * d, 8 * d + 8)
        back_far_ref[at] = jnp.where(even_n, back_plus[d], back_minus[d])
        back_near_ref[at] = jnp.where(even_n, back_minus[d], back_plus[d])


def collect_kernel(local_ref, own_ref, raw_ref, up_ref, low_ref, forces_ref, energy_ref):
    even_n = lax.axis_index("inner") % 2 == 0
    plus = jnp.where(even_n, low_ref[...], up_ref[...])
    minus = jnp.where(even_n, up_ref[...], low_ref[...])
    lists_low = raw_ref[0, LISTS : LISTS + 8].astype(jnp.int32)
    lists_high = raw_ref[0, LISTS + 8 : LISTS + 16].astype(jnp.int32)
    rows = lax.broadcasted_iota(jnp.int32, (8, LANES), 0)
    ids, values = [], []
    for k, (dx, dy) in enumerate(DIRS):
        ids += [lists_low[k : k + 1], lists_high[k : k + 1]]
        if dy == 0:
            at = 8 * ((dx + 1) // 2)
            tile = own_ref[at : at + 8]
        else:
            at = 8 * (dx + 1)
            tile = (minus if dy < 0 else plus)[at : at + 8]
        turned = pltpu.roll(tile, 4, 0)
        values += [jnp.where(rows < 4, tile, turned), jnp.where(rows < 4, turned, tile)]
    ids = jnp.concatenate(ids, 1)
    values = jnp.concatenate(values, 1)
    total = local_ref[...] + scatter(values, onehot_low(ids & 127), ids >> 7, (0, 1))
    for j in range(4):
        forces_ref[:, j * LANES : (j + 1) * LANES] = total[4 * j : 4 * j + 3]
        energy_ref[:, j * LANES : (j + 1) * LANES] = total[4 * j + 3 : 4 * j + 4]


def on_device(
    positions,
    species,
    send_lists,
    centers,
    neighbours,
    live_blocks,
    w_rad,
    emb_center,
    emb_neigh,
    w_env,
    w_lat,
    w_out,
):
    pair_len = centers.shape[0]
    atom_count = positions.shape[1]
    feat = w_env.shape[1] // 3
    width = len(SPAN) * pair_len
    chunks = pair_len // LANES

    def rows(count):
        return jax.ShapeDtypeStruct((count, LANES), F32)

    packed = pl.pallas_call(
        pack_kernel,
        out_shape=jax.ShapeDtypeStruct((lax.axis_size("outer"), PACKED, LANES), F32),
        in_specs=[pl.BlockSpec(memory_space=pltpu.HBM)] * 5
        + [pl.BlockSpec(memory_space=pltpu.SMEM)],
        scratch_shapes=[
            pltpu.VMEM(positions.shape, F32),
            pltpu.VMEM((1, atom_count), jnp.int32),
            pltpu.VMEM(send_lists.shape, jnp.int32),
            pltpu.VMEM((chunks, LANES), jnp.int32),
            pltpu.VMEM((chunks, LANES), jnp.int32),
            pltpu.SemaphoreType.DMA((5,)),
        ],
        compiler_params=SMALL,
        name="pack_domain",
    )(
        *(
            pltpu.with_memory_space_constraint(value, pltpu.HBM)
            for value in (
                positions,
                species.reshape(1, atom_count),
                send_lists,
                centers.reshape(chunks, LANES),
                neighbours.reshape(chunks, LANES),
            )
        ),
        live_blocks,
    )
    raw = all_rows(packed)
    far, near, mid = pl.pallas_call(
        sends_kernel,
        out_shape=[rows(72), rows(72), rows(48)],
        compiler_params=SMALL,
        name="gather_sends",
    )(raw)
    up = exchange(far, "inner", 1)
    low = exchange(near, "inner", 0)
    local, own, far, near = pl.pallas_call(
        lambda *refs: pair_kernel(feat, pair_len, *refs),
        out_shape=[rows(16), rows(16), rows(24), rows(24)],
        scratch_shapes=[
            pltpu.VMEM((len(SPAN), pair_len, pair_len), BF16),
            pltpu.VMEM((9 * feat, width), BF16),
            pltpu.VMEM((9 * feat, width), F32),
        ],
        compiler_params=LARGE,
        name="pair_terms",
    )(raw, mid, up, low, w_rad, emb_center, emb_neigh, w_env.T, w_lat, w_out.reshape(1, -1))
    up = exchange(far, "inner", 1)
    low = exchange(near, "inner", 0)
    forces, energy = pl.pallas_call(
        collect_kernel,
        out_shape=[
            jax.ShapeDtypeStruct((3, atom_count), F32),
            jax.ShapeDtypeStruct((1, atom_count), F32),
        ],
        compiler_params=SMALL,
        name="collect_terms",
    )(local, own, packed, up, low)
    return forces, energy.reshape(atom_count)


def solution(mesh):
    return jax.shard_map(
        on_device,
        mesh=mesh,
        in_specs=(
            P(None, AXES),
            P(AXES),
            P(None, AXES),
            P(AXES),
            P(AXES),
            P(AXES),
            P(),
            P(),
            P(),
            P(),
            P(),
            P(),
        ),
        out_specs=(P(None, AXES), P(AXES)),
        check_vma=False,
    )
```

time: 57.2 us -> 56.1 us (0.981)
  blocking collectives: 0 us -> 22.8 us
  starting transfers between devices: 41 us -> 18.5 us
  Pallas kernels: 5.08 us -> 10.7 us
  waiting for transfers between devices: 6.08 us -> 1.64 us
  local copies, waits for them, and re-layouts: 2.93 us -> 0.67 us
    all_to_all x0 -> x1, blocking collectives: none -> 22.8 us  [all_rows(): return lax.all_to_all(block, 'outer', 0, 0)]
    ppermute x8 -> x4, starting transfers between devices: 41 us -> 18.5 us  [exchange(): return lax.ppermute(block, AXES, route)]
    pallas_call x2 -> x3, Pallas kernels: 4.18 us -> 9.78 us  [the longest x1 8.58 us: on_device(): pl.pallas_call(lambda *refs: pair_kernel(feat, pair_len, *refs), out_shap...]
    ppermute x8 -> x4, waiting for transfers between devices: 6.08 us -> 1.64 us  [exchange(): return lax.ppermute(block, AXES, route)]
    unnamed x25 -> x12, local copies, waits for them, and re-layouts: 2.77 us -> 0.67 us
  transfers between devices with their start and end apart: 8 -> 4, of which waited for: 4 -> 2; matrix products, arithmetic and copies ran while one was open for 0% -> 0% of each run, Pallas kernels for 0% -> 0%
where the time goes in v3:
time: 56.1 us; the launch traced here: 55.7 us
  blocking collectives  22.8 us (41%)
  starting transfers between devices  18.5 us (33%)
  Pallas kernels  10.7 us (19%)
  waiting for transfers between devices  1.64 us (3%)
  between operations  1.37 us (2%)
  local copies, waits for them, and re-layouts  0.67 us (1%)
    all_to_all x1, blocking collectives, all_rows(): return lax.all_to_all(block, 'outer', 0, 0)  22.8 us
    ppermute x4, starting transfers between devices, exchange(): return lax.ppermute(block, AXES, route)  18.5 us
    pallas_call x1, Pallas kernels, on_device(): pl.pallas_call(lambda *refs: pair_kernel(feat, pair_len, *refs), out_shap...  8.58 us
    ppermute x4, waiting for transfers between devices, exchange(): return lax.ppermute(block, AXES, route)  1.64 us
  transfers between devices with their start and end apart: 4, of which 2 were waited for; matrix products, arithmetic and copies ran while one was open for 0% of the time, Pallas kernels for 0%

profile of v3, /device:TPU:1, one launch (start us, length us, event | category | flops | bytes accessed | tf_op | source)
XLA Modules:
  0.0 55.7 jit_solution(18353937070084310818)
XLA Ops:
  1.3 0.8 %pack_domain.1.raw_ref = f32[8,48,128]{2,1,0:T(8,128)S(1)} custom-call(f32[3,512]{1,0:T(4,128)} %pos_hbm.1, s32[1,512]{1,0:T(1,128)} %bitcast.10, s32[8,176]{1,0:T(8,128)} %lists_hbm.1, s32[6,128]{1,0:T(8,128)} %bitcast.8, s32[6,128]{1,0:T(8,128)} %bitcast.9, s32[1]{0:T(128)S(6)} %copy.14.live_ref), custom_call_target="tpu_custom_call" | custom-call | tf_op jit(solution)/shard_map/pack_domain/pallas_call | solution.py:483
  2.1 22.8 %all_to_all.5.raw_ref.refs_0_ = f32[8,48,128]{2,1,0:T(8,128)S(1)} all-to-all(f32[8,48,128]{2,1,0:T(8,128)S(1)} %pack_domain.1.raw_ref), channel_id=1, replica_groups=mesh['outer'=8,'inner'=64] {'outer'}, dimensions={0} | all-to-all | bytes 393216 | tf_op jit(solution)/shard_map/all_to_all | solution.py:42
  24.9 0.0 copy-start
  24.9 0.0 copy-start.1
  24.9 0.0 copy-start.4
  24.9 0.4 gather_sends.1
  25.3 0.0 copy-start.2
  25.3 6.9 %collective-permute-start = (f32[72,128]{1,0:T(8,128)S(1)}, f32[72,128]{1,0:T(8,128)S(1)}, u32[]{:S(2)}, u32[]{:S(2)}) collective-permute-start(f32[72,128]{1,0:T(8,128)S(1)} %get-tuple-element.12), channel_id=1, source_target_pairs={{0,63},{1,2},{2,1},{3,4},{4,3},{5,6},{6,5},{7,8},{8,7},{9,10},{10,... | collective-permute-start | bytes 110600 | tf_op jit(solution)/shard_map/ppermute | solution.py:38
  32.2 3.3 %collective-permute-start.1 = (f32[72,128]{1,0:T(8,128)S(1)}, f32[72,128]{1,0:T(8,128)S(1)}, u32[]{:S(2)}, u32[]{:S(2)}) collective-permute-start(f32[72,128]{1,0:T(8,128)S(1)} %get-tuple-element.13), channel_id=1, source_target_pairs={{0,1},{1,0},{2,3},{3,2},{4,5},{5,4},{6,7},{7,6},{8,9},{9,8},{10,11... | collective-permute-start | bytes 110600 | tf_op jit(solution)/shard_map/ppermute | solution.py:38
  35.5 0.0 collective-permute-done.refs_2_
  35.5 0.8 %collective-permute-done.1.refs_3_ = f32[72,128]{1,0:T(8,128)S(1)} collective-permute-done((f32[72,128]{1,0:T(8,128)S(1)}, f32[72,128]{1,0:T(8,128)S(1)}, u32[]{:S(2)}, u32[]{:S(2)}) %collective-permute-start.1) | collective-permute-done | bytes 36896 | tf_op jit(solution)/shard_map/ppermute | solution.py:38
  36.4 0.0 copy-start.3
  36.4 0.0 copy-start.5
  36.4 0.0 copy-done
  36.4 0.0 copy-done.1
  36.4 0.0 copy-done.4
  36.4 0.0 copy-done.2
  36.4 0.6 %copy-done.3 = bf16[7,128]{1,0:T(8,128)(2,1)S(1)} copy-done((bf16[7,128]{1,0:T(8,128)(2,1)S(1)}, bf16[7,128]{1,0:T(8,128)(2,1)}, u32[]{:S(2)}) %copy-start.3) | copy-done | bytes 1816
  37.1 0.0 copy-done.5
  37.1 8.6 %pair_terms.1 = (f32[16,128]{1,0:T(8,128)S(1)}, f32[16,128]{1,0:T(8,128)S(1)}, f32[24,128]{1,0:T(8,128)S(1)}, f32[24,128]{1,0:T(8,128)S(1)}) custom-call(f32[8,48,128]{2,1,0:T(8,128)S(1)} %all_to_all.5.raw_ref.refs_0_, f32[48,128]{1,0:T(8,128)S(1)} %get-tuple-element.11.refs_1_, f32[72,128]{1,0:T(8,128)S(1)} %collective-permute-done.refs_2_, ...), custom_call_target="tpu_custom_call" | custom-call | tf_op jit(solution)/shard_map/pair_terms/pallas_call | solution.py:520
  45.6 1.9 %collective-permute-start.2 = (f32[24,128]{1,0:T(8,128)S(1)}, f32[24,128]{1,0:T(8,128)S(1)}, u32[]{:S(2)}, u32[]{:S(2)}) collective-permute-start(f32[24,128]{1,0:T(8,128)S(1)} %get-tuple-element.16), channel_id=1, source_target_pairs={{0,63},{1,2},{2,1},{3,4},{4,3},{5,6},{6,5},{7,8},{8,7},{9,10},{10,... | collective-permute-start | bytes 36872 | tf_op jit(solution)/shard_map/ppermute | solution.py:38
  47.6 6.4 %collective-permute-start.3 = (f32[24,128]{1,0:T(8,128)S(1)}, f32[24,128]{1,0:T(8,128)S(1)}, u32[]{:S(2)}, u32[]{:S(2)}) collective-permute-start(f32[24,128]{1,0:T(8,128)S(1)} %get-tuple-element.17), channel_id=1, source_target_pairs={{0,1},{1,0},{2,3},{3,2},{4,5},{5,4},{6,7},{7,6},{8,9},{9,8},{10,11... | collective-permute-start | bytes 36872 | tf_op jit(solution)/shard_map/ppermute | solution.py:38
  54.0 0.0 collective-permute-done.2.up_ref
  54.0 0.8 %collective-permute-done.3.low_ref = f32[24,128]{1,0:T(8,128)S(1)} collective-permute-done((f32[24,128]{1,0:T(8,128)S(1)}, f32[24,128]{1,0:T(8,128)S(1)}, u32[]{:S(2)}, u32[]{:S(2)}) %collective-permute-start.3) | collective-permute-done | bytes 12320 | tf_op jit(solution)/shard_map/ppermute | solution.py:38
  54.8 0.9 %collect_terms.1 = (f32[3,512]{1,0:T(4,128)}, f32[1,512]{1,0:T(1,128)}) custom-call(f32[16,128]{1,0:T(8,128)S(1)} %get-tuple-element.14.local_ref, f32[16,128]{1,0:T(8,128)S(1)} %get-tuple-element.15.own_ref, f32[8,48,128]{2,1,0:T(8,128)S(1)} %pack_domain.1.raw_ref, f32[24,128]{1,0:T(8,128)S(1)} %collective-permute-done.2.up_ref, ...), custom_call_target="tpu_custom_call" | custom-call | tf_op jit(solution)/shard_map/collect_terms/pallas_call | solution.py:533
Async XLA Ops:
  24.9 11.4 %copy-start = (bf16[320,128]{1,0:T(8,128)(2,1)S(1)}, bf16[320,128]{1,0:T(8,128)(2,1)}, u32[]{:S(2)}) copy-start(bf16[320,128]{1,0:T(8,128)(2,1)} %refs_8_.1) | copy-start | bytes 245764
  24.9 11.4 %copy-start.1 = (bf16[128,192]{0,1:T(8,128)(2,1)S(1)}, bf16[128,192]{0,1:T(8,128)(2,1)}, u32[]{:S(2)}) copy-start(bf16[128,192]{0,1:T(8,128)(2,1)} %param.21) | copy-start | bytes 147460
  24.9 11.5 %copy-start.4 = (bf16[7,128]{1,0:T(8,128)(2,1)S(1)}, bf16[7,128]{1,0:T(8,128)(2,1)}, u32[]{:S(2)}) copy-start(bf16[7,128]{1,0:T(8,128)(2,1)} %refs_6_.1) | copy-start | bytes 5380
  25.3 11.1 %copy-start.2 = (f32[8,128]{1,0:T(8,128)S(1)}, f32[8,128]{1,0:T(8,128)}, u32[]{:S(2)}) copy-start(f32[8,128]{1,0:T(8,128)} %refs_4_.1) | copy-start | bytes 12292
  25.3 10.2 %collective-permute-start = (f32[72,128]{1,0:T(8,128)S(1)}, f32[72,128]{1,0:T(8,128)S(1)}, u32[]{:S(2)}, u32[]{:S(2)}) collective-permute-start(f32[72,128]{1,0:T(8,128)S(1)} %get-tuple-element.12), channel_id=1, source_target_pairs={{0,63},{1,2},{2,1},{3,4},{4,3},{5,6},{6,5},{7,8},{8,7},{9,10},{10,... | collective-permute-start | bytes 110600 | tf_op jit(solution)/shard_map/ppermute | solution.py:38
  32.2 4.1 %collective-permute-start.1 = (f32[72,128]{1,0:T(8,128)S(1)}, f32[72,128]{1,0:T(8,128)S(1)}, u32[]{:S(2)}, u32[]{:S(2)}) collective-permute-start(f32[72,128]{1,0:T(8,128)S(1)} %get-tuple-element.13), channel_id=1, source_target_pairs={{0,1},{1,0},{2,3},{3,2},{4,5},{5,4},{6,7},{7,6},{8,9},{9,8},{10,11... | collective-permute-start | bytes 110600 | tf_op jit(solution)/shard_map/ppermute | solution.py:38
  36.4 0.7 %copy-start.3 = (bf16[7,128]{1,0:T(8,128)(2,1)S(1)}, bf16[7,128]{1,0:T(8,128)(2,1)}, u32[]{:S(2)}) copy-start(bf16[7,128]{1,0:T(8,128)(2,1)} %refs_5_.1) | copy-start | bytes 5380
  36.4 0.7 %copy-start.5 = (bf16[128]{0:T(256)(128)(2,1)S(1)}, bf16[128]{0:T(256)(128)(2,1)}, u32[]{:S(2)}) copy-start(bf16[128]{0:T(256)(128)(2,1)} %param.23) | copy-start | bytes 772
  45.6 8.4 %collective-permute-start.2 = (f32[24,128]{1,0:T(8,128)S(1)}, f32[24,128]{1,0:T(8,128)S(1)}, u32[]{:S(2)}, u32[]{:S(2)}) collective-permute-start(f32[24,128]{1,0:T(8,128)S(1)} %get-tuple-element.16), channel_id=1, source_target_pairs={{0,63},{1,2},{2,1},{3,4},{4,3},{5,6},{6,5},{7,8},{8,7},{9,10},{10,... | collective-permute-start | bytes 36872 | tf_op jit(solution)/shard_map/ppermute | solution.py:38
  47.6 7.2 %collective-permute-start.3 = (f32[24,128]{1,0:T(8,128)S(1)}, f32[24,128]{1,0:T(8,128)S(1)}, u32[]{:S(2)}, u32[]{:S(2)}) collective-permute-start(f32[24,128]{1,0:T(8,128)S(1)} %get-tuple-element.17), channel_id=1, source_target_pairs={{0,1},{1,0},{2,3},{3,2},{4,5},{5,4},{6,7},{7,6},{8,9},{9,8},{10,11... | collective-permute-start | bytes 36872 | tf_op jit(solution)/shard_map/ppermute | solution.py:38

commit v4 on v3

v4 whole, which is shorter than its diff:
```python
import math

import jax
import jax.numpy as jnp
from jax import lax
from jax.experimental import pallas as pl
from jax.experimental.pallas import tpu as pltpu
from jax.sharding import PartitionSpec as P

AXES = ("outer", "inner")
CUTOFF = 6.0
ROOT3 = math.sqrt(3.0)
ROOT5 = math.sqrt(5.0)
ROOT15 = math.sqrt(15.0)
LANES = 128
F32 = jnp.float32
BF16 = jnp.bfloat16
SMALL = pltpu.CompilerParams(vmem_limit_bytes=8 * 1024 * 1024)
LARGE = pltpu.CompilerParams(vmem_limit_bytes=32 * 1024 * 1024)
DIRS = ((-1, -1), (-1, 0), (-1, 1), (0, -1), (0, 1), (1, -1), (1, 0), (1, 1))
SPAN = (-1, 0, 1)
TABLE, LISTS, CENTERS, NEIGH, PACKED = 0, 16, 32, 40, 48
LIVE = 38
ORDER_OF = (0, 1, 1, 1, 2, 2, 2, 2, 2)


def exchange(block, along, parity, step=1):
    outer_len = lax.axis_size("outer")
    inner_len = lax.axis_size("inner")

    def partner(i, count):
        return (i + step if i // step % 2 == parity else i - step) % count

    route = []
    for o in range(outer_len):
        for n in range(inner_len):
            if along == "outer":
                there = (partner(o, outer_len), n)
            else:
                there = (o, partner(n, inner_len))
            route.append((o * inner_len + n, there[0] * inner_len + there[1]))
    return lax.ppermute(block, AXES, route)


def dot(lhs, rhs):
    return jnp.dot(lhs, rhs, preferred_element_type=F32)


def dot_rows(lhs, rhs):
    return lax.dot_general(lhs, rhs, (((0,), (0,)), ((), ())), preferred_element_type=F32)


def parts(value, count):
    out = []
    for _ in range(count):
        piece = value.astype(BF16)
        out.append(piece)
        value = value - piece.astype(F32)
    return out


def hits(left, right):
    return jnp.where(left == right, jnp.ones((), BF16), jnp.zeros((), BF16))


def down_lanes(row):
    return jnp.broadcast_to(row, (LANES, LANES)).T.astype(BF16)


def onehot_low(low_row):
    rows = lax.broadcasted_iota(jnp.int32, (LANES, low_row.shape[1]), 0).astype(F32).astype(BF16)
    return hits(rows, low_row.astype(F32).astype(BF16))


def high_mask(high_row, group):
    rows = lax.broadcasted_iota(jnp.int32, (8, high_row.shape[1]), 0)
    return high_row == 2 * group + jnp.where(rows >= 4, 1, 0)


def gather(table, low_hot, high_row):
    size = table.shape[0]
    found = dot(jnp.concatenate(parts(table, 3), 0), low_hot)
    found = found[0:size] + found[size : 2 * size] + found[2 * size :]
    total = None
    for group in range(size // 8):
        term = jnp.where(high_mask(high_row, group), found[8 * group : 8 * group + 8], 0.0)
        total = term if total is None else total + term
    return total + pltpu.roll(total, 4, 0)


def scatter(values, low_hot_t, high_row, groups):
    spread = [jnp.where(high_mask(high_row, group), values, 0.0) for group in groups]
    spread = jnp.concatenate(spread, 0)
    size = 8 * len(groups)
    summed = dot(jnp.concatenate(parts(spread, 2), 0), low_hot_t)
    return summed[0:size] + summed[size:]


def pack_kernel(
    pos_hbm,
    spec_hbm,
    lists_hbm,
    centers_hbm,
    neigh_hbm,
    live_ref,
    out_ref,
    pos,
    spec,
    lists,
    centers,
    neigh,
    sems,
):
    fetched = []
    for j, (src, dst) in enumerate(
        (
            (pos_hbm, pos),
            (spec_hbm, spec),
            (lists_hbm, lists),
            (centers_hbm, centers),
            (neigh_hbm, neigh),
        )
    ):
        copy = pltpu.make_async_copy(src, dst, sems.at[j])
        copy.start()
        fetched.append(copy)
    for copy in fetched:
        copy.wait()
    rows = []
    for j in range(4):
        at = slice(j * LANES, (j + 1) * LANES)
        rows.append(pos[:, at])
        rows.append(spec[:, at].astype(F32))
    ids = lists[...].astype(F32)
    rest = ids.shape[1] - LANES
    rows.append(ids[:, 0:LANES])
    rows.append(jnp.concatenate([ids[:, LANES:], jnp.zeros((8, LANES - rest), F32)], 1))
    rows.append(centers[...].astype(F32))
    rows.append(jnp.full((1, LANES), live_ref[0].astype(F32)))
    rows.append(jnp.zeros((1, LANES), F32))
    rows.append(neigh[...].astype(F32))
    rows.append(jnp.zeros((2, LANES), F32))
    out_ref[...] = jnp.concatenate(rows, 0)


def weights_kernel(
    w_rad_hbm,
    emb_center_hbm,
    emb_neigh_hbm,
    w_env_hbm,
    w_lat_hbm,
    w_out_hbm,
    front_ref,
    w_env_ref,
    w_lat_ref,
    w_out_ref,
    w_rad,
    emb_center,
    emb_neigh,
    w_out,
    sems,
):
    fetched = []
    for j, (src, dst) in enumerate(
        (
            (w_rad_hbm, w_rad),
            (emb_center_hbm, emb_center),
            (emb_neigh_hbm, emb_neigh),
            (w_env_hbm, w_env_ref),
            (w_lat_hbm, w_lat_ref),
            (w_out_hbm, w_out),
        )
    ):
        copy = pltpu.make_async_copy(src, dst, sems.at[j])
        copy.start()
        fetched.append(copy)
    for copy in fetched:
        copy.wait()
    lat = w_lat_ref.shape[1]
    w1, w2, w3 = parts(w_rad[...], 3)
    none = jnp.zeros((1, lat), BF16)
    front_ref[...] = jnp.concatenate(
        [w1, w2, w1, w3, w2, w1, emb_center[...], none, emb_neigh[...], none], 0
    )
    w_lat_ref[lat:] = w_lat_ref[lat:] * jnp.full((), 2.0, BF16)
    w_out_ref[...] = jnp.broadcast_to(w_out[...], (16, lat))


def tile_of(a, dx):
    return 3 * (a + 1) + dx + 1


def sends_kernel(
    own_ref, near2_ref, near1_ref, far1_ref, far2_ref, _, far_ref, near_ref, mid_ref, raw_ref
):
    even_n = lax.axis_index("inner") % 2 == 0
    outer = lax.axis_index("outer")
    even_o = outer % 2 == 0
    even_o2 = outer // 2 % 2 == 0
    by_source = {
        -2: jnp.where(even_o2, far2_ref[...], near2_ref[...]),
        -1: jnp.where(even_o, far1_ref[...], near1_ref[...]),
        0: own_ref[...],
        1: jnp.where(even_o, near1_ref[...], far1_ref[...]),
        2: jnp.where(even_o2, near2_ref[...], far2_ref[...]),
    }
    for d, a in enumerate(SPAN):
        raw_ref[d] = by_source[a]
    rows = lax.broadcasted_iota(jnp.int32, (8, LANES), 0)
    for source in range(-2, 3):
        raw = by_source[source]
        wanted = [
            k for k in range(8) if abs(source + DIRS[k][0]) <= 1
        ]
        low = raw[LISTS : LISTS + 8].astype(jnp.int32)
        high = raw[LISTS + 8 : LISTS + 16].astype(jnp.int32)
        ids = [part[k : k + 1] for k in wanted for part in (low, high)]
        ids = jnp.concatenate(ids, 1)
        taken = gather(raw[TABLE : TABLE + 16], onehot_low(ids & 127), ids >> 7)
        tiles = {}
        for j, k in enumerate(wanted):
            at = 2 * j * LANES
            tiles[k] = jnp.where(
                rows < 4, taken[:, at : at + LANES], taken[:, at + LANES : at + 2 * LANES]
            )
        for dx in SPAN:
            a = source + dx
            if abs(a) > 1:
                continue
            t = tile_of(a, dx)
            minus, plus = tiles[DIRS.index((dx, -1))], tiles[DIRS.index((dx, 1))]
            far_ref[8 * t : 8 * t + 8] = jnp.where(even_n, minus, plus)
            near_ref[8 * t : 8 * t + 8] = jnp.where(even_n, plus, minus)
            if dx:
                m = 2 * (a + 1) + (dx + 1) // 2
                mid_ref[8 * m : 8 * m + 8] = tiles[DIRS.index((dx, 0))]


def silu_parts(pre):
    sig = 0.5 * jnp.tanh(0.5 * pre) + 0.5
    act = pre * sig
    return act, sig + act - act * sig


def half_turns(value):
    whole = jnp.floor(value + 0.5)
    rest = (value - whole) * math.pi
    sign = 1.0 - 2.0 * (whole - 2.0 * jnp.floor(whole * 0.5))
    r2 = rest * rest
    sine, cosine = -1.0 / 39916800, 1.0 / 479001600
    for term in (1.0 / 362880, -1.0 / 5040, 1.0 / 120, -1.0 / 6, 1.0):
        sine = term + r2 * sine
    for term in (-1.0 / 3628800, 1.0 / 40320, -1.0 / 720, 1.0 / 24, -0.5, 1.0):
        cosine = term + r2 * cosine
    return sign * rest * sine, sign * cosine


def pair_kernel(
    feat,
    pair_len,
    raw_ref,
    mid_ref,
    up_ref,
    low_ref,
    front_ref,
    w_env_ref,
    w_lat_ref,
    w_out_ref,
    local_ref,
    own_ref,
    back_far_ref,
    back_near_ref,
    same_ref,
    hot_t_ref,
    contrib_ref,
    gath_ref,
    back_ref,
):
    chunks = pair_len // LANES
    lat = w_lat_ref.shape[1]
    even_n = lax.axis_index("inner") % 2 == 0
    lanes = lax.broadcasted_iota(jnp.int32, (1, LANES), 1).astype(F32).astype(BF16)

    front = front_ref[...]
    w1, w2 = front[0:8], front[8:16]
    w_env = w_env_ref[...]
    w_lat = w_lat_ref[...]
    w_out = w_out_ref[0:8].astype(F32).T[:, 0:1]

    def as_row(tile):
        return jnp.concatenate([tile[i : i + 1] for i in range(chunks)], 1)

    def onehot_t(low_tile):
        return jnp.concatenate(
            [hits(down_lanes(low_tile[i : i + 1].astype(F32)), lanes) for i in range(chunks)], 0
        )

    def feat_rows(k):
        return slice(k * feat, (k + 1) * feat)

    def of_order(value, k):
        return value[feat_rows(ORDER_OF[k])]

    def domain(d):
        return slice(d * pair_len, (d + 1) * pair_len)

    def build_same(d):
        shifted = raw_ref[d, CENTERS : CENTERS + 8] - 256.0
        across = shifted.astype(BF16)
        for i in range(chunks):
            down = down_lanes(shifted[i : i + 1])
            for j in range(chunks):
                same_ref[d, i * LANES : (i + 1) * LANES, j * LANES : (j + 1) * LANES] = hits(
                    down, across[j : j + 1]
                )

    def place(d):
        a = SPAN[d]
        raw = raw_ref.at[d]
        centers = raw[CENTERS : CENTERS + 8]
        table = [raw[TABLE : TABLE + 16]]
        for dx, dy in DIRS:
            t = 8 * tile_of(a, dx)
            if dy == 0:
                m = 8 * (2 * (a + 1) + (dx + 1) // 2)
                table.append(mid_ref[m : m + 8])
                continue
            by_low, by_up = low_ref[t : t + 8], up_ref[t : t + 8]
            if dy < 0:
                table.append(jnp.where(even_n, by_low, by_up))
            else:
                table.append(jnp.where(even_n, by_up, by_low))
        table = jnp.concatenate(table, 0)
        neigh = raw[NEIGH : NEIGH + 8].astype(jnp.int32)
        ghost = neigh - 512
        listed = (ghost * 745) >> 17
        entry = ghost - 176 * listed
        is_local = neigh < 512
        neigh_low = jnp.where(is_local, neigh & 127, entry & 127)
        hot_t_ref[d] = onehot_t(neigh_low)
        neigh_high = as_row(jnp.where(is_local, neigh >> 7, 4 + 2 * listed + (entry >> 7)))
        center_ids = as_row(centers.astype(jnp.int32))
        center_high = center_ids >> 7
        at_neigh = gather(table, onehot_low(as_row(neigh_low)), neigh_high)
        at_center = gather(table[0:16], onehot_low(center_ids & 127), center_high)
        if a == 0:
            hot_t_ref[len(SPAN)] = onehot_t(centers.astype(jnp.int32) & 127)
        block = lax.broadcasted_iota(jnp.int32, (1, pair_len), 1) // 128
        mask = jnp.where(block.astype(F32) < raw[LIVE : LIVE + 1, 0:1], 1.0, 0.0)
        return at_neigh, at_center, mask, neigh_high, center_high

    placed = [place(d) for d in range(len(SPAN))]
    at_neigh, at_center, mask = (jnp.concatenate([p[i] for p in placed], 1) for i in range(3))
    width = mask.shape[1]
    moved = at_neigh - at_center
    rx, ry, rz = moved[0:1], moved[1:2], moved[2:3]
    squared = rx * rx + ry * ry + rz * rz + 1.0
    inv = lax.rsqrt(squared)
    dist = squared * inv
    ux, uy, uz = rx * inv, ry * inv, rz * inv
    slack = 1.0 - squared * (1.0 / (CUTOFF * CUTOFF))
    env = slack * slack
    scaled = env * mask
    ns = (lax.broadcasted_iota(jnp.int32, (8, width), 0) + 1).astype(F32)
    sine, cosine = half_turns(ns * (dist * (1.0 / CUTOFF)))
    scale = inv * env
    kinds = lax.broadcasted_iota(jnp.int32, (8, width), 0).astype(F32)
    hot_center = jnp.where(at_center[3:4] == kinds, 1.0, 0.0).astype(BF16)
    hot_neigh = jnp.where(at_neigh[3:4] == kinds, 1.0, 0.0).astype(BF16)
    b1, b2, b3 = parts(sine * scale, 3)
    pre = dot_rows(front, jnp.concatenate([b1, b1, b2, b1, b2, b3, hot_center, hot_neigh], 0))
    for d in range(len(SPAN)):
        build_same(d)
    latent, slope = silu_parts(pre)
    half = latent.astype(BF16)
    raw = dot(w_env, half)
    weight = raw * scaled
    shape = [
        None,
        ROOT3 * ux,
        ROOT3 * uy,
        ROOT3 * uz,
        ROOT15 * ux * uy,
        ROOT15 * uy * uz,
        0.5 * ROOT5 * (2.0 * uz * uz - ux * ux - uy * uy),
        ROOT15 * ux * uz,
        0.5 * ROOT15 * (ux * ux - uy * uy),
    ]
    shape_half = [None] + [row.astype(BF16) for row in shape[1:]]

    def spread_same(d, value, out_ref):
        at = domain(d)
        value = value[:, at]
        for k in range(9):
            rows = of_order(value, k)
            contrib_ref[d, feat_rows(k)] = (rows if k == 0 else rows * shape[k][:, at]).astype(BF16)
        out_ref[d] = dot(contrib_ref[d], same_ref[d])

    def gathered_sums(d, in_ref):
        at = domain(d)
        sums = [None, None, None]
        for k in range(9):
            term = in_ref[d, feat_rows(k)]
            if k:
                term = term * shape[k][:, at]
            order = ORDER_OF[k]
            sums[order] = term if sums[order] is None else sums[order] + term
        return jnp.concatenate(sums, 0)

    for d in range(len(SPAN)):
        spread_same(d, weight, gath_ref)
    sums = jnp.concatenate([gathered_sums(d, gath_ref) for d in range(len(SPAN))], 1)
    joined = jnp.concatenate([half, (weight * sums).astype(BF16)], 0)
    update, slope2 = silu_parts(dot_rows(w_lat, joined))
    refined = (latent + update).astype(BF16)
    raw_energy = dot(w_out_ref[...], refined)[0:1]
    d_refined = scaled * w_out
    d_joined = dot(w_lat, (d_refined * slope2).astype(BF16))
    d_latent = d_refined + d_joined[:lat]
    d_inv = d_joined[lat:]
    d_weight = d_inv * sums
    d_sums = d_inv * weight
    for d in range(len(SPAN)):
        spread_same(d, d_sums, back_ref)
    d_order, d_shape = [], []
    for d in range(len(SPAN)):
        at = domain(d)
        d_order.append(gathered_sums(d, back_ref))
        here = []
        for k in range(1, 9):
            both = (
                of_order(d_sums, k)[:, at] * gath_ref[d, feat_rows(k)]
                + of_order(weight, k)[:, at] * back_ref[d, feat_rows(k)]
            )
            here.append(jnp.sum(both, axis=0, keepdims=True))
        d_shape.append(here)
    d_weight = d_weight + jnp.concatenate(d_order, 1)
    d_shape = [None] + [jnp.concatenate([here[k] for here in d_shape], 1) for k in range(8)]
    d_scaled = raw_energy + jnp.sum(d_weight * raw, axis=0, keepdims=True)
    d_latent = d_latent + scaled * dot_rows(w_env, d_weight.astype(BF16))
    d_pre = (d_latent * slope).astype(BF16)
    d_basis = dot(jnp.concatenate([w1, w2], 0), d_pre)
    d_basis = d_basis[0:8] + d_basis[8:16]

    along = jnp.sum(d_basis * sine, axis=0, keepdims=True)
    turned = jnp.sum(d_basis * cosine * ns, axis=0, keepdims=True)
    d_env = along * inv + mask * d_scaled
    dx = (
        ROOT3 * d_shape[1]
        + ROOT15 * (uy * d_shape[4] + uz * d_shape[7] + ux * d_shape[8])
        - ROOT5 * ux * d_shape[6]
    )
    dy = (
        ROOT3 * d_shape[2]
        + ROOT15 * (ux * d_shape[4] + uz * d_shape[5] - uy * d_shape[8])
        - ROOT5 * uy * d_shape[6]
    )
    dz = (
        ROOT3 * d_shape[3]
        + ROOT15 * (uy * d_shape[5] + ux * d_shape[7])
        + 2.0 * ROOT5 * uz * d_shape[6]
    )
    d_inv = along * env + dx * rx + dy * ry + dz * rz
    d_dist = turned * (math.pi / CUTOFF) * scale - d_inv * inv * inv
    d_squared = 0.5 * inv * d_dist - (2.0 / (CUTOFF * CUTOFF)) * slack * d_env
    gx = dx * inv + 2.0 * rx * d_squared
    gy = dy * inv + 2.0 * ry * d_squared
    gz = dz * inv + 2.0 * rz * d_squared
    rows4 = [gx, gy, gz, 0.5 * scaled * raw_energy]
    values = jnp.concatenate(rows4 + rows4, 0)
    rows = lax.broadcasted_iota(jnp.int32, (8, width), 0)
    flipped = jnp.where((rows & 3) == 3, values, -values)
    for d, a in enumerate(SPAN):
        neigh_high, center_high = placed[d][3:]
        groups = [2 + DIRS.index((a, -1)), 2 + DIRS.index((a, 1))]
        groups += [2 + DIRS.index((a, 0))] if a else [0, 1]
        terms = scatter(flipped[:, domain(d)], hot_t_ref[d], neigh_high, groups)
        minus, plus = terms[0:8], terms[8:16]
        at = slice(8 * d, 8 * d + 8)
        back_far_ref[at] = jnp.where(even_n, plus, minus)
        back_near_ref[at] = jnp.where(even_n, minus, plus)
        if a:
            own_ref[8 * (d // 2) : 8 * (d // 2) + 8] = terms[16:24]
        else:
            center_terms = scatter(values[:, domain(d)], hot_t_ref[len(SPAN)], center_high, (0, 1))
            local_ref[...] = terms[16:32] + center_terms


def collect_kernel(local_ref, own_ref, raw_ref, up_ref, low_ref, forces_ref, energy_ref):
    even_n = lax.axis_index("inner") % 2 == 0
    plus = jnp.where(even_n, low_ref[...], up_ref[...])
    minus = jnp.where(even_n, up_ref[...], low_ref[...])
    lists_low = raw_ref[LISTS : LISTS + 8].astype(jnp.int32)
    lists_high = raw_ref[LISTS + 8 : LISTS + 16].astype(jnp.int32)
    rows = lax.broadcasted_iota(jnp.int32, (8, LANES), 0)
    ids, values = [], []
    for k, (dx, dy) in enumerate(DIRS):
        ids += [lists_low[k : k + 1], lists_high[k : k + 1]]
        if dy == 0:
            at = 8 * ((dx + 1) // 2)
            tile = own_ref[at : at + 8]
        else:
            at = 8 * (dx + 1)
            tile = (minus if dy < 0 else plus)[at : at + 8]
        turned = pltpu.roll(tile, 4, 0)
        values += [jnp.where(rows < 4, tile, turned), jnp.where(rows < 4, turned, tile)]
    ids = jnp.concatenate(ids, 1)
    values = jnp.concatenate(values, 1)
    hot_t = []
    lanes = lax.broadcasted_iota(jnp.int32, (1, LANES), 1).astype(F32).astype(BF16)
    for k in range(len(DIRS)):
        for tile in (lists_low, lists_high):
            hot_t.append(hits(down_lanes((tile[k : k + 1] & 127).astype(F32)), lanes))
    total = local_ref[...] + scatter(values, jnp.concatenate(hot_t, 0), ids >> 7, (0, 1))
    for j in range(4):
        forces_ref[:, j * LANES : (j + 1) * LANES] = total[4 * j : 4 * j + 3]
        energy_ref[:, j * LANES : (j + 1) * LANES] = total[4 * j + 3 : 4 * j + 4]


def on_device(
    positions,
    species,
    send_lists,
    centers,
    neighbours,
    live_blocks,
    w_rad,
    emb_center,
    emb_neigh,
    w_env,
    w_lat,
    w_out,
):
    pair_len = centers.shape[0]
    atom_count = positions.shape[1]
    feat = w_env.shape[1] // 3
    lat = w_env.shape[0]
    chunks = pair_len // LANES

    def rows(count):
        return jax.ShapeDtypeStruct((count, LANES), F32)

    packed = pl.pallas_call(
        pack_kernel,
        out_shape=rows(PACKED),
        in_specs=[pl.BlockSpec(memory_space=pltpu.HBM)] * 5
        + [pl.BlockSpec(memory_space=pltpu.SMEM)],
        scratch_shapes=[
            pltpu.VMEM(positions.shape, F32),
            pltpu.VMEM((1, atom_count), jnp.int32),
            pltpu.VMEM(send_lists.shape, jnp.int32),
            pltpu.VMEM((chunks, LANES), jnp.int32),
            pltpu.VMEM((chunks, LANES), jnp.int32),
            pltpu.SemaphoreType.DMA((5,)),
        ],
        compiler_params=SMALL,
        name="pack_domain",
    )(
        *(
            pltpu.with_memory_space_constraint(value, pltpu.HBM)
            for value in (
                positions,
                species.reshape(1, atom_count),
                send_lists,
                centers.reshape(chunks, LANES),
                neighbours.reshape(chunks, LANES),
            )
        ),
        live_blocks,
    )
    weights = pl.pallas_call(
        weights_kernel,
        out_shape=[
            jax.ShapeDtypeStruct((64, lat), BF16),
            jax.ShapeDtypeStruct((w_env.shape[1], lat), BF16),
            jax.ShapeDtypeStruct(w_lat.shape, BF16),
            jax.ShapeDtypeStruct((16, lat), BF16),
        ],
        in_specs=[pl.BlockSpec(memory_space=pltpu.HBM)] * 6,
        scratch_shapes=[
            pltpu.VMEM(w_rad.shape, F32),
            pltpu.VMEM(emb_center.shape, BF16),
            pltpu.VMEM(emb_neigh.shape, BF16),
            pltpu.VMEM((1, lat), BF16),
            pltpu.SemaphoreType.DMA((6,)),
        ],
        compiler_params=SMALL,
        cost_estimate=pl.CostEstimate(flops=0, bytes_accessed=4_000_000, transcendentals=0),
        name="place_weights",
    )(
        *(
            pltpu.with_memory_space_constraint(value, pltpu.HBM)
            for value in (w_rad, emb_center, emb_neigh, w_env.T, w_lat, w_out.reshape(1, -1))
        )
    )
    far2 = exchange(packed, "outer", 1, 2)
    far1 = exchange(packed, "outer", 1)
    near1 = exchange(packed, "outer", 0)
    near2 = exchange(packed, "outer", 0, 2)
    far, near, mid, raw = pl.pallas_call(
        sends_kernel,
        out_shape=[
            rows(72),
            rows(72),
            rows(48),
            jax.ShapeDtypeStruct((len(SPAN), PACKED, LANES), F32),
        ],
        compiler_params=SMALL,
        name="gather_sends",
    )(packed, near2, near1, far1, far2, weights[3])
    up = exchange(far, "inner", 1)
    low = exchange(near, "inner", 0)
    local, own, far, near = pl.pallas_call(
        lambda *refs: pair_kernel(feat, pair_len, *refs),
        out_shape=[rows(16), rows(16), rows(24), rows(24)],
        scratch_shapes=[
            pltpu.VMEM((len(SPAN), pair_len, pair_len), BF16),
            pltpu.VMEM((len(SPAN) + 1, pair_len, LANES), BF16),
            pltpu.VMEM((len(SPAN), 9 * feat, pair_len), BF16),
            pltpu.VMEM((len(SPAN), 9 * feat, pair_len), F32),
            pltpu.VMEM((len(SPAN), 9 * feat, pair_len), F32),
        ],
        compiler_params=LARGE,
        name="pair_terms",
    )(raw, mid, up, low, *weights)
    up = exchange(far, "inner", 1)
    low = exchange(near, "inner", 0)
    forces, energy = pl.pallas_call(
        collect_kernel,
        out_shape=[
            jax.ShapeDtypeStruct((3, atom_count), F32),
            jax.ShapeDtypeStruct((1, atom_count), F32),
        ],
        compiler_params=SMALL,
        name="collect_terms",
    )(local, own, packed, up, low)
    return forces, energy.reshape(atom_count)


def solution(mesh):
    return jax.shard_map(
        on_device,
        mesh=mesh,
        in_specs=(
            P(None, AXES),
            P(AXES),
            P(None, AXES),
            P(AXES),
            P(AXES),
            P(AXES),
            P(),
            P(),
            P(),
            P(),
            P(),
            P(),
        ),
        out_specs=(P(None, AXES), P(AXES)),
        check_vma=False,
    )
```

time: 56.1 us -> 57 us (1.016)
  blocking collectives: 22.8 us -> 0 us
  starting transfers between devices: 18.5 us -> 40.2 us
  waiting for transfers between devices: 1.64 us -> 3.34 us
  Pallas kernels: 10.7 us -> 11.7 us
  local copies, waits for them, and re-layouts: 0.67 us -> 0 us
    all_to_all x1 -> x0, blocking collectives: 22.8 us -> none  [all_rows(): return lax.all_to_all(block, 'outer', 0, 0)]
    ppermute x4 -> x8, starting transfers between devices: 18.5 us -> 40.2 us  [exchange(): return lax.ppermute(block, AXES, route)]
    ppermute x4 -> x8, waiting for transfers between devices: 1.64 us -> 3.34 us  [exchange(): return lax.ppermute(block, AXES, route)]
    pallas_call x2 -> x3, Pallas kernels: 1.2 us -> 2.22 us  [the longest x1 1.04 us: on_device(): pl.pallas_call(weights_kernel, out_shape=[jax.ShapeDtypeStruct((64, lat),...]
    unnamed x12 -> x0, local copies, waits for them, and re-layouts: 0.67 us -> none
  transfers between devices with their start and end apart: 4 -> 8, of which waited for: 2 -> 3; matrix products, arithmetic and copies ran while one was open for 0% -> 0% of each run, Pallas kernels for 0% -> 2%
where the time goes in v4:
time: 57 us; the launch traced here: 56.6 us
  starting transfers between devices  40.2 us (71%)
  Pallas kernels  11.7 us (21%)
  waiting for transfers between devices  3.34 us (6%)
  between operations  1.39 us (2%)
    ppermute x8, starting transfers between devices, exchange(): return lax.ppermute(block, AXES, route)  40.2 us
    pallas_call x1, Pallas kernels, on_device(): pl.pallas_call(lambda *refs: pair_kernel(feat, pair_len, *refs), out_shap...  8.5 us
    ppermute x8, waiting for transfers between devices, exchange(): return lax.ppermute(block, AXES, route)  3.34 us
  transfers between devices with their start and end apart: 8, of which 3 were waited for; matrix products, arithmetic and copies ran while one was open for 0% of the time, Pallas kernels for 2%

profile of v4, /device:TPU:1, one launch (start us, length us, event | category | flops | bytes accessed | tf_op | source)
XLA Modules:
  0.0 56.6 jit_solution(13081567867904839654)
XLA Ops:
  1.3 0.8 %pack_domain.1.own_ref.raw_ref = f32[48,128]{1,0:T(8,128)S(1)} custom-call(f32[3,512]{1,0:T(4,128)} %pos_hbm.1, s32[1,512]{1,0:T(1,128)} %bitcast.9, s32[8,176]{1,0:T(8,128)} %lists_hbm.1, s32[6,128]{1,0:T(8,128)} %bitcast.7, s32[6,128]{1,0:T(8,128)} %bitcast.8, s32[1]{0:T(128)S(6)} %copy.14.live_ref), custom_call_target="tpu_custom_call" | custom-call | tf_op jit(solution)/shard_map/pack_domain/pallas_call | solution.py:543
  2.1 13.9 %collective-permute-start.3 = (f32[48,128]{1,0:T(8,128)S(1)}, f32[48,128]{1,0:T(8,128)S(1)}, u32[]{:S(2)}, u32[]{:S(2)}) collective-permute-start(f32[48,128]{1,0:T(8,128)S(1)} %pack_domain.1.own_ref.raw_ref), channel_id=1, source_target_pairs={{0,384},{1,385},{2,386},{3,387},{4,388},{5,389},{6,390},{7,391},{8... | collective-permute-start | bytes 73736 | tf_op jit(solution)/shard_map/ppermute | solution.py:42
  16.0 1.9 %collective-permute-start.2 = (f32[48,128]{1,0:T(8,128)S(1)}, f32[48,128]{1,0:T(8,128)S(1)}, u32[]{:S(2)}, u32[]{:S(2)}) collective-permute-start(f32[48,128]{1,0:T(8,128)S(1)} %pack_domain.1.own_ref.raw_ref), channel_id=1, source_target_pairs={{0,448},{1,449},{2,450},{3,451},{4,452},{5,453},{6,454},{7,455},{8... | collective-permute-start | bytes 73736 | tf_op jit(solution)/shard_map/ppermute | solution.py:42
  17.9 2.2 %collective-permute-start.1 = (f32[48,128]{1,0:T(8,128)S(1)}, f32[48,128]{1,0:T(8,128)S(1)}, u32[]{:S(2)}, u32[]{:S(2)}) collective-permute-start(f32[48,128]{1,0:T(8,128)S(1)} %pack_domain.1.own_ref.raw_ref), channel_id=1, source_target_pairs={{0,64},{1,65},{2,66},{3,67},{4,68},{5,69},{6,70},{7,71},{8,72},{9,... | collective-permute-start | bytes 73736 | tf_op jit(solution)/shard_map/ppermute | solution.py:42
  20.2 3.7 %collective-permute-start = (f32[48,128]{1,0:T(8,128)S(1)}, f32[48,128]{1,0:T(8,128)S(1)}, u32[]{:S(2)}, u32[]{:S(2)}) collective-permute-start(f32[48,128]{1,0:T(8,128)S(1)} %pack_domain.1.own_ref.raw_ref), channel_id=1, source_target_pairs={{0,128},{1,129},{2,130},{3,131},{4,132},{5,133},{6,134},{7,135},{8... | collective-permute-start | bytes 73736 | tf_op jit(solution)/shard_map/ppermute | solution.py:42
  23.9 1.0 %place_weights.1 = (bf16[64,128]{1,0:T(8,128)(2,1)S(1)}, bf16[192,128]{1,0:T(8,128)(2,1)S(1)}, bf16[320,128]{1,0:T(8,128)(2,1)S(1)}, bf16[16,128]{1,0:T(8,128)(2,1)S(1)}) custom-call(f32[8,128]{1,0:T(8,128)} %w_rad_hbm.1, bf16[7,128]{1,0:T(8,128)(2,1)} %emb_center_hbm.1, bf16[7,128]{1,0:T(8,128)(2,1)} %emb_neigh_hbm.1, bf16[192,128]{1,0:T(8,128)(2,1)} %bitcast.6, ...), custom_call_target="tpu_custom_call" | custom-call | bytes 4000000 | tf_op jit(solution)/shard_map/place_weights/pallas_call | solution.py:571
  24.9 0.0 collective-permute-done.3.far2_ref
  24.9 1.7 %collective-permute-done.2.far1_ref = f32[48,128]{1,0:T(8,128)S(1)} collective-permute-done((f32[48,128]{1,0:T(8,128)S(1)}, f32[48,128]{1,0:T(8,128)S(1)}, u32[]{:S(2)}, u32[]{:S(2)}) %collective-permute-start.2) | collective-permute-done | bytes 24608 | tf_op jit(solution)/shard_map/ppermute | solution.py:42
  26.6 0.0 collective-permute-done.1.near1_ref
  26.6 0.0 collective-permute-done.near2_ref
  26.6 0.4 gather_sends.1
  27.0 5.3 %collective-permute-start.4 = (f32[72,128]{1,0:T(8,128)S(1)}, f32[72,128]{1,0:T(8,128)S(1)}, u32[]{:S(2)}, u32[]{:S(2)}) collective-permute-start(f32[72,128]{1,0:T(8,128)S(1)} %get-tuple-element.19), channel_id=1, source_target_pairs={{0,63},{1,2},{2,1},{3,4},{4,3},{5,6},{6,5},{7,8},{8,7},{9,10},{10,... | collective-permute-start | bytes 110600 | tf_op jit(solution)/shard_map/ppermute | solution.py:42
  32.3 4.8 %collective-permute-start.5 = (f32[72,128]{1,0:T(8,128)S(1)}, f32[72,128]{1,0:T(8,128)S(1)}, u32[]{:S(2)}, u32[]{:S(2)}) collective-permute-start(f32[72,128]{1,0:T(8,128)S(1)} %get-tuple-element.20), channel_id=1, source_target_pairs={{0,1},{1,0},{2,3},{3,2},{4,5},{5,4},{6,7},{7,6},{8,9},{9,8},{10,11... | collective-permute-start | bytes 110600 | tf_op jit(solution)/shard_map/ppermute | solution.py:42
  37.1 0.0 collective-permute-done.4.refs_2_
  37.2 0.8 %collective-permute-done.5.refs_3_ = f32[72,128]{1,0:T(8,128)S(1)} collective-permute-done((f32[72,128]{1,0:T(8,128)S(1)}, f32[72,128]{1,0:T(8,128)S(1)}, u32[]{:S(2)}, u32[]{:S(2)}) %collective-permute-start.5) | collective-permute-done | bytes 36896 | tf_op jit(solution)/shard_map/ppermute | solution.py:42
  38.0 8.5 %pair_terms.1 = (f32[16,128]{1,0:T(8,128)S(1)}, f32[16,128]{1,0:T(8,128)S(1)}, f32[24,128]{1,0:T(8,128)S(1)}, f32[24,128]{1,0:T(8,128)S(1)}) custom-call(f32[3,48,128]{2,1,0:T(8,128)S(1)} %get-tuple-element.17.refs_0_, f32[48,128]{1,0:T(8,128)S(1)} %get-tuple-element.18.refs_1_, f32[72,128]{1,0:T(8,128)S(1)} %collective-permute-done.4.refs_2_, ...), custom_call_target="tpu_custom_call" | custom-call | tf_op jit(solution)/shard_map/pair_terms/pallas_call | solution.py:613
  46.5 1.9 %collective-permute-start.6 = (f32[24,128]{1,0:T(8,128)S(1)}, f32[24,128]{1,0:T(8,128)S(1)}, u32[]{:S(2)}, u32[]{:S(2)}) collective-permute-start(f32[24,128]{1,0:T(8,128)S(1)} %get-tuple-element.26), channel_id=1, source_target_pairs={{0,63},{1,2},{2,1},{3,4},{4,3},{5,6},{6,5},{7,8},{8,7},{9,10},{10,... | collective-permute-start | bytes 36872 | tf_op jit(solution)/shard_map/ppermute | solution.py:42
  48.4 6.4 %collective-permute-start.7 = (f32[24,128]{1,0:T(8,128)S(1)}, f32[24,128]{1,0:T(8,128)S(1)}, u32[]{:S(2)}, u32[]{:S(2)}) collective-permute-start(f32[24,128]{1,0:T(8,128)S(1)} %get-tuple-element.27), channel_id=1, source_target_pairs={{0,1},{1,0},{2,3},{3,2},{4,5},{5,4},{6,7},{7,6},{8,9},{9,8},{10,11... | collective-permute-start | bytes 36872 | tf_op jit(solution)/shard_map/ppermute | solution.py:42
  54.8 0.0 collective-permute-done.6.up_ref
  54.8 0.8 %collective-permute-done.7.low_ref = f32[24,128]{1,0:T(8,128)S(1)} collective-permute-done((f32[24,128]{1,0:T(8,128)S(1)}, f32[24,128]{1,0:T(8,128)S(1)}, u32[]{:S(2)}, u32[]{:S(2)}) %collective-permute-start.7) | collective-permute-done | bytes 12320 | tf_op jit(solution)/shard_map/ppermute | solution.py:42
  55.7 1.0 %collect_terms.1 = (f32[3,512]{1,0:T(4,128)}, f32[1,512]{1,0:T(1,128)}) custom-call(f32[16,128]{1,0:T(8,128)S(1)} %get-tuple-element.24.local_ref, f32[16,128]{1,0:T(8,128)S(1)} %get-tuple-element.25.own_ref, f32[48,128]{1,0:T(8,128)S(1)} %pack_domain.1.own_ref.raw_ref, f32[24,128]{1,0:T(8,128)S(1)} %collective-permute-done.6.up_ref, ...), custom_call_target="tpu_custom_call" | custom-call | tf_op jit(solution)/shard_map/collect_terms/pallas_call | solution.py:628
Async XLA Ops:
  2.1 22.8 %collective-permute-start.3 = (f32[48,128]{1,0:T(8,128)S(1)}, f32[48,128]{1,0:T(8,128)S(1)}, u32[]{:S(2)}, u32[]{:S(2)}) collective-permute-start(f32[48,128]{1,0:T(8,128)S(1)} %pack_domain.1.own_ref.raw_ref), channel_id=1, source_target_pairs={{0,384},{1,385},{2,386},{3,387},{4,388},{5,389},{6,390},{7,391},{8... | collective-permute-start | bytes 73736 | tf_op jit(solution)/shard_map/ppermute | solution.py:42
  16.0 10.6 %collective-permute-start.2 = (f32[48,128]{1,0:T(8,128)S(1)}, f32[48,128]{1,0:T(8,128)S(1)}, u32[]{:S(2)}, u32[]{:S(2)}) collective-permute-start(f32[48,128]{1,0:T(8,128)S(1)} %pack_domain.1.own_ref.raw_ref), channel_id=1, source_target_pairs={{0,448},{1,449},{2,450},{3,451},{4,452},{5,453},{6,454},{7,455},{8... | collective-permute-start | bytes 73736 | tf_op jit(solution)/shard_map/ppermute | solution.py:42
  17.9 8.7 %collective-permute-start.1 = (f32[48,128]{1,0:T(8,128)S(1)}, f32[48,128]{1,0:T(8,128)S(1)}, u32[]{:S(2)}, u32[]{:S(2)}) collective-permute-start(f32[48,128]{1,0:T(8,128)S(1)} %pack_domain.1.own_ref.raw_ref), channel_id=1, source_target_pairs={{0,64},{1,65},{2,66},{3,67},{4,68},{5,69},{6,70},{7,71},{8,72},{9,... | collective-permute-start | bytes 73736 | tf_op jit(solution)/shard_map/ppermute | solution.py:42
  20.2 6.5 %collective-permute-start = (f32[48,128]{1,0:T(8,128)S(1)}, f32[48,128]{1,0:T(8,128)S(1)}, u32[]{:S(2)}, u32[]{:S(2)}) collective-permute-start(f32[48,128]{1,0:T(8,128)S(1)} %pack_domain.1.own_ref.raw_ref), channel_id=1, source_target_pairs={{0,128},{1,129},{2,130},{3,131},{4,132},{5,133},{6,134},{7,135},{8... | collective-permute-start | bytes 73736 | tf_op jit(solution)/shard_map/ppermute | solution.py:42
  27.0 10.1 %collective-permute-start.4 = (f32[72,128]{1,0:T(8,128)S(1)}, f32[72,128]{1,0:T(8,128)S(1)}, u32[]{:S(2)}, u32[]{:S(2)}) collective-permute-start(f32[72,128]{1,0:T(8,128)S(1)} %get-tuple-element.19), channel_id=1, source_target_pairs={{0,63},{1,2},{2,1},{3,4},{4,3},{5,6},{6,5},{7,8},{8,7},{9,10},{10,... | collective-permute-start | bytes 110600 | tf_op jit(solution)/shard_map/ppermute | solution.py:42
  32.3 5.7 %collective-permute-start.5 = (f32[72,128]{1,0:T(8,128)S(1)}, f32[72,128]{1,0:T(8,128)S(1)}, u32[]{:S(2)}, u32[]{:S(2)}) collective-permute-start(f32[72,128]{1,0:T(8,128)S(1)} %get-tuple-element.20), channel_id=1, source_target_pairs={{0,1},{1,0},{2,3},{3,2},{4,5},{5,4},{6,7},{7,6},{8,9},{9,8},{10,11... | collective-permute-start | bytes 110600 | tf_op jit(solution)/shard_map/ppermute | solution.py:42
  46.5 8.3 %collective-permute-start.6 = (f32[24,128]{1,0:T(8,128)S(1)}, f32[24,128]{1,0:T(8,128)S(1)}, u32[]{:S(2)}, u32[]{:S(2)}) collective-permute-start(f32[24,128]{1,0:T(8,128)S(1)} %get-tuple-element.26), channel_id=1, source_target_pairs={{0,63},{1,2},{2,1},{3,4},{4,3},{5,6},{6,5},{7,8},{8,7},{9,10},{10,... | collective-permute-start | bytes 36872 | tf_op jit(solution)/shard_map/ppermute | solution.py:42
  48.4 7.2 %collective-permute-start.7 = (f32[24,128]{1,0:T(8,128)S(1)}, f32[24,128]{1,0:T(8,128)S(1)}, u32[]{:S(2)}, u32[]{:S(2)}) collective-permute-start(f32[24,128]{1,0:T(8,128)S(1)} %get-tuple-element.27), channel_id=1, source_target_pairs={{0,1},{1,0},{2,3},{3,2},{4,5},{5,4},{6,7},{7,6},{8,9},{9,8},{10,11... | collective-permute-start | bytes 36872 | tf_op jit(solution)/shard_map/ppermute | solution.py:42

commit v5 on v4

--- a/solution.py
+++ b/solution.py
@@ -18,28 +18,40 @@
 SMALL = pltpu.CompilerParams(vmem_limit_bytes=8 * 1024 * 1024)
 LARGE = pltpu.CompilerParams(vmem_limit_bytes=32 * 1024 * 1024)
 DIRS = ((-1, -1), (-1, 0), (-1, 1), (0, -1), (0, 1), (1, -1), (1, 0), (1, 1))
-SPAN = (-1, 0, 1)
 TABLE, LISTS, CENTERS, NEIGH, PACKED = 0, 16, 32, 40, 48
 LIVE = 38
 ORDER_OF = (0, 1, 1, 1, 2, 2, 2, 2, 2)
 
 
-def exchange(block, along, parity, step=1):
+def permute(block, place):
     outer_len = lax.axis_size("outer")
     inner_len = lax.axis_size("inner")
-
-    def partner(i, count):
-        return (i + step if i // step % 2 == parity else i - step) % count
-
     route = []
     for o in range(outer_len):
         for n in range(inner_len):
-            if along == "outer":
-                there = (partner(o, outer_len), n)
-            else:
-                there = (o, partner(n, inner_len))
-            route.append((o * inner_len + n, there[0] * inner_len + there[1]))
+            there = place(o, n)
+            if there is not None:
+                to = there[0] % outer_len * inner_len + there[1] % inner_len
+                route.append((o * inner_len + n, to))
     return lax.ppermute(block, AXES, route)
+
+
+def swap_inner(block, parity):
+    return permute(block, lambda o, n: (o, n + 1 if n % 2 == parity else n - 1))
+
+
+def swap_outer(block, parity, rows):
+    def place(o, n):
+        return (o + 1 if o % 2 == parity else o - 1, n) if o in rows else None
+
+    return permute(block, place)
+
+
+def over_border(block):
+    def place(o, n):
+        return {1: (o - 2, n), 2: (o + 2, n)}.get(o % 4)
+
+    return permute(block, place)
 
 
 def dot(lhs, rhs):
@@ -186,54 +198,60 @@
     w_out_ref[...] = jnp.broadcast_to(w_out[...], (16, lat))
 
 
-def tile_of(a, dx):
-    return 3 * (a + 1) + dx + 1
+def tile_at(extra, side):
+    return 8 * (3 * extra + 1 - side)
 
 
 def sends_kernel(
-    own_ref, near2_ref, near1_ref, far1_ref, far2_ref, _, far_ref, near_ref, mid_ref, raw_ref
+    own_ref, low_ref, border_ref, cross_ref, high_ref, _, far_ref, near_ref, mid_ref, raw_ref
 ):
     even_n = lax.axis_index("inner") % 2 == 0
     outer = lax.axis_index("outer")
-    even_o = outer % 2 == 0
-    even_o2 = outer // 2 % 2 == 0
-    by_source = {
-        -2: jnp.where(even_o2, far2_ref[...], near2_ref[...]),
-        -1: jnp.where(even_o, far1_ref[...], near1_ref[...]),
-        0: own_ref[...],
-        1: jnp.where(even_o, near1_ref[...], far1_ref[...]),
-        2: jnp.where(even_o2, near2_ref[...], far2_ref[...]),
-    }
-    for d, a in enumerate(SPAN):
-        raw_ref[d] = by_source[a]
+    odd = outer % 2 == 1
     rows = lax.broadcasted_iota(jnp.int32, (8, LANES), 0)
-    for source in range(-2, 3):
-        raw = by_source[source]
-        wanted = [
-            k for k in range(8) if abs(source + DIRS[k][0]) <= 1
-        ]
-        low = raw[LISTS : LISTS + 8].astype(jnp.int32)
-        high = raw[LISTS + 8 : LISTS + 16].astype(jnp.int32)
-        ids = [part[k : k + 1] for k in wanted for part in (low, high)]
+    own, cross = own_ref[...], cross_ref[...]
+    beside = jnp.where(outer < lax.axis_size("outer") // 2, low_ref[...], high_ref[...])
+    raw_ref[0] = own
+    raw_ref[1] = cross
+
+    def tiles_of(raw, sides):
+        halves = [raw[LISTS + 8 * i : LISTS + 8 * i + 8].astype(jnp.int32) for i in range(2)]
+        names, ids = [], []
+        for side in sides:
+            if side == 0:
+                picked = [half[3:5] for half in halves]
+                names += [(0, -1), (0, 1)]
+            else:
+                upper = odd if side > 0 else jnp.logical_not(odd)
+                picked = [jnp.where(upper, half[5:8], half[0:3]) for half in halves]
+                names += [(side, dy) for dy in (-1, 0, 1)]
+            for i in range(picked[0].shape[0]):
+                ids += [picked[0][i : i + 1], picked[1][i : i + 1]]
         ids = jnp.concatenate(ids, 1)
         taken = gather(raw[TABLE : TABLE + 16], onehot_low(ids & 127), ids >> 7)
         tiles = {}
-        for j, k in enumerate(wanted):
+        for j, name in enumerate(names):
             at = 2 * j * LANES
-            tiles[k] = jnp.where(
+            tiles[name] = jnp.where(
                 rows < 4, taken[:, at : at + LANES], taken[:, at + LANES : at + 2 * LANES]
             )
-        for dx in SPAN:
-            a = source + dx
-            if abs(a) > 1:
-                continue
-            t = tile_of(a, dx)
-            minus, plus = tiles[DIRS.index((dx, -1))], tiles[DIRS.index((dx, 1))]
-            far_ref[8 * t : 8 * t + 8] = jnp.where(even_n, minus, plus)
-            near_ref[8 * t : 8 * t + 8] = jnp.where(even_n, plus, minus)
-            if dx:
-                m = 2 * (a + 1) + (dx + 1) // 2
-                mid_ref[8 * m : 8 * m + 8] = tiles[DIRS.index((dx, 0))]
+        return tiles
+
+    by_own = tiles_of(own, (1, 0))
+    by_cross = tiles_of(cross, (0, -1))
+    by_beside = tiles_of(beside, (1,))
+    by_border = tiles_of(border_ref[...], (-1,))
+    sources = ({1: by_beside, 0: by_own, -1: by_cross}, {1: by_own, 0: by_cross, -1: by_border})
+    for extra in range(2):
+        for side in (1, 0, -1):
+            tiles = sources[extra][side]
+            minus, plus = tiles[side, -1], tiles[side, 1]
+            at = tile_at(extra, side)
+            far_ref[at : at + 8] = jnp.where(even_n, minus, plus)
+            near_ref[at : at + 8] = jnp.where(even_n, plus, minus)
+            if side:
+                m = 8 * (2 * extra + (1 - side) // 2)
+                mid_ref[m : m + 8] = tiles[side, 0]
 
 
 def silu_parts(pre):
@@ -255,7 +273,15 @@
     return sign * rest * sine, sign * cosine
 
 
-def pair_kernel(
+def pair_kernel(feat, pair_len, *refs):
+    place = lax.axis_index("outer") % 4
+    at_border = (place == 0) | (place == 3)
+    pl.when(at_border)(lambda: pair_body(2, feat, pair_len, *refs))
+    pl.when(jnp.logical_not(at_border))(lambda: pair_body(1, feat, pair_len, *refs))
+
+
+def pair_body(
+    count,
     feat,
     pair_len,
     raw_ref,
@@ -267,7 +293,8 @@
     w_lat_ref,
     w_out_ref,
     local_ref,
-    own_ref,
+    edge_near_ref,
+    edge_far_ref,
     back_far_ref,
     back_near_ref,
     same_ref,
@@ -279,6 +306,7 @@
     chunks = pair_len // LANES
     lat = w_lat_ref.shape[1]
     even_n = lax.axis_index("inner") % 2 == 0
+    odd = lax.axis_index("outer") % 2 == 1
     lanes = lax.broadcasted_iota(jnp.int32, (1, LANES), 1).astype(F32).astype(BF16)
 
     front = front_ref[...]
@@ -315,21 +343,23 @@
                 )
 
     def place(d):
-        a = SPAN[d]
         raw = raw_ref.at[d]
         centers = raw[CENTERS : CENTERS + 8]
         table = [raw[TABLE : TABLE + 16]]
+
+        def ghost_tile(side, dy):
+            if dy == 0:
+                m = 8 * (2 * d + (1 - side) // 2)
+                return mid_ref[m : m + 8]
+            t = tile_at(d, side)
+            by_low, by_up = low_ref[t : t + 8], up_ref[t : t + 8]
+            return jnp.where(even_n, by_low, by_up) if dy < 0 else jnp.where(even_n, by_up, by_low)
+
         for dx, dy in DIRS:
-            t = 8 * tile_of(a, dx)
-            if dy == 0:
-                m = 8 * (2 * (a + 1) + (dx + 1) // 2)
-                table.append(mid_ref[m : m + 8])
-                continue
-            by_low, by_up = low_ref[t : t + 8], up_ref[t : t + 8]
-            if dy < 0:
-                table.append(jnp.where(even_n, by_low, by_up))
+            if dx == 0:
+                table.append(ghost_tile(0, dy))
             else:
-                table.append(jnp.where(even_n, by_up, by_low))
+                table.append(jnp.where(odd, ghost_tile(dx, dy), ghost_tile(-dx, dy)))
         table = jnp.concatenate(table, 0)
         neigh = raw[NEIGH : NEIGH + 8].astype(jnp.int32)
         ghost = neigh - 512
@@ -343,13 +373,13 @@
         center_high = center_ids >> 7
         at_neigh = gather(table, onehot_low(as_row(neigh_low)), neigh_high)
         at_center = gather(table[0:16], onehot_low(center_ids & 127), center_high)
-        if a == 0:
-            hot_t_ref[len(SPAN)] = onehot_t(centers.astype(jnp.int32) & 127)
+        if d == 0:
+            hot_t_ref[2] = onehot_t(centers.astype(jnp.int32) & 127)
         block = lax.broadcasted_iota(jnp.int32, (1, pair_len), 1) // 128
         mask = jnp.where(block.astype(F32) < raw[LIVE : LIVE + 1, 0:1], 1.0, 0.0)
         return at_neigh, at_center, mask, neigh_high, center_high
 
-    placed = [place(d) for d in range(len(SPAN))]
+    placed = [place(d) for d in range(count)]
     at_neigh, at_center, mask = (jnp.concatenate([p[i] for p in placed], 1) for i in range(3))
     width = mask.shape[1]
     moved = at_neigh - at_center
@@ -369,7 +399,7 @@
     hot_neigh = jnp.where(at_neigh[3:4] == kinds, 1.0, 0.0).astype(BF16)
     b1, b2, b3 = parts(sine * scale, 3)
     pre = dot_rows(front, jnp.concatenate([b1, b1, b2, b1, b2, b3, hot_center, hot_neigh], 0))
-    for d in range(len(SPAN)):
+    for d in range(count):
         build_same(d)
     latent, slope = silu_parts(pre)
     half = latent.astype(BF16)
@@ -407,9 +437,9 @@
             sums[order] = term if sums[order] is None else sums[order] + term
         return jnp.concatenate(sums, 0)
 
-    for d in range(len(SPAN)):
+    for d in range(count):
         spread_same(d, weight, gath_ref)
-    sums = jnp.concatenate([gathered_sums(d, gath_ref) for d in range(len(SPAN))], 1)
+    sums = jnp.concatenate([gathered_sums(d, gath_ref) for d in range(count)], 1)
     joined = jnp.concatenate([half, (weight * sums).astype(BF16)], 0)
     update, slope2 = silu_parts(dot_rows(w_lat, joined))
     refined = (latent + update).astype(BF16)
@@ -420,10 +450,10 @@
     d_inv = d_joined[lat:]
     d_weight = d_inv * sums
     d_sums = d_inv * weight
-    for d in range(len(SPAN)):
+    for d in range(count):
         spread_same(d, d_sums, back_ref)
     d_order, d_shape = [], []
-    for d in range(len(SPAN)):
+    for d in range(count):
         at = domain(d)
         d_order.append(gathered_sums(d, back_ref))
         here = []
@@ -470,38 +500,63 @@
     values = jnp.concatenate(rows4 + rows4, 0)
     rows = lax.broadcasted_iota(jnp.int32, (8, width), 0)
     flipped = jnp.where((rows & 3) == 3, values, -values)
-    for d, a in enumerate(SPAN):
-        neigh_high, center_high = placed[d][3:]
-        groups = [2 + DIRS.index((a, -1)), 2 + DIRS.index((a, 1))]
-        groups += [2 + DIRS.index((a, 0))] if a else [0, 1]
-        terms = scatter(flipped[:, domain(d)], hot_t_ref[d], neigh_high, groups)
-        minus, plus = terms[0:8], terms[8:16]
-        at = slice(8 * d, 8 * d + 8)
+    first = jnp.where(odd, 5, 0)
+
+    def groups_of(side):
+        return [2 + (first if side > 0 else 5 - first) + i for i in range(3)]
+
+    neigh_high, center_high = placed[0][3:]
+    groups = [0, 1, 2 + 3, 2 + 4] + groups_of(1) + (groups_of(-1) if count == 1 else [])
+    terms = scatter(flipped[:, domain(0)], hot_t_ref[0], neigh_high, groups)
+    center_terms = scatter(values[:, domain(0)], hot_t_ref[2], center_high, (0, 1))
+    local_ref[...] = terms[0:16] + center_terms
+    tiles = [terms[8 * i : 8 * i + 8] for i in range(2, len(groups))]
+    if count == 2:
+        terms = scatter(flipped[:, domain(1)], hot_t_ref[1], placed[1][3], groups_of(1))
+        tiles += [terms[8 * i : 8 * i + 8] for i in range(3)]
+    edge_near_ref[...] = tiles[3]
+    edge_far_ref[...] = tiles[6]
+    for j, (minus, plus) in enumerate(
+        ((tiles[0], tiles[1]), (tiles[2], tiles[4]), (tiles[5], tiles[7]))
+    ):
+        at = slice(8 * j, 8 * j + 8)
         back_far_ref[at] = jnp.where(even_n, plus, minus)
         back_near_ref[at] = jnp.where(even_n, minus, plus)
-        if a:
-            own_ref[8 * (d // 2) : 8 * (d // 2) + 8] = terms[16:24]
-        else:
-            center_terms = scatter(values[:, domain(d)], hot_t_ref[len(SPAN)], center_high, (0, 1))
-            local_ref[...] = terms[16:32] + center_terms
-
-
-def collect_kernel(local_ref, own_ref, raw_ref, up_ref, low_ref, forces_ref, energy_ref):
+
+
+def collect_kernel(
+    local_ref,
+    raw_ref,
+    up_ref,
+    low_ref,
+    edge_far_ref,
+    cross_ref,
+    beside_ref,
+    forces_ref,
+    energy_ref,
+):
     even_n = lax.axis_index("inner") % 2 == 0
+    odd = lax.axis_index("outer") % 2 == 1
+    place = lax.axis_index("outer") % 4
+    at_border = (place == 0) | (place == 3)
     plus = jnp.where(even_n, low_ref[...], up_ref[...])
     minus = jnp.where(even_n, up_ref[...], low_ref[...])
+    over = jnp.concatenate([minus[16:24], edge_far_ref[...], plus[16:24]], 0)
+    toward = jnp.where(at_border, over, cross_ref[...])
+    away = beside_ref[...]
+    above = jnp.where(odd, toward, away)
+    below = jnp.where(odd, away, toward)
     lists_low = raw_ref[LISTS : LISTS + 8].astype(jnp.int32)
     lists_high = raw_ref[LISTS + 8 : LISTS + 16].astype(jnp.int32)
     rows = lax.broadcasted_iota(jnp.int32, (8, LANES), 0)
     ids, values = [], []
     for k, (dx, dy) in enumerate(DIRS):
         ids += [lists_low[k : k + 1], lists_high[k : k + 1]]
-        if dy == 0:
-            at = 8 * ((dx + 1) // 2)
-            tile = own_ref[at : at + 8]
+        if dx == 0:
+            tile = (minus if dy < 0 else plus)[0:8]
         else:
-            at = 8 * (dx + 1)
-            tile = (minus if dy < 0 else plus)[at : at + 8]
+            at = 8 * (dy + 1)
+            tile = (above if dx > 0 else below)[at : at + 8]
         turned = pltpu.roll(tile, 4, 0)
         values += [jnp.where(rows < 4, tile, turned), jnp.where(rows < 4, turned, tile)]
     ids = jnp.concatenate(ids, 1)
@@ -593,38 +648,51 @@
             for value in (w_rad, emb_center, emb_neigh, w_env.T, w_lat, w_out.reshape(1, -1))
         )
     )
-    far2 = exchange(packed, "outer", 1, 2)
-    far1 = exchange(packed, "outer", 1)
-    near1 = exchange(packed, "outer", 0)
-    near2 = exchange(packed, "outer", 0, 2)
+    row_count = lax.axis_size("outer")
+    low_half = range(row_count // 2)
+    high_half = range(row_count // 2, row_count)
+    beside_low = swap_outer(packed, 0, low_half)
+    border = over_border(packed)
+    cross = swap_outer(packed, 1, range(row_count))
+    beside_high = swap_outer(packed, 0, high_half)
     far, near, mid, raw = pl.pallas_call(
         sends_kernel,
         out_shape=[
-            rows(72),
-            rows(72),
             rows(48),
-            jax.ShapeDtypeStruct((len(SPAN), PACKED, LANES), F32),
+            rows(48),
+            rows(32),
+            jax.ShapeDtypeStruct((2, PACKED, LANES), F32),
         ],
         compiler_params=SMALL,
         name="gather_sends",
-    )(packed, near2, near1, far1, far2, weights[3])
-    up = exchange(far, "inner", 1)
-    low = exchange(near, "inner", 0)
-    local, own, far, near = pl.pallas_call(
+    )(packed, beside_low, border, cross, beside_high, weights[3])
+    up = swap_inner(far, 1)
+    low = swap_inner(near, 0)
+    local, edge_near, edge_far, far, near = pl.pallas_call(
         lambda *refs: pair_kernel(feat, pair_len, *refs),
-        out_shape=[rows(16), rows(16), rows(24), rows(24)],
+        out_shape=[rows(16), rows(8), rows(8), rows(24), rows(24)],
         scratch_shapes=[
-            pltpu.VMEM((len(SPAN), pair_len, pair_len), BF16),
-            pltpu.VMEM((len(SPAN) + 1, pair_len, LANES), BF16),
-            pltpu.VMEM((len(SPAN), 9 * feat, pair_len), BF16),
-            pltpu.VMEM((len(SPAN), 9 * feat, pair_len), F32),
-            pltpu.VMEM((len(SPAN), 9 * feat, pair_len), F32),
+            pltpu.VMEM((2, pair_len, pair_len), BF16),
+            pltpu.VMEM((3, pair_len, LANES), BF16),
+            pltpu.VMEM((2, 9 * feat, pair_len), BF16),
+            pltpu.VMEM((2, 9 * feat, pair_len), F32),
+            pltpu.VMEM((2, 9 * feat, pair_len), F32),
         ],
         compiler_params=LARGE,
         name="pair_terms",
     )(raw, mid, up, low, *weights)
-    up = exchange(far, "inner", 1)
-    low = exchange(near, "inner", 0)
+    up = swap_inner(far, 1)
+    low = swap_inner(near, 0)
+    even_n = lax.axis_index("inner") % 2 == 0
+    plus = jnp.where(even_n, low, up)
+    minus = jnp.where(even_n, up, low)
+    inside = [o for o in range(row_count) if o % 4 in (1, 2)]
+    cross = swap_outer(
+        jnp.concatenate([minus[16:24], edge_far, plus[16:24]], 0), 1, inside
+    )
+    beside = swap_outer(
+        jnp.concatenate([minus[8:16], edge_near, plus[8:16]], 0), 0, range(row_count)
+    )
     forces, energy = pl.pallas_call(
         collect_kernel,
         out_shape=[
@@ -633,7 +701,7 @@
         ],
         compiler_params=SMALL,
         name="collect_terms",
-    )(local, own, packed, up, low)
+    )(local, packed, up, low, edge_far, cross, beside)
     return forces, energy.reshape(atom_count)
 
 

time: 57 us -> 56.2 us (0.986)
  the two profiles are of different devices: /device:TPU:1 before, /device:TPU:2 now
where the time goes in v5:
time: 56.2 us; the launch traced here: 55.8 us
  starting transfers between devices  40.3 us (72%)
  waiting for transfers between devices  7.18 us (13%)
  Pallas kernels  6.9 us (12%)
  between operations  1.43 us (3%)
    ppermute x10, starting transfers between devices, permute(): return lax.ppermute(block, AXES, route)  40.3 us
    ppermute x10, waiting for transfers between devices, permute(): return lax.ppermute(block, AXES, route)  7.18 us
    pallas_call x1, Pallas kernels, on_device(): pl.pallas_call(lambda *refs: pair_kernel(feat, pair_len, *refs), out_shap...  3.79 us
  transfers between devices with their start and end apart: 10, of which 6 were waited for; matrix products, arithmetic and copies ran while one was open for 0% of the time, Pallas kernels for 2%

profile of v5, /device:TPU:2, one launch (start us, length us, event | category | flops | bytes accessed | tf_op | source)
XLA Modules:
  0.0 55.8 jit_solution(8826598583956327405)
XLA Ops:
  1.3 0.8 %pack_domain.1.own_ref.raw_ref = f32[48,128]{1,0:T(8,128)S(1)} custom-call(f32[3,512]{1,0:T(4,128)} %pos_hbm.1, s32[1,512]{1,0:T(1,128)} %bitcast.9, s32[8,176]{1,0:T(8,128)} %lists_hbm.1, s32[6,128]{1,0:T(8,128)} %bitcast.7, s32[6,128]{1,0:T(8,128)} %bitcast.8, s32[1]{0:T(128)S(6)} %copy.14.live_ref), custom_call_target="tpu_custom_call" | custom-call | tf_op jit(solution)/shard_map/pack_domain/pallas_call | solution.py:598
  2.1 7.8 %collective-permute-start = (f32[48,128]{1,0:T(8,128)S(1)}, f32[48,128]{1,0:T(8,128)S(1)}, u32[]{:S(2)}, u32[]{:S(2)}) collective-permute-start(f32[48,128]{1,0:T(8,128)S(1)} %pack_domain.1.own_ref.raw_ref), channel_id=1, source_target_pairs={{0,64},{1,65},{2,66},{3,67},{4,68},{5,69},{6,70},{7,71},{8,72},{9,... | collective-permute-start | bytes 73736 | tf_op jit(solution)/shard_map/ppermute | solution.py:36
  9.9 5.3 %collective-permute-start.1 = (f32[48,128]{1,0:T(8,128)S(1)}, f32[48,128]{1,0:T(8,128)S(1)}, u32[]{:S(2)}, u32[]{:S(2)}) collective-permute-start(f32[48,128]{1,0:T(8,128)S(1)} %pack_domain.1.own_ref.raw_ref), channel_id=1, source_target_pairs={{64,448},{65,449},{66,450},{67,451},{68,452},{69,453},{70,454},{71... | collective-permute-start | bytes 73736 | tf_op jit(solution)/shard_map/ppermute | solution.py:36
  15.2 1.9 %collective-permute-start.2 = (f32[48,128]{1,0:T(8,128)S(1)}, f32[48,128]{1,0:T(8,128)S(1)}, u32[]{:S(2)}, u32[]{:S(2)}) collective-permute-start(f32[48,128]{1,0:T(8,128)S(1)} %pack_domain.1.own_ref.raw_ref), channel_id=1, source_target_pairs={{0,448},{1,449},{2,450},{3,451},{4,452},{5,453},{6,454},{7,455},{8... | collective-permute-start | bytes 73736 | tf_op jit(solution)/shard_map/ppermute | solution.py:36
  17.2 0.7 %collective-permute-start.3 = (f32[48,128]{1,0:T(8,128)S(1)}, f32[48,128]{1,0:T(8,128)S(1)}, u32[]{:S(2)}, u32[]{:S(2)}) collective-permute-start(f32[48,128]{1,0:T(8,128)S(1)} %pack_domain.1.own_ref.raw_ref), channel_id=1, source_target_pairs={{256,320},{257,321},{258,322},{259,323},{260,324},{261,325},{262,3... | collective-permute-start | bytes 73736 | tf_op jit(solution)/shard_map/ppermute | solution.py:36
  17.8 1.0 %place_weights.1 = (bf16[64,128]{1,0:T(8,128)(2,1)S(1)}, bf16[192,128]{1,0:T(8,128)(2,1)S(1)}, bf16[320,128]{1,0:T(8,128)(2,1)S(1)}, bf16[16,128]{1,0:T(8,128)(2,1)S(1)}) custom-call(f32[8,128]{1,0:T(8,128)} %w_rad_hbm.1, bf16[7,128]{1,0:T(8,128)(2,1)} %emb_center_hbm.1, bf16[7,128]{1,0:T(8,128)(2,1)} %emb_neigh_hbm.1, bf16[192,128]{1,0:T(8,128)(2,1)} %bitcast.6, ...), custom_call_target="tpu_custom_call" | custom-call | bytes 4000000 | tf_op jit(solution)/shard_map/place_weights/pallas_call | solution.py:626
  18.9 0.0 collective-permute-done.low_ref
  18.9 0.0 collective-permute-done.1.border_ref
  18.9 2.1 %collective-permute-done.2.cross_ref = f32[48,128]{1,0:T(8,128)S(1)} collective-permute-done((f32[48,128]{1,0:T(8,128)S(1)}, f32[48,128]{1,0:T(8,128)S(1)}, u32[]{:S(2)}, u32[]{:S(2)}) %collective-permute-start.2) | collective-permute-done | bytes 24608 | tf_op jit(solution)/shard_map/ppermute | solution.py:36
  21.0 0.0 collective-permute-done.3.high_ref
  21.0 0.3 gather_sends.1
  21.3 6.1 %collective-permute-start.4 = (f32[48,128]{1,0:T(8,128)S(1)}, f32[48,128]{1,0:T(8,128)S(1)}, u32[]{:S(2)}, u32[]{:S(2)}) collective-permute-start(f32[48,128]{1,0:T(8,128)S(1)} %get-tuple-element.20), channel_id=1, source_target_pairs={{0,63},{1,2},{2,1},{3,4},{4,3},{5,6},{6,5},{7,8},{8,7},{9,10},{10,... | collective-permute-start | bytes 73736 | tf_op jit(solution)/shard_map/ppermute | solution.py:36
  27.4 1.9 %collective-permute-start.5 = (f32[48,128]{1,0:T(8,128)S(1)}, f32[48,128]{1,0:T(8,128)S(1)}, u32[]{:S(2)}, u32[]{:S(2)}) collective-permute-start(f32[48,128]{1,0:T(8,128)S(1)} %get-tuple-element.21), channel_id=1, source_target_pairs={{0,1},{1,0},{2,3},{3,2},{4,5},{5,4},{6,7},{7,6},{8,9},{9,8},{10,11... | collective-permute-start | bytes 73736 | tf_op jit(solution)/shard_map/ppermute | solution.py:36
  29.3 1.0 %collective-permute-done.4.refs_2_ = f32[48,128]{1,0:T(8,128)S(1)} collective-permute-done((f32[48,128]{1,0:T(8,128)S(1)}, f32[48,128]{1,0:T(8,128)S(1)}, u32[]{:S(2)}, u32[]{:S(2)}) %collective-permute-start.4) | collective-permute-done | bytes 24608 | tf_op jit(solution)/shard_map/ppermute | solution.py:36
  30.3 0.2 collective-permute-done.5.refs_3_
  30.5 3.8 %pair_terms.1 = (f32[16,128]{1,0:T(8,128)S(1)}, f32[8,128]{1,0:T(8,128)S(1)}, f32[8,128]{1,0:T(8,128)S(1)}, f32[24,128]{1,0:T(8,128)S(1)}, f32[24,128]{1,0:T(8,128)S(1)}) custom-call(f32[2,48,128]{2,1,0:T(8,128)S(1)} %get-tuple-element.18.refs_0_, f32[32,128]{1,0:T(8,128)S(1)} %get-tuple-element.19.refs_1_, f32[48,128]{1,0:T(8,128)S(1)} %collective-permute-done.4.refs_2_, ...), custom_call_target="tpu_custom_call" | custom-call | tf_op jit(solution)/shard_map/pair_terms/pallas_call | solution.py:671
  34.3 6.0 %collective-permute-start.6 = (f32[24,128]{1,0:T(8,128)S(1)}, f32[24,128]{1,0:T(8,128)S(1)}, u32[]{:S(2)}, u32[]{:S(2)}) collective-permute-start(f32[24,128]{1,0:T(8,128)S(1)} %get-tuple-element.26), channel_id=1, source_target_pairs={{0,63},{1,2},{2,1},{3,4},{4,3},{5,6},{6,5},{7,8},{8,7},{9,10},{10,... | collective-permute-start | bytes 36872 | tf_op jit(solution)/shard_map/ppermute | solution.py:36
  40.2 1.9 %collective-permute-start.7 = (f32[24,128]{1,0:T(8,128)S(1)}, f32[24,128]{1,0:T(8,128)S(1)}, u32[]{:S(2)}, u32[]{:S(2)}) collective-permute-start(f32[24,128]{1,0:T(8,128)S(1)} %get-tuple-element.27), channel_id=1, source_target_pairs={{0,1},{1,0},{2,3},{3,2},{4,5},{5,4},{6,7},{7,6},{8,9},{9,8},{10,11... | collective-permute-start | bytes 36872 | tf_op jit(solution)/shard_map/ppermute | solution.py:36
  42.2 1.0 %collective-permute-done.6.up_ref = f32[24,128]{1,0:T(8,128)S(1)} collective-permute-done((f32[24,128]{1,0:T(8,128)S(1)}, f32[24,128]{1,0:T(8,128)S(1)}, u32[]{:S(2)}, u32[]{:S(2)}) %collective-permute-start.6) | collective-permute-done | bytes 12320 | tf_op jit(solution)/shard_map/ppermute | solution.py:36
  43.2 0.1 collective-permute-done.7.low_ref
  43.3 5.9 %collective-permute-start.9 = (f32[24,128]{1,0:T(8,128)S(1)}, f32[24,128]{1,0:T(8,128)S(1)}, u32[]{:S(2)}, u32[]{:S(2)}) collective-permute-start(f32[24,128]{1,0:T(8,128)S(1)} %pad_maximum_fusion.1), channel_id=1, source_target_pairs={{0,64},{1,65},{2,66},{3,67},{4,68},{5,69},{6,70},{7,71},{8,72},{9,... | collective-permute-start | bytes 36872 | tf_op jit(solution)/shard_map/ppermute | solution.py:36
  49.2 2.7 %collective-permute-start.8 = (f32[24,128]{1,0:T(8,128)S(1)}, f32[24,128]{1,0:T(8,128)S(1)}, u32[]{:S(2)}, u32[]{:S(2)}) collective-permute-start(f32[24,128]{1,0:T(8,128)S(1)} %pad_maximum_fusion), channel_id=1, source_target_pairs={{64,128},{65,129},{66,130},{67,131},{68,132},{69,133},{70,134},{71... | collective-permute-start | bytes 36872 | tf_op jit(solution)/shard_map/ppermute | solution.py:36
  52.0 0.0 collective-permute-done.9.beside_ref
  52.0 2.8 %collective-permute-done.8.cross_ref = f32[24,128]{1,0:T(8,128)S(1)} collective-permute-done((f32[24,128]{1,0:T(8,128)S(1)}, f32[24,128]{1,0:T(8,128)S(1)}, u32[]{:S(2)}, u32[]{:S(2)}) %collective-permute-start.8) | collective-permute-done | bytes 12320 | tf_op jit(solution)/shard_map/ppermute | solution.py:36
  54.8 1.0 %collect_terms.1 = (f32[3,512]{1,0:T(4,128)}, f32[1,512]{1,0:T(1,128)}) custom-call(f32[16,128]{1,0:T(8,128)S(1)} %get-tuple-element.25.local_ref, f32[48,128]{1,0:T(8,128)S(1)} %pack_domain.1.own_ref.raw_ref, f32[24,128]{1,0:T(8,128)S(1)} %collective-permute-done.6.up_ref, f32[24,128]{1,0:T(8,128)S(1)} %collective-permute-done.7.low_ref, ...), custom_call_target="tpu_custom_call" | custom-call | tf_op jit(solution)/shard_map/collect_terms/pallas_call | solution.py:696
  (4 shorter events, 0.0 us)
Async XLA Ops:
  2.1 16.8 %collective-permute-start = (f32[48,128]{1,0:T(8,128)S(1)}, f32[48,128]{1,0:T(8,128)S(1)}, u32[]{:S(2)}, u32[]{:S(2)}) collective-permute-start(f32[48,128]{1,0:T(8,128)S(1)} %pack_domain.1.own_ref.raw_ref), channel_id=1, source_target_pairs={{0,64},{1,65},{2,66},{3,67},{4,68},{5,69},{6,70},{7,71},{8,72},{9,... | collective-permute-start | bytes 73736 | tf_op jit(solution)/shard_map/ppermute | solution.py:36
  9.9 9.0 %collective-permute-start.1 = (f32[48,128]{1,0:T(8,128)S(1)}, f32[48,128]{1,0:T(8,128)S(1)}, u32[]{:S(2)}, u32[]{:S(2)}) collective-permute-start(f32[48,128]{1,0:T(8,128)S(1)} %pack_domain.1.own_ref.raw_ref), channel_id=1, source_target_pairs={{64,448},{65,449},{66,450},{67,451},{68,452},{69,453},{70,454},{71... | collective-permute-start | bytes 73736 | tf_op jit(solution)/shard_map/ppermute | solution.py:36
  15.2 5.7 %collective-permute-start.2 = (f32[48,128]{1,0:T(8,128)S(1)}, f32[48,128]{1,0:T(8,128)S(1)}, u32[]{:S(2)}, u32[]{:S(2)}) collective-permute-start(f32[48,128]{1,0:T(8,128)S(1)} %pack_domain.1.own_ref.raw_ref), channel_id=1, source_target_pairs={{0,448},{1,449},{2,450},{3,451},{4,452},{5,453},{6,454},{7,455},{8... | collective-permute-start | bytes 73736 | tf_op jit(solution)/shard_map/ppermute | solution.py:36
  17.2 3.8 %collective-permute-start.3 = (f32[48,128]{1,0:T(8,128)S(1)}, f32[48,128]{1,0:T(8,128)S(1)}, u32[]{:S(2)}, u32[]{:S(2)}) collective-permute-start(f32[48,128]{1,0:T(8,128)S(1)} %pack_domain.1.own_ref.raw_ref), channel_id=1, source_target_pairs={{256,320},{257,321},{258,322},{259,323},{260,324},{261,325},{262,3... | collective-permute-start | bytes 73736 | tf_op jit(solution)/shard_map/ppermute | solution.py:36
  21.3 9.1 %collective-permute-start.4 = (f32[48,128]{1,0:T(8,128)S(1)}, f32[48,128]{1,0:T(8,128)S(1)}, u32[]{:S(2)}, u32[]{:S(2)}) collective-permute-start(f32[48,128]{1,0:T(8,128)S(1)} %get-tuple-element.20), channel_id=1, source_target_pairs={{0,63},{1,2},{2,1},{3,4},{4,3},{5,6},{6,5},{7,8},{8,7},{9,10},{10,... | collective-permute-start | bytes 73736 | tf_op jit(solution)/shard_map/ppermute | solution.py:36
  27.4 3.1 %collective-permute-start.5 = (f32[48,128]{1,0:T(8,128)S(1)}, f32[48,128]{1,0:T(8,128)S(1)}, u32[]{:S(2)}, u32[]{:S(2)}) collective-permute-start(f32[48,128]{1,0:T(8,128)S(1)} %get-tuple-element.21), channel_id=1, source_target_pairs={{0,1},{1,0},{2,3},{3,2},{4,5},{5,4},{6,7},{7,6},{8,9},{9,8},{10,11... | collective-permute-start | bytes 73736 | tf_op jit(solution)/shard_map/ppermute | solution.py:36
  34.3 8.9 %collective-permute-start.6 = (f32[24,128]{1,0:T(8,128)S(1)}, f32[24,128]{1,0:T(8,128)S(1)}, u32[]{:S(2)}, u32[]{:S(2)}) collective-permute-start(f32[24,128]{1,0:T(8,128)S(1)} %get-tuple-element.26), channel_id=1, source_target_pairs={{0,63},{1,2},{2,1},{3,4},{4,3},{5,6},{6,5},{7,8},{8,7},{9,10},{10,... | collective-permute-start | bytes 36872 | tf_op jit(solution)/shard_map/ppermute | solution.py:36
  40.2 3.1 %collective-permute-start.7 = (f32[24,128]{1,0:T(8,128)S(1)}, f32[24,128]{1,0:T(8,128)S(1)}, u32[]{:S(2)}, u32[]{:S(2)}) collective-permute-start(f32[24,128]{1,0:T(8,128)S(1)} %get-tuple-element.27), channel_id=1, source_target_pairs={{0,1},{1,0},{2,3},{3,2},{4,5},{5,4},{6,7},{7,6},{8,9},{9,8},{10,11... | collective-permute-start | bytes 36872 | tf_op jit(solution)/shard_map/ppermute | solution.py:36
  43.3 8.7 %collective-permute-start.9 = (f32[24,128]{1,0:T(8,128)S(1)}, f32[24,128]{1,0:T(8,128)S(1)}, u32[]{:S(2)}, u32[]{:S(2)}) collective-permute-start(f32[24,128]{1,0:T(8,128)S(1)} %pad_maximum_fusion.1), channel_id=1, source_target_pairs={{0,64},{1,65},{2,66},{3,67},{4,68},{5,69},{6,70},{7,71},{8,72},{9,... | collective-permute-start | bytes 36872 | tf_op jit(solution)/shard_map/ppermute | solution.py:36
  49.2 5.6 %collective-permute-start.8 = (f32[24,128]{1,0:T(8,128)S(1)}, f32[24,128]{1,0:T(8,128)S(1)}, u32[]{:S(2)}, u32[]{:S(2)}) collective-permute-start(f32[24,128]{1,0:T(8,128)S(1)} %pad_maximum_fusion), channel_id=1, source_target_pairs={{64,128},{65,129},{66,130},{67,131},{68,132},{69,133},{70,134},{71... | collective-permute-start | bytes 36872 | tf_op jit(solution)/shard_map/ppermute | solution.py:36

commit v6 on v5

--- a/solution.py
+++ b/solution.py
@@ -530,8 +530,8 @@
     up_ref,
     low_ref,
     edge_far_ref,
+    beside_ref,
     cross_ref,
-    beside_ref,
     forces_ref,
     energy_ref,
 ):
@@ -701,7 +701,7 @@
         ],
         compiler_params=SMALL,
         name="collect_terms",
-    )(local, packed, up, low, edge_far, cross, beside)
+    )(local, packed, up, low, edge_far, beside, cross)
     return forces, energy.reshape(atom_count)
 
 

time: 56.2 us -> 53.5 us (0.952)
  the two profiles are of different devices: /device:TPU:2 before, /device:TPU:1 now
where the time goes in v6:
time: 53.5 us; the launch traced here: 53.1 us
  starting transfers between devices  38.9 us (73%)
  Pallas kernels  9.14 us (17%)
  waiting for transfers between devices  3.6 us (7%)
  between operations  1.46 us (3%)
    ppermute x10, starting transfers between devices, permute(): return lax.ppermute(block, AXES, route)  38.9 us
    pallas_call x1, Pallas kernels, on_device(): pl.pallas_call(lambda *refs: pair_kernel(feat, pair_len, *refs), out_shap...  6.02 us
    ppermute x10, waiting for transfers between devices, permute(): return lax.ppermute(block, AXES, route)  3.6 us
  transfers between devices with their start and end apart: 10, of which 3 were waited for; matrix products, arithmetic and copies ran while one was open for 0% of the time, Pallas kernels for 2%

profile of v6, /device:TPU:1, one launch (start us, length us, event | category | flops | bytes accessed | tf_op | source)
XLA Modules:
  0.0 53.1 jit_solution(9633778870962672039)
XLA Ops:
  1.3 0.8 %pack_domain.1.own_ref.raw_ref = f32[48,128]{1,0:T(8,128)S(1)} custom-call(f32[3,512]{1,0:T(4,128)} %pos_hbm.1, s32[1,512]{1,0:T(1,128)} %bitcast.9, s32[8,176]{1,0:T(8,128)} %lists_hbm.1, s32[6,128]{1,0:T(8,128)} %bitcast.7, s32[6,128]{1,0:T(8,128)} %bitcast.8, s32[1]{0:T(128)S(6)} %copy.14.live_ref), custom_call_target="tpu_custom_call" | custom-call | tf_op jit(solution)/shard_map/pack_domain/pallas_call | solution.py:598
  2.1 3.9 %collective-permute-start = (f32[48,128]{1,0:T(8,128)S(1)}, f32[48,128]{1,0:T(8,128)S(1)}, u32[]{:S(2)}, u32[]{:S(2)}) collective-permute-start(f32[48,128]{1,0:T(8,128)S(1)} %pack_domain.1.own_ref.raw_ref), channel_id=1, source_target_pairs={{0,64},{1,65},{2,66},{3,67},{4,68},{5,69},{6,70},{7,71},{8,72},{9,... | collective-permute-start | bytes 73736 | tf_op jit(solution)/shard_map/ppermute | solution.py:36
  6.0 1.3 %collective-permute-start.1 = (f32[48,128]{1,0:T(8,128)S(1)}, f32[48,128]{1,0:T(8,128)S(1)}, u32[]{:S(2)}, u32[]{:S(2)}) collective-permute-start(f32[48,128]{1,0:T(8,128)S(1)} %pack_domain.1.own_ref.raw_ref), channel_id=1, source_target_pairs={{64,448},{65,449},{66,450},{67,451},{68,452},{69,453},{70,454},{71... | collective-permute-start | bytes 73736 | tf_op jit(solution)/shard_map/ppermute | solution.py:36
  7.3 10.4 %collective-permute-start.2 = (f32[48,128]{1,0:T(8,128)S(1)}, f32[48,128]{1,0:T(8,128)S(1)}, u32[]{:S(2)}, u32[]{:S(2)}) collective-permute-start(f32[48,128]{1,0:T(8,128)S(1)} %pack_domain.1.own_ref.raw_ref), channel_id=1, source_target_pairs={{0,448},{1,449},{2,450},{3,451},{4,452},{5,453},{6,454},{7,455},{8... | collective-permute-start | bytes 73736 | tf_op jit(solution)/shard_map/ppermute | solution.py:36
  17.7 0.7 %collective-permute-start.3 = (f32[48,128]{1,0:T(8,128)S(1)}, f32[48,128]{1,0:T(8,128)S(1)}, u32[]{:S(2)}, u32[]{:S(2)}) collective-permute-start(f32[48,128]{1,0:T(8,128)S(1)} %pack_domain.1.own_ref.raw_ref), channel_id=1, source_target_pairs={{256,320},{257,321},{258,322},{259,323},{260,324},{261,325},{262,3... | collective-permute-start | bytes 73736 | tf_op jit(solution)/shard_map/ppermute | solution.py:36
  18.4 1.0 %place_weights.1 = (bf16[64,128]{1,0:T(8,128)(2,1)S(1)}, bf16[192,128]{1,0:T(8,128)(2,1)S(1)}, bf16[320,128]{1,0:T(8,128)(2,1)S(1)}, bf16[16,128]{1,0:T(8,128)(2,1)S(1)}) custom-call(f32[8,128]{1,0:T(8,128)} %w_rad_hbm.1, bf16[7,128]{1,0:T(8,128)(2,1)} %emb_center_hbm.1, bf16[7,128]{1,0:T(8,128)(2,1)} %emb_neigh_hbm.1, bf16[192,128]{1,0:T(8,128)(2,1)} %bitcast.6, ...), custom_call_target="tpu_custom_call" | custom-call | bytes 4000000 | tf_op jit(solution)/shard_map/place_weights/pallas_call | solution.py:626
  19.4 0.0 collective-permute-done.low_ref
  19.5 0.0 collective-permute-done.1.border_ref
  19.5 0.0 collective-permute-done.2.cross_ref
  19.5 0.0 collective-permute-done.3.high_ref
  19.5 0.3 gather_sends.1
  19.8 4.4 %collective-permute-start.4 = (f32[48,128]{1,0:T(8,128)S(1)}, f32[48,128]{1,0:T(8,128)S(1)}, u32[]{:S(2)}, u32[]{:S(2)}) collective-permute-start(f32[48,128]{1,0:T(8,128)S(1)} %get-tuple-element.20), channel_id=1, source_target_pairs={{0,63},{1,2},{2,1},{3,4},{4,3},{5,6},{6,5},{7,8},{8,7},{9,10},{10,... | collective-permute-start | bytes 73736 | tf_op jit(solution)/shard_map/ppermute | solution.py:36
  24.2 6.8 %collective-permute-start.5 = (f32[48,128]{1,0:T(8,128)S(1)}, f32[48,128]{1,0:T(8,128)S(1)}, u32[]{:S(2)}, u32[]{:S(2)}) collective-permute-start(f32[48,128]{1,0:T(8,128)S(1)} %get-tuple-element.21), channel_id=1, source_target_pairs={{0,1},{1,0},{2,3},{3,2},{4,5},{5,4},{6,7},{7,6},{8,9},{9,8},{10,11... | collective-permute-start | bytes 73736 | tf_op jit(solution)/shard_map/ppermute | solution.py:36
  31.1 0.0 collective-permute-done.4.refs_2_
  31.1 0.8 %collective-permute-done.5.refs_3_ = f32[48,128]{1,0:T(8,128)S(1)} collective-permute-done((f32[48,128]{1,0:T(8,128)S(1)}, f32[48,128]{1,0:T(8,128)S(1)}, u32[]{:S(2)}, u32[]{:S(2)}) %collective-permute-start.5) | collective-permute-done | bytes 24608 | tf_op jit(solution)/shard_map/ppermute | solution.py:36
  31.9 6.0 %pair_terms.1 = (f32[16,128]{1,0:T(8,128)S(1)}, f32[8,128]{1,0:T(8,128)S(1)}, f32[8,128]{1,0:T(8,128)S(1)}, f32[24,128]{1,0:T(8,128)S(1)}, f32[24,128]{1,0:T(8,128)S(1)}) custom-call(f32[2,48,128]{2,1,0:T(8,128)S(1)} %get-tuple-element.18.refs_0_, f32[32,128]{1,0:T(8,128)S(1)} %get-tuple-element.19.refs_1_, f32[48,128]{1,0:T(8,128)S(1)} %collective-permute-done.4.refs_2_, ...), custom_call_target="tpu_custom_call" | custom-call | tf_op jit(solution)/shard_map/pair_terms/pallas_call | solution.py:671
  37.9 1.9 %collective-permute-start.6 = (f32[24,128]{1,0:T(8,128)S(1)}, f32[24,128]{1,0:T(8,128)S(1)}, u32[]{:S(2)}, u32[]{:S(2)}) collective-permute-start(f32[24,128]{1,0:T(8,128)S(1)} %get-tuple-element.26), channel_id=1, source_target_pairs={{0,63},{1,2},{2,1},{3,4},{4,3},{5,6},{6,5},{7,8},{8,7},{9,10},{10,... | collective-permute-start | bytes 36872 | tf_op jit(solution)/shard_map/ppermute | solution.py:36
  39.9 6.3 %collective-permute-start.7 = (f32[24,128]{1,0:T(8,128)S(1)}, f32[24,128]{1,0:T(8,128)S(1)}, u32[]{:S(2)}, u32[]{:S(2)}) collective-permute-start(f32[24,128]{1,0:T(8,128)S(1)} %get-tuple-element.27), channel_id=1, source_target_pairs={{0,1},{1,0},{2,3},{3,2},{4,5},{5,4},{6,7},{7,6},{8,9},{9,8},{10,11... | collective-permute-start | bytes 36872 | tf_op jit(solution)/shard_map/ppermute | solution.py:36
  46.2 0.0 collective-permute-done.6.up_ref
  46.2 0.8 %collective-permute-done.7.low_ref = f32[24,128]{1,0:T(8,128)S(1)} collective-permute-done((f32[24,128]{1,0:T(8,128)S(1)}, f32[24,128]{1,0:T(8,128)S(1)}, u32[]{:S(2)}, u32[]{:S(2)}) %collective-permute-start.7) | collective-permute-done | bytes 12320 | tf_op jit(solution)/shard_map/ppermute | solution.py:36
  47.0 0.7 %collective-permute-start.9 = (f32[24,128]{1,0:T(8,128)S(1)}, f32[24,128]{1,0:T(8,128)S(1)}, u32[]{:S(2)}, u32[]{:S(2)}) collective-permute-start(f32[24,128]{1,0:T(8,128)S(1)} %pad_maximum_fusion.1), channel_id=1, source_target_pairs={{64,128},{65,129},{66,130},{67,131},{68,132},{69,133},{70,134},{71... | collective-permute-start | bytes 36872 | tf_op jit(solution)/shard_map/ppermute | solution.py:36
  47.7 2.4 %collective-permute-start.8 = (f32[24,128]{1,0:T(8,128)S(1)}, f32[24,128]{1,0:T(8,128)S(1)}, u32[]{:S(2)}, u32[]{:S(2)}) collective-permute-start(f32[24,128]{1,0:T(8,128)S(1)} %pad_maximum_fusion), channel_id=1, source_target_pairs={{0,64},{1,65},{2,66},{3,67},{4,68},{5,69},{6,70},{7,71},{8,72},{9,... | collective-permute-start | bytes 36872 | tf_op jit(solution)/shard_map/ppermute | solution.py:36
  50.1 0.0 collective-permute-done.9.cross_ref
  50.1 2.0 %collective-permute-done.8.beside_ref = f32[24,128]{1,0:T(8,128)S(1)} collective-permute-done((f32[24,128]{1,0:T(8,128)S(1)}, f32[24,128]{1,0:T(8,128)S(1)}, u32[]{:S(2)}, u32[]{:S(2)}) %collective-permute-start.8) | collective-permute-done | bytes 12320 | tf_op jit(solution)/shard_map/ppermute | solution.py:36
  52.1 1.0 %collect_terms.1 = (f32[3,512]{1,0:T(4,128)}, f32[1,512]{1,0:T(1,128)}) custom-call(f32[16,128]{1,0:T(8,128)S(1)} %get-tuple-element.25.local_ref, f32[48,128]{1,0:T(8,128)S(1)} %pack_domain.1.own_ref.raw_ref, f32[24,128]{1,0:T(8,128)S(1)} %collective-permute-done.6.up_ref, f32[24,128]{1,0:T(8,128)S(1)} %collective-permute-done.7.low_ref, ...), custom_call_target="tpu_custom_call" | custom-call | tf_op jit(solution)/shard_map/collect_terms/pallas_call | solution.py:696
  (4 shorter events, 0.0 us)
Async XLA Ops:
  2.1 17.4 %collective-permute-start = (f32[48,128]{1,0:T(8,128)S(1)}, f32[48,128]{1,0:T(8,128)S(1)}, u32[]{:S(2)}, u32[]{:S(2)}) collective-permute-start(f32[48,128]{1,0:T(8,128)S(1)} %pack_domain.1.own_ref.raw_ref), channel_id=1, source_target_pairs={{0,64},{1,65},{2,66},{3,67},{4,68},{5,69},{6,70},{7,71},{8,72},{9,... | collective-permute-start | bytes 73736 | tf_op jit(solution)/shard_map/ppermute | solution.py:36
  6.0 13.4 %collective-permute-start.1 = (f32[48,128]{1,0:T(8,128)S(1)}, f32[48,128]{1,0:T(8,128)S(1)}, u32[]{:S(2)}, u32[]{:S(2)}) collective-permute-start(f32[48,128]{1,0:T(8,128)S(1)} %pack_domain.1.own_ref.raw_ref), channel_id=1, source_target_pairs={{64,448},{65,449},{66,450},{67,451},{68,452},{69,453},{70,454},{71... | collective-permute-start | bytes 73736 | tf_op jit(solution)/shard_map/ppermute | solution.py:36
  7.3 12.1 %collective-permute-start.2 = (f32[48,128]{1,0:T(8,128)S(1)}, f32[48,128]{1,0:T(8,128)S(1)}, u32[]{:S(2)}, u32[]{:S(2)}) collective-permute-start(f32[48,128]{1,0:T(8,128)S(1)} %pack_domain.1.own_ref.raw_ref), channel_id=1, source_target_pairs={{0,448},{1,449},{2,450},{3,451},{4,452},{5,453},{6,454},{7,455},{8... | collective-permute-start | bytes 73736 | tf_op jit(solution)/shard_map/ppermute | solution.py:36
  17.7 1.8 %collective-permute-start.3 = (f32[48,128]{1,0:T(8,128)S(1)}, f32[48,128]{1,0:T(8,128)S(1)}, u32[]{:S(2)}, u32[]{:S(2)}) collective-permute-start(f32[48,128]{1,0:T(8,128)S(1)} %pack_domain.1.own_ref.raw_ref), channel_id=1, source_target_pairs={{256,320},{257,321},{258,322},{259,323},{260,324},{261,325},{262,3... | collective-permute-start | bytes 73736 | tf_op jit(solution)/shard_map/ppermute | solution.py:36
  19.8 11.3 %collective-permute-start.4 = (f32[48,128]{1,0:T(8,128)S(1)}, f32[48,128]{1,0:T(8,128)S(1)}, u32[]{:S(2)}, u32[]{:S(2)}) collective-permute-start(f32[48,128]{1,0:T(8,128)S(1)} %get-tuple-element.20), channel_id=1, source_target_pairs={{0,63},{1,2},{2,1},{3,4},{4,3},{5,6},{6,5},{7,8},{8,7},{9,10},{10,... | collective-permute-start | bytes 73736 | tf_op jit(solution)/shard_map/ppermute | solution.py:36
  24.2 7.7 %collective-permute-start.5 = (f32[48,128]{1,0:T(8,128)S(1)}, f32[48,128]{1,0:T(8,128)S(1)}, u32[]{:S(2)}, u32[]{:S(2)}) collective-permute-start(f32[48,128]{1,0:T(8,128)S(1)} %get-tuple-element.21), channel_id=1, source_target_pairs={{0,1},{1,0},{2,3},{3,2},{4,5},{5,4},{6,7},{7,6},{8,9},{9,8},{10,11... | collective-permute-start | bytes 73736 | tf_op jit(solution)/shard_map/ppermute | solution.py:36
  37.9 8.2 %collective-permute-start.6 = (f32[24,128]{1,0:T(8,128)S(1)}, f32[24,128]{1,0:T(8,128)S(1)}, u32[]{:S(2)}, u32[]{:S(2)}) collective-permute-start(f32[24,128]{1,0:T(8,128)S(1)} %get-tuple-element.26), channel_id=1, source_target_pairs={{0,63},{1,2},{2,1},{3,4},{4,3},{5,6},{6,5},{7,8},{8,7},{9,10},{10,... | collective-permute-start | bytes 36872 | tf_op jit(solution)/shard_map/ppermute | solution.py:36
  39.9 7.1 %collective-permute-start.7 = (f32[24,128]{1,0:T(8,128)S(1)}, f32[24,128]{1,0:T(8,128)S(1)}, u32[]{:S(2)}, u32[]{:S(2)}) collective-permute-start(f32[24,128]{1,0:T(8,128)S(1)} %get-tuple-element.27), channel_id=1, source_target_pairs={{0,1},{1,0},{2,3},{3,2},{4,5},{5,4},{6,7},{7,6},{8,9},{9,8},{10,11... | collective-permute-start | bytes 36872 | tf_op jit(solution)/shard_map/ppermute | solution.py:36
  47.0 3.1 %collective-permute-start.9 = (f32[24,128]{1,0:T(8,128)S(1)}, f32[24,128]{1,0:T(8,128)S(1)}, u32[]{:S(2)}, u32[]{:S(2)}) collective-permute-start(f32[24,128]{1,0:T(8,128)S(1)} %pad_maximum_fusion.1), channel_id=1, source_target_pairs={{64,128},{65,129},{66,130},{67,131},{68,132},{69,133},{70,134},{71... | collective-permute-start | bytes 36872 | tf_op jit(solution)/shard_map/ppermute | solution.py:36
  47.7 4.4 %collective-permute-start.8 = (f32[24,128]{1,0:T(8,128)S(1)}, f32[24,128]{1,0:T(8,128)S(1)}, u32[]{:S(2)}, u32[]{:S(2)}) collective-permute-start(f32[24,128]{1,0:T(8,128)S(1)} %pad_maximum_fusion), channel_id=1, source_target_pairs={{0,64},{1,65},{2,66},{3,67},{4,68},{5,69},{6,70},{7,71},{8,72},{9,... | collective-permute-start | bytes 36872 | tf_op jit(solution)/shard_map/ppermute | solution.py:36

commit v7 on v6

--- a/solution.py
+++ b/solution.py
@@ -47,11 +47,15 @@
     return permute(block, place)
 
 
-def over_border(block):
-    def place(o, n):
-        return {1: (o - 2, n), 2: (o + 2, n)}.get(o % 4)
-
-    return permute(block, place)
+def copy_rows(block, rows):
+    return permute(block, lambda o, n: (rows[o], n) if o in rows else None)
+
+
+def row_kind():
+    half = lax.axis_size("outer") // 2
+    row = lax.axis_index("outer")
+    place = lax.rem(row, half)
+    return row < half, (place == 0) | (place == half - 1)
 
 
 def dot(lhs, rhs):
@@ -203,14 +207,15 @@
 
 
 def sends_kernel(
-    own_ref, low_ref, border_ref, cross_ref, high_ref, _, far_ref, near_ref, mid_ref, raw_ref
+    own_ref, high_ref, cross_ref, second_ref, first_ref, _, far_ref, near_ref, mid_ref, raw_ref
 ):
     even_n = lax.axis_index("inner") % 2 == 0
-    outer = lax.axis_index("outer")
-    odd = outer % 2 == 1
+    odd = lax.axis_index("outer") % 2 == 1
+    low_half, at_border = row_kind()
     rows = lax.broadcasted_iota(jnp.int32, (8, LANES), 0)
     own, cross = own_ref[...], cross_ref[...]
-    beside = jnp.where(outer < lax.axis_size("outer") // 2, low_ref[...], high_ref[...])
+    beside = jnp.where(at_border, second_ref[...], first_ref[...])
+    beside = jnp.where(low_half, beside, high_ref[...])
     raw_ref[0] = own
     raw_ref[1] = cross
 
@@ -240,7 +245,7 @@
     by_own = tiles_of(own, (1, 0))
     by_cross = tiles_of(cross, (0, -1))
     by_beside = tiles_of(beside, (1,))
-    by_border = tiles_of(border_ref[...], (-1,))
+    by_border = tiles_of(first_ref[...], (-1,))
     sources = ({1: by_beside, 0: by_own, -1: by_cross}, {1: by_own, 0: by_cross, -1: by_border})
     for extra in range(2):
         for side in (1, 0, -1):
@@ -274,10 +279,10 @@
 
 
 def pair_kernel(feat, pair_len, *refs):
-    place = lax.axis_index("outer") % 4
-    at_border = (place == 0) | (place == 3)
-    pl.when(at_border)(lambda: pair_body(2, feat, pair_len, *refs))
-    pl.when(jnp.logical_not(at_border))(lambda: pair_body(1, feat, pair_len, *refs))
+    low_half, at_border = row_kind()
+    two = low_half & at_border
+    pl.when(two)(lambda: pair_body(2, feat, pair_len, *refs))
+    pl.when(jnp.logical_not(two))(lambda: pair_body(1, feat, pair_len, *refs))
 
 
 def pair_body(
@@ -295,6 +300,7 @@
     local_ref,
     edge_near_ref,
     edge_far_ref,
+    edge_over_ref,
     back_far_ref,
     back_near_ref,
     same_ref,
@@ -506,7 +512,7 @@
         return [2 + (first if side > 0 else 5 - first) + i for i in range(3)]
 
     neigh_high, center_high = placed[0][3:]
-    groups = [0, 1, 2 + 3, 2 + 4] + groups_of(1) + (groups_of(-1) if count == 1 else [])
+    groups = [0, 1, 2 + 3, 2 + 4] + groups_of(1) + groups_of(-1)
     terms = scatter(flipped[:, domain(0)], hot_t_ref[0], neigh_high, groups)
     center_terms = scatter(values[:, domain(0)], hot_t_ref[2], center_high, (0, 1))
     local_ref[...] = terms[0:16] + center_terms
@@ -514,59 +520,100 @@
     if count == 2:
         terms = scatter(flipped[:, domain(1)], hot_t_ref[1], placed[1][3], groups_of(1))
         tiles += [terms[8 * i : 8 * i + 8] for i in range(3)]
+    else:
+        tiles += [jnp.zeros((8, LANES), F32)] * 3
     edge_near_ref[...] = tiles[3]
     edge_far_ref[...] = tiles[6]
+    edge_over_ref[...] = tiles[9]
     for j, (minus, plus) in enumerate(
-        ((tiles[0], tiles[1]), (tiles[2], tiles[4]), (tiles[5], tiles[7]))
+        (
+            (tiles[0], tiles[1]),
+            (tiles[2], tiles[4]),
+            (tiles[5], tiles[7]),
+            (tiles[8], tiles[10]),
+        )
     ):
         at = slice(8 * j, 8 * j + 8)
         back_far_ref[at] = jnp.where(even_n, plus, minus)
         back_near_ref[at] = jnp.where(even_n, minus, plus)
 
 
+def list_rows(raw_ref):
+    odd = lax.axis_index("outer") % 2 == 1
+    low = raw_ref[LISTS : LISTS + 8].astype(jnp.int32)
+    high = raw_ref[LISTS + 8 : LISTS + 16].astype(jnp.int32)
+    wide = jnp.concatenate([low, high], 1)
+    below, above = wide[0:3], wide[5:8]
+    return jnp.where(odd, below, above), jnp.where(odd, above, below), wide[3:5]
+
+
+def flat(ids):
+    return jnp.concatenate([ids[i : i + 1] for i in range(ids.shape[0])], 1)
+
+
+def spread_tile(tile):
+    rows = lax.broadcasted_iota(jnp.int32, (8, LANES), 0)
+    turned = pltpu.roll(tile, 4, 0)
+    return [jnp.where(rows < 4, tile, turned), jnp.where(rows < 4, turned, tile)]
+
+
+def hot_rows(ids):
+    lanes = lax.broadcasted_iota(jnp.int32, (1, LANES), 1).astype(F32).astype(BF16)
+    low = (ids & 127).astype(F32)
+    return jnp.concatenate(
+        [
+            hits(down_lanes(low[:, i : i + LANES]), lanes)
+            for i in range(0, ids.shape[1], LANES)
+        ],
+        0,
+    )
+
+
+def begin_kernel(
+    local_ref, raw_ref, up_ref, low_ref, edge_far_ref, total_ref, hot_ref, toward_ref
+):
+    even_n = lax.axis_index("inner") % 2 == 0
+    away, toward, along = list_rows(raw_ref)
+    plus = jnp.where(even_n, low_ref[...], up_ref[...])
+    minus = jnp.where(even_n, up_ref[...], low_ref[...])
+    toward_ref[0:8] = minus[16:24]
+    toward_ref[8:16] = edge_far_ref[...]
+    toward_ref[16:24] = plus[16:24]
+    ids = flat(along)
+    values = jnp.concatenate(spread_tile(minus[0:8]) + spread_tile(plus[0:8]), 1)
+    total_ref[...] = local_ref[...] + scatter(values, hot_rows(ids), ids >> 7, (0, 1))
+    hot_ref[...] = hot_rows(jnp.concatenate([flat(away), flat(toward)], 1))
+
+
 def collect_kernel(
-    local_ref,
+    total_ref,
+    hot_ref,
     raw_ref,
     up_ref,
     low_ref,
-    edge_far_ref,
+    edge_over_ref,
+    over_ref,
+    inside_ref,
     beside_ref,
-    cross_ref,
     forces_ref,
     energy_ref,
 ):
     even_n = lax.axis_index("inner") % 2 == 0
-    odd = lax.axis_index("outer") % 2 == 1
-    place = lax.axis_index("outer") % 4
-    at_border = (place == 0) | (place == 3)
-    plus = jnp.where(even_n, low_ref[...], up_ref[...])
-    minus = jnp.where(even_n, up_ref[...], low_ref[...])
-    over = jnp.concatenate([minus[16:24], edge_far_ref[...], plus[16:24]], 0)
-    toward = jnp.where(at_border, over, cross_ref[...])
+    low_half, at_border = row_kind()
+    plus = jnp.where(even_n, low_ref[24:32], up_ref[24:32])
+    minus = jnp.where(even_n, up_ref[24:32], low_ref[24:32])
+    toward = jnp.concatenate([minus, edge_over_ref[...], plus], 0)
+    toward = jnp.where(low_half, toward, over_ref[...])
+    toward = jnp.where(at_border, toward, inside_ref[...])
     away = beside_ref[...]
-    above = jnp.where(odd, toward, away)
-    below = jnp.where(odd, away, toward)
-    lists_low = raw_ref[LISTS : LISTS + 8].astype(jnp.int32)
-    lists_high = raw_ref[LISTS + 8 : LISTS + 16].astype(jnp.int32)
-    rows = lax.broadcasted_iota(jnp.int32, (8, LANES), 0)
-    ids, values = [], []
-    for k, (dx, dy) in enumerate(DIRS):
-        ids += [lists_low[k : k + 1], lists_high[k : k + 1]]
-        if dx == 0:
-            tile = (minus if dy < 0 else plus)[0:8]
-        else:
-            at = 8 * (dy + 1)
-            tile = (above if dx > 0 else below)[at : at + 8]
-        turned = pltpu.roll(tile, 4, 0)
-        values += [jnp.where(rows < 4, tile, turned), jnp.where(rows < 4, turned, tile)]
-    ids = jnp.concatenate(ids, 1)
+    ids = list_rows(raw_ref)
+    ids = jnp.concatenate([flat(ids[0]), flat(ids[1])], 1)
+    values = []
+    for tiles in (away, toward):
+        for j in range(3):
+            values += spread_tile(tiles[8 * j : 8 * j + 8])
     values = jnp.concatenate(values, 1)
-    hot_t = []
-    lanes = lax.broadcasted_iota(jnp.int32, (1, LANES), 1).astype(F32).astype(BF16)
-    for k in range(len(DIRS)):
-        for tile in (lists_low, lists_high):
-            hot_t.append(hits(down_lanes((tile[k : k + 1] & 127).astype(F32)), lanes))
-    total = local_ref[...] + scatter(values, jnp.concatenate(hot_t, 0), ids >> 7, (0, 1))
+    total = total_ref[...] + scatter(values, hot_ref[...], ids >> 7, (0, 1))
     for j in range(4):
         forces_ref[:, j * LANES : (j + 1) * LANES] = total[4 * j : 4 * j + 3]
         energy_ref[:, j * LANES : (j + 1) * LANES] = total[4 * j + 3 : 4 * j + 4]
@@ -648,13 +695,12 @@
             for value in (w_rad, emb_center, emb_neigh, w_env.T, w_lat, w_out.reshape(1, -1))
         )
     )
-    row_count = lax.axis_size("outer")
-    low_half = range(row_count // 2)
-    high_half = range(row_count // 2, row_count)
-    beside_low = swap_outer(packed, 0, low_half)
-    border = over_border(packed)
-    cross = swap_outer(packed, 1, range(row_count))
-    beside_high = swap_outer(packed, 0, high_half)
+    count = lax.axis_size("outer")
+    half = count // 2
+    first = copy_rows(packed, {0: 1, half - 1: half - 2, half + 1: half - 1, count - 2: 0})
+    second = copy_rows(packed, {1: 0, half - 2: half - 1})
+    cross = swap_outer(packed, 1, range(count))
+    high = swap_outer(packed, 0, range(half, count))
     far, near, mid, raw = pl.pallas_call(
         sends_kernel,
         out_shape=[
@@ -665,12 +711,12 @@
         ],
         compiler_params=SMALL,
         name="gather_sends",
-    )(packed, beside_low, border, cross, beside_high, weights[3])
+    )(packed, high, cross, second, first, weights[3])
     up = swap_inner(far, 1)
     low = swap_inner(near, 0)
-    local, edge_near, edge_far, far, near = pl.pallas_call(
+    local, edge_near, edge_far, edge_over, far, near = pl.pallas_call(
         lambda *refs: pair_kernel(feat, pair_len, *refs),
-        out_shape=[rows(16), rows(8), rows(8), rows(24), rows(24)],
+        out_shape=[rows(16), rows(8), rows(8), rows(8), rows(32), rows(32)],
         scratch_shapes=[
             pltpu.VMEM((2, pair_len, pair_len), BF16),
             pltpu.VMEM((3, pair_len, LANES), BF16),
@@ -686,13 +732,18 @@
     even_n = lax.axis_index("inner") % 2 == 0
     plus = jnp.where(even_n, low, up)
     minus = jnp.where(even_n, up, low)
-    inside = [o for o in range(row_count) if o % 4 in (1, 2)]
-    cross = swap_outer(
-        jnp.concatenate([minus[16:24], edge_far, plus[16:24]], 0), 1, inside
-    )
-    beside = swap_outer(
-        jnp.concatenate([minus[8:16], edge_near, plus[8:16]], 0), 0, range(row_count)
-    )
+    toward = jnp.concatenate([minus[16:24], edge_far, plus[16:24]], 0)
+    away = jnp.concatenate([minus[8:16], edge_near, plus[8:16]], 0)
+    inside = swap_outer(toward, 1, [o for o in range(count) if o % half not in (0, half - 1)])
+    beside = swap_outer(away, 0, range(count))
+    total, hot, toward = pl.pallas_call(
+        begin_kernel,
+        out_shape=[rows(16), jax.ShapeDtypeStruct((6 * 2 * LANES, LANES), BF16), rows(24)],
+        compiler_params=SMALL,
+        cost_estimate=pl.CostEstimate(flops=0, bytes_accessed=4_000_000, transcendentals=0),
+        name="begin_terms",
+    )(local, packed, up, low, edge_far)
+    over = copy_rows(toward, {0: count - 1, half - 1: half})
     forces, energy = pl.pallas_call(
         collect_kernel,
         out_shape=[
@@ -701,7 +752,7 @@
         ],
         compiler_params=SMALL,
         name="collect_terms",
-    )(local, packed, up, low, edge_far, beside, cross)
+    )(total, hot, packed, up, low, edge_over, over, inside, beside)
     return forces, energy.reshape(atom_count)
 
 

time: 53.5 us -> 57.4 us (1.073)
  starting transfers between devices: 38.9 us -> 43.9 us
  waiting for transfers between devices: 3.6 us -> 2.42 us
    ppermute x10 -> x11, starting transfers between devices: 38.9 us -> 43.9 us  [permute(): return lax.ppermute(block, AXES, route)]
    ppermute x10 -> x11, waiting for transfers between devices: 3.6 us -> 2.42 us  [permute(): return lax.ppermute(block, AXES, route)]
  transfers between devices with their start and end apart: 10 -> 11, of which waited for: 3 -> 3; matrix products, arithmetic and copies ran while one was open for 0% -> 0% of each run, Pallas kernels for 2% -> 2%
where the time goes in v7:
time: 57.4 us; the launch traced here: 57 us
  starting transfers between devices  43.9 us (76%)
  Pallas kernels  9.19 us (16%)
  waiting for transfers between devices  2.42 us (4%)
  between operations  1.48 us (3%)
    ppermute x11, starting transfers between devices, permute(): return lax.ppermute(block, AXES, route)  43.9 us
    pallas_call x1, Pallas kernels, on_device(): pl.pallas_call(lambda *refs: pair_kernel(feat, pair_len, *refs), out_shap...  6.01 us
    ppermute x11, waiting for transfers between devices, permute(): return lax.ppermute(block, AXES, route)  2.42 us
  transfers between devices with their start and end apart: 11, of which 3 were waited for; matrix products, arithmetic and copies ran while one was open for 0% of the time, Pallas kernels for 2%

profile of v7, /device:TPU:1, one launch (start us, length us, event | category | flops | bytes accessed | tf_op | source)
XLA Modules:
  0.0 57.0 jit_solution(13145480457357179178)
XLA Ops:
  1.3 0.8 %pack_domain.1.own_ref.raw_ref = f32[48,128]{1,0:T(8,128)S(1)} custom-call(f32[3,512]{1,0:T(4,128)} %pos_hbm.1, s32[1,512]{1,0:T(1,128)} %bitcast.9, s32[8,176]{1,0:T(8,128)} %lists_hbm.1, s32[6,128]{1,0:T(8,128)} %bitcast.7, s32[6,128]{1,0:T(8,128)} %bitcast.8, s32[1]{0:T(128)S(6)} %copy.14.live_ref), custom_call_target="tpu_custom_call" | custom-call | tf_op jit(solution)/shard_map/pack_domain/pallas_call | solution.py:645
  2.1 3.9 %collective-permute-start.3 = (f32[48,128]{1,0:T(8,128)S(1)}, f32[48,128]{1,0:T(8,128)S(1)}, u32[]{:S(2)}, u32[]{:S(2)}) collective-permute-start(f32[48,128]{1,0:T(8,128)S(1)} %pack_domain.1.own_ref.raw_ref), channel_id=1, source_target_pairs={{0,64},{1,65},{2,66},{3,67},{4,68},{5,69},{6,70},{7,71},{8,72},{9,... | collective-permute-start | bytes 73736 | tf_op jit(solution)/shard_map/ppermute | solution.py:36
  6.0 1.3 %collective-permute-start.2 = (f32[48,128]{1,0:T(8,128)S(1)}, f32[48,128]{1,0:T(8,128)S(1)}, u32[]{:S(2)}, u32[]{:S(2)}) collective-permute-start(f32[48,128]{1,0:T(8,128)S(1)} %pack_domain.1.own_ref.raw_ref), channel_id=1, source_target_pairs={{64,0},{65,1},{66,2},{67,3},{68,4},{69,5},{70,6},{71,7},{72,8},{73... | collective-permute-start | bytes 73736 | tf_op jit(solution)/shard_map/ppermute | solution.py:36
  7.3 9.7 %collective-permute-start.1 = (f32[48,128]{1,0:T(8,128)S(1)}, f32[48,128]{1,0:T(8,128)S(1)}, u32[]{:S(2)}, u32[]{:S(2)}) collective-permute-start(f32[48,128]{1,0:T(8,128)S(1)} %pack_domain.1.own_ref.raw_ref), channel_id=1, source_target_pairs={{0,448},{1,449},{2,450},{3,451},{4,452},{5,453},{6,454},{7,455},{8... | collective-permute-start | bytes 73736 | tf_op jit(solution)/shard_map/ppermute | solution.py:36
  17.1 0.7 %collective-permute-start = (f32[48,128]{1,0:T(8,128)S(1)}, f32[48,128]{1,0:T(8,128)S(1)}, u32[]{:S(2)}, u32[]{:S(2)}) collective-permute-start(f32[48,128]{1,0:T(8,128)S(1)} %pack_domain.1.own_ref.raw_ref), channel_id=1, source_target_pairs={{256,320},{257,321},{258,322},{259,323},{260,324},{261,325},{262,3... | collective-permute-start | bytes 73736 | tf_op jit(solution)/shard_map/ppermute | solution.py:36
  17.8 1.0 %place_weights.1 = (bf16[64,128]{1,0:T(8,128)(2,1)S(1)}, bf16[192,128]{1,0:T(8,128)(2,1)S(1)}, bf16[320,128]{1,0:T(8,128)(2,1)S(1)}, bf16[16,128]{1,0:T(8,128)(2,1)S(1)}) custom-call(f32[8,128]{1,0:T(8,128)} %w_rad_hbm.1, bf16[7,128]{1,0:T(8,128)(2,1)} %emb_center_hbm.1, bf16[7,128]{1,0:T(8,128)(2,1)} %emb_neigh_hbm.1, bf16[192,128]{1,0:T(8,128)(2,1)} %bitcast.6, ...), custom_call_target="tpu_custom_call" | custom-call | bytes 4000000 | tf_op jit(solution)/shard_map/place_weights/pallas_call | solution.py:673
  18.8 0.0 collective-permute-done.3.first_ref
  18.8 0.0 collective-permute-done.2.second_ref
  18.8 0.0 collective-permute-done.1.cross_ref
  18.8 0.0 collective-permute-done.high_ref
  18.9 0.3 gather_sends.1
  19.2 5.1 %collective-permute-start.4 = (f32[48,128]{1,0:T(8,128)S(1)}, f32[48,128]{1,0:T(8,128)S(1)}, u32[]{:S(2)}, u32[]{:S(2)}) collective-permute-start(f32[48,128]{1,0:T(8,128)S(1)} %get-tuple-element.24), channel_id=1, source_target_pairs={{0,63},{1,2},{2,1},{3,4},{4,3},{5,6},{6,5},{7,8},{8,7},{9,10},{10,... | collective-permute-start | bytes 73736 | tf_op jit(solution)/shard_map/ppermute | solution.py:36
  24.3 6.8 %collective-permute-start.5 = (f32[48,128]{1,0:T(8,128)S(1)}, f32[48,128]{1,0:T(8,128)S(1)}, u32[]{:S(2)}, u32[]{:S(2)}) collective-permute-start(f32[48,128]{1,0:T(8,128)S(1)} %get-tuple-element.25), channel_id=1, source_target_pairs={{0,1},{1,0},{2,3},{3,2},{4,5},{5,4},{6,7},{7,6},{8,9},{9,8},{10,11... | collective-permute-start | bytes 73736 | tf_op jit(solution)/shard_map/ppermute | solution.py:36
  31.1 0.0 collective-permute-done.4.refs_2_
  31.1 0.8 %collective-permute-done.5.refs_3_ = f32[48,128]{1,0:T(8,128)S(1)} collective-permute-done((f32[48,128]{1,0:T(8,128)S(1)}, f32[48,128]{1,0:T(8,128)S(1)}, u32[]{:S(2)}, u32[]{:S(2)}) %collective-permute-start.5) | collective-permute-done | bytes 24608 | tf_op jit(solution)/shard_map/ppermute | solution.py:36
  31.9 6.0 %pair_terms.1 = (f32[16,128]{1,0:T(8,128)S(1)}, f32[8,128]{1,0:T(8,128)S(1)}, f32[8,128]{1,0:T(8,128)S(1)}, f32[8,128]{1,0:T(8,128)S(1)}, f32[32,128]{1,0:T(8,128)S(1)}, /*index=5*/f32[32,128]{1,0:T(8,128)S(1)}) custom-call(f32[2,48,128]{2,1,0:T(8,128)S(1)} %get-tuple-element.22.refs_0_, f32[32,128]{1,0:T(8,128)S(1)} %get-tuple-element.23.refs_1_, ...), custom_call_target="tpu_custom_call" | custom-call | tf_op jit(solution)/shard_map/pair_terms/pallas_call | solution.py:717
  37.9 1.9 %collective-permute-start.6 = (f32[32,128]{1,0:T(8,128)S(1)}, f32[32,128]{1,0:T(8,128)S(1)}, u32[]{:S(2)}, u32[]{:S(2)}) collective-permute-start(f32[32,128]{1,0:T(8,128)S(1)} %get-tuple-element.30), channel_id=1, source_target_pairs={{0,63},{1,2},{2,1},{3,4},{4,3},{5,6},{6,5},{7,8},{8,7},{9,10},{10,... | collective-permute-start | bytes 49160 | tf_op jit(solution)/shard_map/ppermute | solution.py:36
  39.9 6.3 %collective-permute-start.7 = (f32[32,128]{1,0:T(8,128)S(1)}, f32[32,128]{1,0:T(8,128)S(1)}, u32[]{:S(2)}, u32[]{:S(2)}) collective-permute-start(f32[32,128]{1,0:T(8,128)S(1)} %get-tuple-element.31), channel_id=1, source_target_pairs={{0,1},{1,0},{2,3},{3,2},{4,5},{5,4},{6,7},{7,6},{8,9},{9,8},{10,11... | collective-permute-start | bytes 49160 | tf_op jit(solution)/shard_map/ppermute | solution.py:36
  46.2 0.0 collective-permute-done.6.up_ref
  46.2 0.8 %collective-permute-done.7.low_ref = f32[32,128]{1,0:T(8,128)S(1)} collective-permute-done((f32[32,128]{1,0:T(8,128)S(1)}, f32[32,128]{1,0:T(8,128)S(1)}, u32[]{:S(2)}, u32[]{:S(2)}) %collective-permute-start.7) | collective-permute-done | bytes 16416 | tf_op jit(solution)/shard_map/ppermute | solution.py:36
  47.0 0.7 %collective-permute-start.9 = (f32[24,128]{1,0:T(8,128)S(1)}, f32[24,128]{1,0:T(8,128)S(1)}, u32[]{:S(2)}, u32[]{:S(2)}) collective-permute-start(f32[24,128]{1,0:T(8,128)S(1)} %pad_maximum_fusion), channel_id=1, source_target_pairs={{64,128},{65,129},{66,130},{67,131},{68,132},{69,133},{70,134},{71... | collective-permute-start | bytes 36872 | tf_op jit(solution)/shard_map/ppermute | solution.py:36
  47.7 1.9 %collective-permute-start.10 = (f32[24,128]{1,0:T(8,128)S(1)}, f32[24,128]{1,0:T(8,128)S(1)}, u32[]{:S(2)}, u32[]{:S(2)}) collective-permute-start(f32[24,128]{1,0:T(8,128)S(1)} %pad_maximum_fusion.1), channel_id=1, source_target_pairs={{0,64},{1,65},{2,66},{3,67},{4,68},{5,69},{6,70},{7,71},{8,72},{9,... | collective-permute-start | bytes 36872 | tf_op jit(solution)/shard_map/ppermute | solution.py:36
  49.6 0.2 begin_terms.1
  49.8 5.5 %collective-permute-start.8 = (f32[24,128]{1,0:T(8,128)S(1)}, f32[24,128]{1,0:T(8,128)S(1)}, u32[]{:S(2)}, u32[]{:S(2)}) collective-permute-start(f32[24,128]{1,0:T(8,128)S(1)} %get-tuple-element.36), channel_id=1, source_target_pairs={{0,448},{1,449},{2,450},{3,451},{4,452},{5,453},{6,454},{7,455},{8... | collective-permute-start | bytes 36872 | tf_op jit(solution)/shard_map/ppermute | solution.py:36
  55.4 0.0 collective-permute-done.9.inside_ref
  55.4 0.0 collective-permute-done.10.beside_ref
  55.4 0.8 %collective-permute-done.8.over_ref = f32[24,128]{1,0:T(8,128)S(1)} collective-permute-done((f32[24,128]{1,0:T(8,128)S(1)}, f32[24,128]{1,0:T(8,128)S(1)}, u32[]{:S(2)}, u32[]{:S(2)}) %collective-permute-start.8) | collective-permute-done | bytes 12320 | tf_op jit(solution)/shard_map/ppermute | solution.py:36
  56.2 0.8 %collect_terms.1 = (f32[3,512]{1,0:T(4,128)}, f32[1,512]{1,0:T(1,128)}) custom-call(f32[16,128]{1,0:T(8,128)S(1)} %get-tuple-element.33.total_ref, bf16[1536,128]{1,0:T(8,128)(2,1)S(1)} %get-tuple-element.34.hot_ref, f32[48,128]{1,0:T(8,128)S(1)} %pack_domain.1.own_ref.raw_ref, f32[32,128]{1,0:T(8,128)S(1)} %collective-permute-done.6.up_ref, ...), custom_call_target="tpu_custom_call" | custom-call | tf_op jit(solution)/shard_map/collect_terms/pallas_call | solution.py:747
  (4 shorter events, 0.0 us)
Async XLA Ops:
  2.1 16.7 %collective-permute-start.3 = (f32[48,128]{1,0:T(8,128)S(1)}, f32[48,128]{1,0:T(8,128)S(1)}, u32[]{:S(2)}, u32[]{:S(2)}) collective-permute-start(f32[48,128]{1,0:T(8,128)S(1)} %pack_domain.1.own_ref.raw_ref), channel_id=1, source_target_pairs={{0,64},{1,65},{2,66},{3,67},{4,68},{5,69},{6,70},{7,71},{8,72},{9,... | collective-permute-start | bytes 73736 | tf_op jit(solution)/shard_map/ppermute | solution.py:36
  6.0 12.8 %collective-permute-start.2 = (f32[48,128]{1,0:T(8,128)S(1)}, f32[48,128]{1,0:T(8,128)S(1)}, u32[]{:S(2)}, u32[]{:S(2)}) collective-permute-start(f32[48,128]{1,0:T(8,128)S(1)} %pack_domain.1.own_ref.raw_ref), channel_id=1, source_target_pairs={{64,0},{65,1},{66,2},{67,3},{68,4},{69,5},{70,6},{71,7},{72,8},{73... | collective-permute-start | bytes 73736 | tf_op jit(solution)/shard_map/ppermute | solution.py:36
  7.3 11.5 %collective-permute-start.1 = (f32[48,128]{1,0:T(8,128)S(1)}, f32[48,128]{1,0:T(8,128)S(1)}, u32[]{:S(2)}, u32[]{:S(2)}) collective-permute-start(f32[48,128]{1,0:T(8,128)S(1)} %pack_domain.1.own_ref.raw_ref), channel_id=1, source_target_pairs={{0,448},{1,449},{2,450},{3,451},{4,452},{5,453},{6,454},{7,455},{8... | collective-permute-start | bytes 73736 | tf_op jit(solution)/shard_map/ppermute | solution.py:36
  17.1 1.8 %collective-permute-start = (f32[48,128]{1,0:T(8,128)S(1)}, f32[48,128]{1,0:T(8,128)S(1)}, u32[]{:S(2)}, u32[]{:S(2)}) collective-permute-start(f32[48,128]{1,0:T(8,128)S(1)} %pack_domain.1.own_ref.raw_ref), channel_id=1, source_target_pairs={{256,320},{257,321},{258,322},{259,323},{260,324},{261,325},{262,3... | collective-permute-start | bytes 73736 | tf_op jit(solution)/shard_map/ppermute | solution.py:36
  19.2 11.9 %collective-permute-start.4 = (f32[48,128]{1,0:T(8,128)S(1)}, f32[48,128]{1,0:T(8,128)S(1)}, u32[]{:S(2)}, u32[]{:S(2)}) collective-permute-start(f32[48,128]{1,0:T(8,128)S(1)} %get-tuple-element.24), channel_id=1, source_target_pairs={{0,63},{1,2},{2,1},{3,4},{4,3},{5,6},{6,5},{7,8},{8,7},{9,10},{10,... | collective-permute-start | bytes 73736 | tf_op jit(solution)/shard_map/ppermute | solution.py:36
  24.3 7.7 %collective-permute-start.5 = (f32[48,128]{1,0:T(8,128)S(1)}, f32[48,128]{1,0:T(8,128)S(1)}, u32[]{:S(2)}, u32[]{:S(2)}) collective-permute-start(f32[48,128]{1,0:T(8,128)S(1)} %get-tuple-element.25), channel_id=1, source_target_pairs={{0,1},{1,0},{2,3},{3,2},{4,5},{5,4},{6,7},{7,6},{8,9},{9,8},{10,11... | collective-permute-start | bytes 73736 | tf_op jit(solution)/shard_map/ppermute | solution.py:36
  37.9 8.2 %collective-permute-start.6 = (f32[32,128]{1,0:T(8,128)S(1)}, f32[32,128]{1,0:T(8,128)S(1)}, u32[]{:S(2)}, u32[]{:S(2)}) collective-permute-start(f32[32,128]{1,0:T(8,128)S(1)} %get-tuple-element.30), channel_id=1, source_target_pairs={{0,63},{1,2},{2,1},{3,4},{4,3},{5,6},{6,5},{7,8},{8,7},{9,10},{10,... | collective-permute-start | bytes 49160 | tf_op jit(solution)/shard_map/ppermute | solution.py:36
  39.9 7.1 %collective-permute-start.7 = (f32[32,128]{1,0:T(8,128)S(1)}, f32[32,128]{1,0:T(8,128)S(1)}, u32[]{:S(2)}, u32[]{:S(2)}) collective-permute-start(f32[32,128]{1,0:T(8,128)S(1)} %get-tuple-element.31), channel_id=1, source_target_pairs={{0,1},{1,0},{2,3},{3,2},{4,5},{5,4},{6,7},{7,6},{8,9},{9,8},{10,11... | collective-permute-start | bytes 49160 | tf_op jit(solution)/shard_map/ppermute | solution.py:36
  47.0 8.4 %collective-permute-start.9 = (f32[24,128]{1,0:T(8,128)S(1)}, f32[24,128]{1,0:T(8,128)S(1)}, u32[]{:S(2)}, u32[]{:S(2)}) collective-permute-start(f32[24,128]{1,0:T(8,128)S(1)} %pad_maximum_fusion), channel_id=1, source_target_pairs={{64,128},{65,129},{66,130},{67,131},{68,132},{69,133},{70,134},{71... | collective-permute-start | bytes 36872 | tf_op jit(solution)/shard_map/ppermute | solution.py:36
  47.7 7.7 %collective-permute-start.10 = (f32[24,128]{1,0:T(8,128)S(1)}, f32[24,128]{1,0:T(8,128)S(1)}, u32[]{:S(2)}, u32[]{:S(2)}) collective-permute-start(f32[24,128]{1,0:T(8,128)S(1)} %pad_maximum_fusion.1), channel_id=1, source_target_pairs={{0,64},{1,65},{2,66},{3,67},{4,68},{5,69},{6,70},{7,71},{8,72},{9,... | collective-permute-start | bytes 36872 | tf_op jit(solution)/shard_map/ppermute | solution.py:36
  49.8 6.3 %collective-permute-start.8 = (f32[24,128]{1,0:T(8,128)S(1)}, f32[24,128]{1,0:T(8,128)S(1)}, u32[]{:S(2)}, u32[]{:S(2)}) collective-permute-start(f32[24,128]{1,0:T(8,128)S(1)} %get-tuple-element.36), channel_id=1, source_target_pairs={{0,448},{1,449},{2,450},{3,451},{4,452},{5,453},{6,454},{7,455},{8... | collective-permute-start | bytes 36872 | tf_op jit(solution)/shard_map/ppermute | solution.py:36

commit v8 on v7

--- a/solution.py
+++ b/solution.py
@@ -207,15 +207,14 @@
 
 
 def sends_kernel(
-    own_ref, high_ref, cross_ref, second_ref, first_ref, _, far_ref, near_ref, mid_ref, raw_ref
+    own_ref, first_ref, border_ref, cross_ref, last_ref, _, far_ref, near_ref, mid_ref, raw_ref
 ):
     even_n = lax.axis_index("inner") % 2 == 0
     odd = lax.axis_index("outer") % 2 == 1
-    low_half, at_border = row_kind()
+    low_half, _ = row_kind()
     rows = lax.broadcasted_iota(jnp.int32, (8, LANES), 0)
     own, cross = own_ref[...], cross_ref[...]
-    beside = jnp.where(at_border, second_ref[...], first_ref[...])
-    beside = jnp.where(low_half, beside, high_ref[...])
+    beside = jnp.where(low_half, first_ref[...], last_ref[...])
     raw_ref[0] = own
     raw_ref[1] = cross
 
@@ -245,7 +244,7 @@
     by_own = tiles_of(own, (1, 0))
     by_cross = tiles_of(cross, (0, -1))
     by_beside = tiles_of(beside, (1,))
-    by_border = tiles_of(first_ref[...], (-1,))
+    by_border = tiles_of(border_ref[...], (-1,))
     sources = ({1: by_beside, 0: by_own, -1: by_cross}, {1: by_own, 0: by_cross, -1: by_border})
     for extra in range(2):
         for side in (1, 0, -1):
@@ -278,9 +277,34 @@
     return sign * rest * sine, sign * cosine
 
 
+def neigh_place(tile):
+    neigh = tile.astype(jnp.int32)
+    ghost = neigh - 512
+    listed = (ghost * 745) >> 17
+    entry = ghost - 176 * listed
+    is_local = neigh < 512
+    low = jnp.where(is_local, neigh & 127, entry & 127)
+    high = jnp.where(is_local, neigh >> 7, 4 + 2 * listed + (entry >> 7))
+    return low, high
+
+
+def columns_kernel(raw_ref, down_ref, hot_t_ref):
+    lanes = lax.broadcasted_iota(jnp.int32, (1, LANES), 1).astype(F32).astype(BF16)
+    for d in range(2):
+        centers = raw_ref[d, CENTERS : CENTERS + 8]
+        low, _ = neigh_place(raw_ref[d, NEIGH : NEIGH + 8])
+        low = low.astype(F32)
+        own_low = (centers.astype(jnp.int32) & 127).astype(F32)
+        for i in range(down_ref.shape[1] // LANES):
+            at = slice(i * LANES, (i + 1) * LANES)
+            down_ref[d, at] = down_lanes(centers[i : i + 1] - 256.0)
+            hot_t_ref[d, at] = hits(down_lanes(low[i : i + 1]), lanes)
+            if d == 0:
+                hot_t_ref[2, at] = hits(down_lanes(own_low[i : i + 1]), lanes)
+
+
 def pair_kernel(feat, pair_len, *refs):
-    low_half, at_border = row_kind()
-    two = low_half & at_border
+    _, two = row_kind()
     pl.when(two)(lambda: pair_body(2, feat, pair_len, *refs))
     pl.when(jnp.logical_not(two))(lambda: pair_body(1, feat, pair_len, *refs))
 
@@ -293,6 +317,8 @@
     mid_ref,
     up_ref,
     low_ref,
+    down_ref,
+    hot_t_ref,
     front_ref,
     w_env_ref,
     w_lat_ref,
@@ -300,11 +326,9 @@
     local_ref,
     edge_near_ref,
     edge_far_ref,
-    edge_over_ref,
     back_far_ref,
     back_near_ref,
     same_ref,
-    hot_t_ref,
     contrib_ref,
     gath_ref,
     back_ref,
@@ -313,8 +337,6 @@
     lat = w_lat_ref.shape[1]
     even_n = lax.axis_index("inner") % 2 == 0
     odd = lax.axis_index("outer") % 2 == 1
-    lanes = lax.broadcasted_iota(jnp.int32, (1, LANES), 1).astype(F32).astype(BF16)
-
     front = front_ref[...]
     w1, w2 = front[0:8], front[8:16]
     w_env = w_env_ref[...]
@@ -324,11 +346,6 @@
     def as_row(tile):
         return jnp.concatenate([tile[i : i + 1] for i in range(chunks)], 1)
 
-    def onehot_t(low_tile):
-        return jnp.concatenate(
-            [hits(down_lanes(low_tile[i : i + 1].astype(F32)), lanes) for i in range(chunks)], 0
-        )
-
     def feat_rows(k):
         return slice(k * feat, (k + 1) * feat)
 
@@ -342,7 +359,7 @@
         shifted = raw_ref[d, CENTERS : CENTERS + 8] - 256.0
         across = shifted.astype(BF16)
         for i in range(chunks):
-            down = down_lanes(shifted[i : i + 1])
+            down = down_ref[d, i * LANES : (i + 1) * LANES]
             for j in range(chunks):
                 same_ref[d, i * LANES : (i + 1) * LANES, j * LANES : (j + 1) * LANES] = hits(
                     down, across[j : j + 1]
@@ -367,20 +384,12 @@
             else:
                 table.append(jnp.where(odd, ghost_tile(dx, dy), ghost_tile(-dx, dy)))
         table = jnp.concatenate(table, 0)
-        neigh = raw[NEIGH : NEIGH + 8].astype(jnp.int32)
-        ghost = neigh - 512
-        listed = (ghost * 745) >> 17
-        entry = ghost - 176 * listed
-        is_local = neigh < 512
-        neigh_low = jnp.where(is_local, neigh & 127, entry & 127)
-        hot_t_ref[d] = onehot_t(neigh_low)
-        neigh_high = as_row(jnp.where(is_local, neigh >> 7, 4 + 2 * listed + (entry >> 7)))
+        neigh_low, neigh_high = neigh_place(raw[NEIGH : NEIGH + 8])
+        neigh_high = as_row(neigh_high)
         center_ids = as_row(centers.astype(jnp.int32))
         center_high = center_ids >> 7
         at_neigh = gather(table, onehot_low(as_row(neigh_low)), neigh_high)
         at_center = gather(table[0:16], onehot_low(center_ids & 127), center_high)
-        if d == 0:
-            hot_t_ref[2] = onehot_t(centers.astype(jnp.int32) & 127)
         block = lax.broadcasted_iota(jnp.int32, (1, pair_len), 1) // 128
         mask = jnp.where(block.astype(F32) < raw[LIVE : LIVE + 1, 0:1], 1.0, 0.0)
         return at_neigh, at_center, mask, neigh_high, center_high
@@ -512,7 +521,7 @@
         return [2 + (first if side > 0 else 5 - first) + i for i in range(3)]
 
     neigh_high, center_high = placed[0][3:]
-    groups = [0, 1, 2 + 3, 2 + 4] + groups_of(1) + groups_of(-1)
+    groups = [0, 1, 2 + 3, 2 + 4] + groups_of(1) + (groups_of(-1) if count == 1 else [])
     terms = scatter(flipped[:, domain(0)], hot_t_ref[0], neigh_high, groups)
     center_terms = scatter(values[:, domain(0)], hot_t_ref[2], center_high, (0, 1))
     local_ref[...] = terms[0:16] + center_terms
@@ -520,17 +529,13 @@
     if count == 2:
         terms = scatter(flipped[:, domain(1)], hot_t_ref[1], placed[1][3], groups_of(1))
         tiles += [terms[8 * i : 8 * i + 8] for i in range(3)]
-    else:
-        tiles += [jnp.zeros((8, LANES), F32)] * 3
     edge_near_ref[...] = tiles[3]
     edge_far_ref[...] = tiles[6]
-    edge_over_ref[...] = tiles[9]
     for j, (minus, plus) in enumerate(
         (
             (tiles[0], tiles[1]),
             (tiles[2], tiles[4]),
             (tiles[5], tiles[7]),
-            (tiles[8], tiles[10]),
         )
     ):
         at = slice(8 * j, 8 * j + 8)
@@ -570,17 +575,14 @@
 
 
 def begin_kernel(
-    local_ref, raw_ref, up_ref, low_ref, edge_far_ref, total_ref, hot_ref, toward_ref
+    local_ref, raw_ref, up_ref, low_ref, total_ref, hot_ref
 ):
     even_n = lax.axis_index("inner") % 2 == 0
     away, toward, along = list_rows(raw_ref)
-    plus = jnp.where(even_n, low_ref[...], up_ref[...])
-    minus = jnp.where(even_n, up_ref[...], low_ref[...])
-    toward_ref[0:8] = minus[16:24]
-    toward_ref[8:16] = edge_far_ref[...]
-    toward_ref[16:24] = plus[16:24]
+    plus = jnp.where(even_n, low_ref[0:8], up_ref[0:8])
+    minus = jnp.where(even_n, up_ref[0:8], low_ref[0:8])
     ids = flat(along)
-    values = jnp.concatenate(spread_tile(minus[0:8]) + spread_tile(plus[0:8]), 1)
+    values = jnp.concatenate(spread_tile(minus) + spread_tile(plus), 1)
     total_ref[...] = local_ref[...] + scatter(values, hot_rows(ids), ids >> 7, (0, 1))
     hot_ref[...] = hot_rows(jnp.concatenate([flat(away), flat(toward)], 1))
 
@@ -591,20 +593,18 @@
     raw_ref,
     up_ref,
     low_ref,
-    edge_over_ref,
-    over_ref,
+    edge_far_ref,
+    beside_ref,
     inside_ref,
-    beside_ref,
     forces_ref,
     energy_ref,
 ):
     even_n = lax.axis_index("inner") % 2 == 0
-    low_half, at_border = row_kind()
-    plus = jnp.where(even_n, low_ref[24:32], up_ref[24:32])
-    minus = jnp.where(even_n, up_ref[24:32], low_ref[24:32])
-    toward = jnp.concatenate([minus, edge_over_ref[...], plus], 0)
-    toward = jnp.where(low_half, toward, over_ref[...])
-    toward = jnp.where(at_border, toward, inside_ref[...])
+    _, at_border = row_kind()
+    plus = jnp.where(even_n, low_ref[16:24], up_ref[16:24])
+    minus = jnp.where(even_n, up_ref[16:24], low_ref[16:24])
+    over = jnp.concatenate([minus, edge_far_ref[...], plus], 0)
+    toward = jnp.where(at_border, over, inside_ref[...])
     away = beside_ref[...]
     ids = list_rows(raw_ref)
     ids = jnp.concatenate([flat(ids[0]), flat(ids[1])], 1)
@@ -697,10 +697,11 @@
     )
     count = lax.axis_size("outer")
     half = count // 2
-    first = copy_rows(packed, {0: 1, half - 1: half - 2, half + 1: half - 1, count - 2: 0})
-    second = copy_rows(packed, {1: 0, half - 2: half - 1})
+    low, high = half - 1, count - 1
+    first = swap_outer(packed, 0, range(half))
+    border = copy_rows(packed, {1: high, low - 1: half, half + 1: low, high - 1: 0})
     cross = swap_outer(packed, 1, range(count))
-    high = swap_outer(packed, 0, range(half, count))
+    last = swap_outer(packed, 0, range(half, count))
     far, near, mid, raw = pl.pallas_call(
         sends_kernel,
         out_shape=[
@@ -711,22 +712,31 @@
         ],
         compiler_params=SMALL,
         name="gather_sends",
-    )(packed, high, cross, second, first, weights[3])
+    )(packed, first, border, cross, last, weights[3])
     up = swap_inner(far, 1)
     low = swap_inner(near, 0)
-    local, edge_near, edge_far, edge_over, far, near = pl.pallas_call(
+    down, hot_t = pl.pallas_call(
+        columns_kernel,
+        out_shape=[
+            jax.ShapeDtypeStruct((2, pair_len, LANES), BF16),
+            jax.ShapeDtypeStruct((3, pair_len, LANES), BF16),
+        ],
+        compiler_params=SMALL,
+        cost_estimate=pl.CostEstimate(flops=0, bytes_accessed=4_000_000, transcendentals=0),
+        name="pair_columns",
+    )(raw)
+    local, edge_near, edge_far, far, near = pl.pallas_call(
         lambda *refs: pair_kernel(feat, pair_len, *refs),
-        out_shape=[rows(16), rows(8), rows(8), rows(8), rows(32), rows(32)],
+        out_shape=[rows(16), rows(8), rows(8), rows(24), rows(24)],
         scratch_shapes=[
             pltpu.VMEM((2, pair_len, pair_len), BF16),
-            pltpu.VMEM((3, pair_len, LANES), BF16),
             pltpu.VMEM((2, 9 * feat, pair_len), BF16),
             pltpu.VMEM((2, 9 * feat, pair_len), F32),
             pltpu.VMEM((2, 9 * feat, pair_len), F32),
         ],
         compiler_params=LARGE,
         name="pair_terms",
-    )(raw, mid, up, low, *weights)
+    )(raw, mid, up, low, down, hot_t, *weights)
     up = swap_inner(far, 1)
     low = swap_inner(near, 0)
     even_n = lax.axis_index("inner") % 2 == 0
@@ -736,14 +746,13 @@
     away = jnp.concatenate([minus[8:16], edge_near, plus[8:16]], 0)
     inside = swap_outer(toward, 1, [o for o in range(count) if o % half not in (0, half - 1)])
     beside = swap_outer(away, 0, range(count))
-    total, hot, toward = pl.pallas_call(
+    total, hot = pl.pallas_call(
         begin_kernel,
-        out_shape=[rows(16), jax.ShapeDtypeStruct((6 * 2 * LANES, LANES), BF16), rows(24)],
+        out_shape=[rows(16), jax.ShapeDtypeStruct((6 * 2 * LANES, LANES), BF16)],
         compiler_params=SMALL,
         cost_estimate=pl.CostEstimate(flops=0, bytes_accessed=4_000_000, transcendentals=0),
         name="begin_terms",
-    )(local, packed, up, low, edge_far)
-    over = copy_rows(toward, {0: count - 1, half - 1: half})
+    )(local, packed, up, low)
     forces, energy = pl.pallas_call(
         collect_kernel,
         out_shape=[
@@ -752,7 +761,7 @@
         ],
         compiler_params=SMALL,
         name="collect_terms",
-    )(total, hot, packed, up, low, edge_over, over, inside, beside)
+    )(total, hot, packed, up, low, edge_far, beside, inside)
     return forces, energy.reshape(atom_count)
 
 

time: 57.4 us -> 53.2 us (0.927)
  starting transfers between devices: 43.9 us -> 39 us
    ppermute x11 -> x10, starting transfers between devices: 43.9 us -> 39 us  [permute(): return lax.ppermute(block, AXES, route)]
    ppermute x11 -> x10, waiting for transfers between devices: 2.42 us -> 2.83 us  [permute(): return lax.ppermute(block, AXES, route)]
  transfers between devices with their start and end apart: 11 -> 10, of which waited for: 3 -> 3; matrix products, arithmetic and copies ran while one was open for 0% -> 0% of each run, Pallas kernels for 2% -> 3%
where the time goes in v8:
time: 53.2 us; the launch traced here: 52.7 us
  starting transfers between devices  39 us (73%)
  Pallas kernels  9.35 us (18%)
  waiting for transfers between devices  2.83 us (5%)
  between operations  1.47 us (3%)
    ppermute x10, starting transfers between devices, permute(): return lax.ppermute(block, AXES, route)  39 us
    pallas_call x1, Pallas kernels, on_device(): pl.pallas_call(lambda *refs: pair_kernel(feat, pair_len, *refs), out_shap...  5.82 us
    ppermute x10, waiting for transfers between devices, permute(): return lax.ppermute(block, AXES, route)  2.83 us
  transfers between devices with their start and end apart: 10, of which 3 were waited for; matrix products, arithmetic and copies ran while one was open for 0% of the time, Pallas kernels for 3%

profile of v8, /device:TPU:1, one launch (start us, length us, event | category | flops | bytes accessed | tf_op | source)
XLA Modules:
  0.0 52.7 jit_solution(3192640382353075277)
XLA Ops:
  1.3 0.8 %pack_domain.1.own_ref.raw_ref = f32[48,128]{1,0:T(8,128)S(1)} custom-call(f32[3,512]{1,0:T(4,128)} %pos_hbm.1, s32[1,512]{1,0:T(1,128)} %bitcast.9, s32[8,176]{1,0:T(8,128)} %lists_hbm.1, s32[6,128]{1,0:T(8,128)} %bitcast.7, s32[6,128]{1,0:T(8,128)} %bitcast.8, s32[1]{0:T(128)S(6)} %copy.14.live_ref), custom_call_target="tpu_custom_call" | custom-call | tf_op jit(solution)/shard_map/pack_domain/pallas_call | solution.py:645
  2.1 3.9 %collective-permute-start = (f32[48,128]{1,0:T(8,128)S(1)}, f32[48,128]{1,0:T(8,128)S(1)}, u32[]{:S(2)}, u32[]{:S(2)}) collective-permute-start(f32[48,128]{1,0:T(8,128)S(1)} %pack_domain.1.own_ref.raw_ref), channel_id=1, source_target_pairs={{0,64},{1,65},{2,66},{3,67},{4,68},{5,69},{6,70},{7,71},{8,72},{9,... | collective-permute-start | bytes 73736 | tf_op jit(solution)/shard_map/ppermute | solution.py:36
  6.0 1.3 %collective-permute-start.1 = (f32[48,128]{1,0:T(8,128)S(1)}, f32[48,128]{1,0:T(8,128)S(1)}, u32[]{:S(2)}, u32[]{:S(2)}) collective-permute-start(f32[48,128]{1,0:T(8,128)S(1)} %pack_domain.1.own_ref.raw_ref), channel_id=1, source_target_pairs={{64,448},{65,449},{66,450},{67,451},{68,452},{69,453},{70,454},{71... | collective-permute-start | bytes 73736 | tf_op jit(solution)/shard_map/ppermute | solution.py:36
  7.3 10.4 %collective-permute-start.2 = (f32[48,128]{1,0:T(8,128)S(1)}, f32[48,128]{1,0:T(8,128)S(1)}, u32[]{:S(2)}, u32[]{:S(2)}) collective-permute-start(f32[48,128]{1,0:T(8,128)S(1)} %pack_domain.1.own_ref.raw_ref), channel_id=1, source_target_pairs={{0,448},{1,449},{2,450},{3,451},{4,452},{5,453},{6,454},{7,455},{8... | collective-permute-start | bytes 73736 | tf_op jit(solution)/shard_map/ppermute | solution.py:36
  17.7 0.7 %collective-permute-start.3 = (f32[48,128]{1,0:T(8,128)S(1)}, f32[48,128]{1,0:T(8,128)S(1)}, u32[]{:S(2)}, u32[]{:S(2)}) collective-permute-start(f32[48,128]{1,0:T(8,128)S(1)} %pack_domain.1.own_ref.raw_ref), channel_id=1, source_target_pairs={{256,320},{257,321},{258,322},{259,323},{260,324},{261,325},{262,3... | collective-permute-start | bytes 73736 | tf_op jit(solution)/shard_map/ppermute | solution.py:36
  18.4 1.0 %place_weights.1 = (bf16[64,128]{1,0:T(8,128)(2,1)S(1)}, bf16[192,128]{1,0:T(8,128)(2,1)S(1)}, bf16[320,128]{1,0:T(8,128)(2,1)S(1)}, bf16[16,128]{1,0:T(8,128)(2,1)S(1)}) custom-call(f32[8,128]{1,0:T(8,128)} %w_rad_hbm.1, bf16[7,128]{1,0:T(8,128)(2,1)} %emb_center_hbm.1, bf16[7,128]{1,0:T(8,128)(2,1)} %emb_neigh_hbm.1, bf16[192,128]{1,0:T(8,128)(2,1)} %bitcast.6, ...), custom_call_target="tpu_custom_call" | custom-call | bytes 4000000 | tf_op jit(solution)/shard_map/place_weights/pallas_call | solution.py:673
  19.4 0.0 collective-permute-done.first_ref
  19.5 0.0 collective-permute-done.1.border_ref
  19.5 0.0 collective-permute-done.2.cross_ref
  19.5 0.0 collective-permute-done.3.last_ref
  19.5 0.3 gather_sends.1
  19.8 4.4 %collective-permute-start.4 = (f32[48,128]{1,0:T(8,128)S(1)}, f32[48,128]{1,0:T(8,128)S(1)}, u32[]{:S(2)}, u32[]{:S(2)}) collective-permute-start(f32[48,128]{1,0:T(8,128)S(1)} %get-tuple-element.24), channel_id=1, source_target_pairs={{0,63},{1,2},{2,1},{3,4},{4,3},{5,6},{6,5},{7,8},{8,7},{9,10},{10,... | collective-permute-start | bytes 73736 | tf_op jit(solution)/shard_map/ppermute | solution.py:36
  24.2 6.8 %collective-permute-start.5 = (f32[48,128]{1,0:T(8,128)S(1)}, f32[48,128]{1,0:T(8,128)S(1)}, u32[]{:S(2)}, u32[]{:S(2)}) collective-permute-start(f32[48,128]{1,0:T(8,128)S(1)} %get-tuple-element.25), channel_id=1, source_target_pairs={{0,1},{1,0},{2,3},{3,2},{4,5},{5,4},{6,7},{7,6},{8,9},{9,8},{10,11... | collective-permute-start | bytes 73736 | tf_op jit(solution)/shard_map/ppermute | solution.py:36
  31.1 0.4 pair_columns.1
  31.4 0.0 collective-permute-done.4.refs_2_
  31.4 0.5 collective-permute-done.5.refs_3_
  31.9 5.8 %pair_terms.1 = (f32[16,128]{1,0:T(8,128)S(1)}, f32[8,128]{1,0:T(8,128)S(1)}, f32[8,128]{1,0:T(8,128)S(1)}, f32[24,128]{1,0:T(8,128)S(1)}, f32[24,128]{1,0:T(8,128)S(1)}) custom-call(f32[2,48,128]{2,1,0:T(8,128)S(1)} %get-tuple-element.22.raw_ref.refs_0_, f32[32,128]{1,0:T(8,128)S(1)} %get-tuple-element.23.refs_1_, ...), custom_call_target="tpu_custom_call" | custom-call | tf_op jit(solution)/shard_map/pair_terms/pallas_call | solution.py:728
  37.7 1.9 %collective-permute-start.6 = (f32[24,128]{1,0:T(8,128)S(1)}, f32[24,128]{1,0:T(8,128)S(1)}, u32[]{:S(2)}, u32[]{:S(2)}) collective-permute-start(f32[24,128]{1,0:T(8,128)S(1)} %get-tuple-element.32), channel_id=1, source_target_pairs={{0,63},{1,2},{2,1},{3,4},{4,3},{5,6},{6,5},{7,8},{8,7},{9,10},{10,... | collective-permute-start | bytes 36872 | tf_op jit(solution)/shard_map/ppermute | solution.py:36
  39.7 6.3 %collective-permute-start.7 = (f32[24,128]{1,0:T(8,128)S(1)}, f32[24,128]{1,0:T(8,128)S(1)}, u32[]{:S(2)}, u32[]{:S(2)}) collective-permute-start(f32[24,128]{1,0:T(8,128)S(1)} %get-tuple-element.33), channel_id=1, source_target_pairs={{0,1},{1,0},{2,3},{3,2},{4,5},{5,4},{6,7},{7,6},{8,9},{9,8},{10,11... | collective-permute-start | bytes 36872 | tf_op jit(solution)/shard_map/ppermute | solution.py:36
  46.0 0.0 collective-permute-done.6.up_ref
  46.0 0.8 %collective-permute-done.7.low_ref = f32[24,128]{1,0:T(8,128)S(1)} collective-permute-done((f32[24,128]{1,0:T(8,128)S(1)}, f32[24,128]{1,0:T(8,128)S(1)}, u32[]{:S(2)}, u32[]{:S(2)}) %collective-permute-start.7) | collective-permute-done | bytes 12320 | tf_op jit(solution)/shard_map/ppermute | solution.py:36
  46.8 0.7 %collective-permute-start.9 = (f32[24,128]{1,0:T(8,128)S(1)}, f32[24,128]{1,0:T(8,128)S(1)}, u32[]{:S(2)}, u32[]{:S(2)}) collective-permute-start(f32[24,128]{1,0:T(8,128)S(1)} %pad_maximum_fusion.1), channel_id=1, source_target_pairs={{64,128},{65,129},{66,130},{67,131},{68,132},{69,133},{70,134},{71... | collective-permute-start | bytes 36872 | tf_op jit(solution)/shard_map/ppermute | solution.py:36
  47.5 2.6 %collective-permute-start.8 = (f32[24,128]{1,0:T(8,128)S(1)}, f32[24,128]{1,0:T(8,128)S(1)}, u32[]{:S(2)}, u32[]{:S(2)}) collective-permute-start(f32[24,128]{1,0:T(8,128)S(1)} %pad_maximum_fusion), channel_id=1, source_target_pairs={{0,64},{1,65},{2,66},{3,67},{4,68},{5,69},{6,70},{7,71},{8,72},{9,... | collective-permute-start | bytes 36872 | tf_op jit(solution)/shard_map/ppermute | solution.py:36
  50.1 0.2 begin_terms.1
  50.3 0.0 collective-permute-done.9.inside_ref
  50.3 1.6 %collective-permute-done.8.beside_ref = f32[24,128]{1,0:T(8,128)S(1)} collective-permute-done((f32[24,128]{1,0:T(8,128)S(1)}, f32[24,128]{1,0:T(8,128)S(1)}, u32[]{:S(2)}, u32[]{:S(2)}) %collective-permute-start.8) | collective-permute-done | bytes 12320 | tf_op jit(solution)/shard_map/ppermute | solution.py:36
  51.9 0.8 %collect_terms.1 = (f32[3,512]{1,0:T(4,128)}, f32[1,512]{1,0:T(1,128)}) custom-call(f32[16,128]{1,0:T(8,128)S(1)} %get-tuple-element.34.total_ref, bf16[1536,128]{1,0:T(8,128)(2,1)S(1)} %get-tuple-element.35.hot_ref, f32[48,128]{1,0:T(8,128)S(1)} %pack_domain.1.own_ref.raw_ref, f32[24,128]{1,0:T(8,128)S(1)} %collective-permute-done.6.up_ref, ...), custom_call_target="tpu_custom_call" | custom-call | tf_op jit(solution)/shard_map/collect_terms/pallas_call | solution.py:756
  (4 shorter events, 0.0 us)
Async XLA Ops:
  2.1 17.4 %collective-permute-start = (f32[48,128]{1,0:T(8,128)S(1)}, f32[48,128]{1,0:T(8,128)S(1)}, u32[]{:S(2)}, u32[]{:S(2)}) collective-permute-start(f32[48,128]{1,0:T(8,128)S(1)} %pack_domain.1.own_ref.raw_ref), channel_id=1, source_target_pairs={{0,64},{1,65},{2,66},{3,67},{4,68},{5,69},{6,70},{7,71},{8,72},{9,... | collective-permute-start | bytes 73736 | tf_op jit(solution)/shard_map/ppermute | solution.py:36
  6.0 13.4 %collective-permute-start.1 = (f32[48,128]{1,0:T(8,128)S(1)}, f32[48,128]{1,0:T(8,128)S(1)}, u32[]{:S(2)}, u32[]{:S(2)}) collective-permute-start(f32[48,128]{1,0:T(8,128)S(1)} %pack_domain.1.own_ref.raw_ref), channel_id=1, source_target_pairs={{64,448},{65,449},{66,450},{67,451},{68,452},{69,453},{70,454},{71... | collective-permute-start | bytes 73736 | tf_op jit(solution)/shard_map/ppermute | solution.py:36
  7.3 12.1 %collective-permute-start.2 = (f32[48,128]{1,0:T(8,128)S(1)}, f32[48,128]{1,0:T(8,128)S(1)}, u32[]{:S(2)}, u32[]{:S(2)}) collective-permute-start(f32[48,128]{1,0:T(8,128)S(1)} %pack_domain.1.own_ref.raw_ref), channel_id=1, source_target_pairs={{0,448},{1,449},{2,450},{3,451},{4,452},{5,453},{6,454},{7,455},{8... | collective-permute-start | bytes 73736 | tf_op jit(solution)/shard_map/ppermute | solution.py:36
  17.7 1.8 %collective-permute-start.3 = (f32[48,128]{1,0:T(8,128)S(1)}, f32[48,128]{1,0:T(8,128)S(1)}, u32[]{:S(2)}, u32[]{:S(2)}) collective-permute-start(f32[48,128]{1,0:T(8,128)S(1)} %pack_domain.1.own_ref.raw_ref), channel_id=1, source_target_pairs={{256,320},{257,321},{258,322},{259,323},{260,324},{261,325},{262,3... | collective-permute-start | bytes 73736 | tf_op jit(solution)/shard_map/ppermute | solution.py:36
  19.8 11.6 %collective-permute-start.4 = (f32[48,128]{1,0:T(8,128)S(1)}, f32[48,128]{1,0:T(8,128)S(1)}, u32[]{:S(2)}, u32[]{:S(2)}) collective-permute-start(f32[48,128]{1,0:T(8,128)S(1)} %get-tuple-element.24), channel_id=1, source_target_pairs={{0,63},{1,2},{2,1},{3,4},{4,3},{5,6},{6,5},{7,8},{8,7},{9,10},{10,... | collective-permute-start | bytes 73736 | tf_op jit(solution)/shard_map/ppermute | solution.py:36
  24.2 7.7 %collective-permute-start.5 = (f32[48,128]{1,0:T(8,128)S(1)}, f32[48,128]{1,0:T(8,128)S(1)}, u32[]{:S(2)}, u32[]{:S(2)}) collective-permute-start(f32[48,128]{1,0:T(8,128)S(1)} %get-tuple-element.25), channel_id=1, source_target_pairs={{0,1},{1,0},{2,3},{3,2},{4,5},{5,4},{6,7},{7,6},{8,9},{9,8},{10,11... | collective-permute-start | bytes 73736 | tf_op jit(solution)/shard_map/ppermute | solution.py:36
  37.7 8.2 %collective-permute-start.6 = (f32[24,128]{1,0:T(8,128)S(1)}, f32[24,128]{1,0:T(8,128)S(1)}, u32[]{:S(2)}, u32[]{:S(2)}) collective-permute-start(f32[24,128]{1,0:T(8,128)S(1)} %get-tuple-element.32), channel_id=1, source_target_pairs={{0,63},{1,2},{2,1},{3,4},{4,3},{5,6},{6,5},{7,8},{8,7},{9,10},{10,... | collective-permute-start | bytes 36872 | tf_op jit(solution)/shard_map/ppermute | solution.py:36
  39.7 7.1 %collective-permute-start.7 = (f32[24,128]{1,0:T(8,128)S(1)}, f32[24,128]{1,0:T(8,128)S(1)}, u32[]{:S(2)}, u32[]{:S(2)}) collective-permute-start(f32[24,128]{1,0:T(8,128)S(1)} %get-tuple-element.33), channel_id=1, source_target_pairs={{0,1},{1,0},{2,3},{3,2},{4,5},{5,4},{6,7},{7,6},{8,9},{9,8},{10,11... | collective-permute-start | bytes 36872 | tf_op jit(solution)/shard_map/ppermute | solution.py:36
  46.8 3.5 %collective-permute-start.9 = (f32[24,128]{1,0:T(8,128)S(1)}, f32[24,128]{1,0:T(8,128)S(1)}, u32[]{:S(2)}, u32[]{:S(2)}) collective-permute-start(f32[24,128]{1,0:T(8,128)S(1)} %pad_maximum_fusion.1), channel_id=1, source_target_pairs={{64,128},{65,129},{66,130},{67,131},{68,132},{69,133},{70,134},{71... | collective-permute-start | bytes 36872 | tf_op jit(solution)/shard_map/ppermute | solution.py:36
  47.5 4.4 %collective-permute-start.8 = (f32[24,128]{1,0:T(8,128)S(1)}, f32[24,128]{1,0:T(8,128)S(1)}, u32[]{:S(2)}, u32[]{:S(2)}) collective-permute-start(f32[24,128]{1,0:T(8,128)S(1)} %pad_maximum_fusion), channel_id=1, source_target_pairs={{0,64},{1,65},{2,66},{3,67},{4,68},{5,69},{6,70},{7,71},{8,72},{9,... | collective-permute-start | bytes 36872 | tf_op jit(solution)/shard_map/ppermute | solution.py:36

commit v9 on v8

--- a/solution.py
+++ b/solution.py
@@ -161,31 +161,21 @@
 
 def weights_kernel(
     w_rad_hbm,
-    emb_center_hbm,
-    emb_neigh_hbm,
     w_env_hbm,
     w_lat_hbm,
-    w_out_hbm,
+    emb_center_ref,
+    emb_neigh_ref,
+    w_out_in_ref,
     front_ref,
     w_env_ref,
     w_lat_ref,
     w_out_ref,
     w_rad,
-    emb_center,
-    emb_neigh,
-    w_out,
     sems,
 ):
     fetched = []
     for j, (src, dst) in enumerate(
-        (
-            (w_rad_hbm, w_rad),
-            (emb_center_hbm, emb_center),
-            (emb_neigh_hbm, emb_neigh),
-            (w_env_hbm, w_env_ref),
-            (w_lat_hbm, w_lat_ref),
-            (w_out_hbm, w_out),
-        )
+        ((w_rad_hbm, w_rad), (w_env_hbm, w_env_ref), (w_lat_hbm, w_lat_ref))
     ):
         copy = pltpu.make_async_copy(src, dst, sems.at[j])
         copy.start()
@@ -196,10 +186,10 @@
     w1, w2, w3 = parts(w_rad[...], 3)
     none = jnp.zeros((1, lat), BF16)
     front_ref[...] = jnp.concatenate(
-        [w1, w2, w1, w3, w2, w1, emb_center[...], none, emb_neigh[...], none], 0
+        [w1, w2, w1, w3, w2, w1, emb_center_ref[...], none, emb_neigh_ref[...], none], 0
     )
     w_lat_ref[lat:] = w_lat_ref[lat:] * jnp.full((), 2.0, BF16)
-    w_out_ref[...] = jnp.broadcast_to(w_out[...], (16, lat))
+    w_out_ref[...] = jnp.broadcast_to(w_out_in_ref[...], (16, lat))
 
 
 def tile_at(extra, side):
@@ -338,10 +328,9 @@
     even_n = lax.axis_index("inner") % 2 == 0
     odd = lax.axis_index("outer") % 2 == 1
     front = front_ref[...]
-    w1, w2 = front[0:8], front[8:16]
     w_env = w_env_ref[...]
     w_lat = w_lat_ref[...]
-    w_out = w_out_ref[0:8].astype(F32).T[:, 0:1]
+    w_out = w_out_ref[...].astype(F32).T[:, 0:1]
 
     def as_row(tile):
         return jnp.concatenate([tile[i : i + 1] for i in range(chunks)], 1)
@@ -484,7 +473,7 @@
     d_scaled = raw_energy + jnp.sum(d_weight * raw, axis=0, keepdims=True)
     d_latent = d_latent + scaled * dot_rows(w_env, d_weight.astype(BF16))
     d_pre = (d_latent * slope).astype(BF16)
-    d_basis = dot(jnp.concatenate([w1, w2], 0), d_pre)
+    d_basis = dot(front_ref[0:16], d_pre)
     d_basis = d_basis[0:8] + d_basis[8:16]
 
     along = jnp.sum(d_basis * sine, axis=0, keepdims=True)
@@ -678,22 +667,20 @@
             jax.ShapeDtypeStruct(w_lat.shape, BF16),
             jax.ShapeDtypeStruct((16, lat), BF16),
         ],
-        in_specs=[pl.BlockSpec(memory_space=pltpu.HBM)] * 6,
-        scratch_shapes=[
-            pltpu.VMEM(w_rad.shape, F32),
-            pltpu.VMEM(emb_center.shape, BF16),
-            pltpu.VMEM(emb_neigh.shape, BF16),
-            pltpu.VMEM((1, lat), BF16),
-            pltpu.SemaphoreType.DMA((6,)),
-        ],
+        in_specs=[pl.BlockSpec(memory_space=pltpu.HBM)] * 3
+        + [pl.BlockSpec(memory_space=pltpu.VMEM)] * 3,
+        scratch_shapes=[pltpu.VMEM(w_rad.shape, F32), pltpu.SemaphoreType.DMA((3,))],
         compiler_params=SMALL,
         cost_estimate=pl.CostEstimate(flops=0, bytes_accessed=4_000_000, transcendentals=0),
         name="place_weights",
     )(
         *(
             pltpu.with_memory_space_constraint(value, pltpu.HBM)
-            for value in (w_rad, emb_center, emb_neigh, w_env.T, w_lat, w_out.reshape(1, -1))
-        )
+            for value in (w_rad, w_env.T, w_lat)
+        ),
+        emb_center,
+        emb_neigh,
+        w_out.reshape(1, -1),
     )
     count = lax.axis_size("outer")
     half = count // 2

time: 53.2 us -> 53.5 us (level)
  local copies, waits for them, and re-layouts: 0.01 us -> 0.65 us
  waiting for transfers between devices: 2.83 us -> 2.28 us
    unnamed x0 -> x6, local copies, waits for them, and re-layouts: none -> 0.64 us
    ppermute x10, waiting for transfers between devices: 2.83 us -> 2.28 us  [permute(): return lax.ppermute(block, AXES, route)]
where the time goes in v9:
time: 53.5 us; the launch traced here: 52.7 us
  starting transfers between devices  39 us (73%)
  Pallas kernels  9.3 us (17%)
  waiting for transfers between devices  2.28 us (4%)
  between operations  1.51 us (3%)
  local copies, waits for them, and re-layouts  0.65 us (1%)
    ppermute x10, starting transfers between devices, permute(): return lax.ppermute(block, AXES, route)  39 us
    pallas_call x1, Pallas kernels, on_device(): pl.pallas_call(lambda *refs: pair_kernel(feat, pair_len, *refs), out_shap...  5.84 us
    ppermute x10, waiting for transfers between devices, permute(): return lax.ppermute(block, AXES, route)  2.28 us
  transfers between devices with their start and end apart: 10, of which 3 were waited for; matrix products, arithmetic and copies ran while one was open for 0% of the time, Pallas kernels for 3%

profile of v9, /device:TPU:1, one launch (start us, length us, event | category | flops | bytes accessed | tf_op | source)
XLA Modules:
  0.0 52.7 jit_solution(68266659645697248)
XLA Ops:
  1.3 0.0 copy-start.1
  1.3 0.8 %pack_domain.1.own_ref.raw_ref = f32[48,128]{1,0:T(8,128)S(1)} custom-call(f32[3,512]{1,0:T(4,128)} %pos_hbm.1, s32[1,512]{1,0:T(1,128)} %bitcast.10, s32[8,176]{1,0:T(8,128)} %lists_hbm.1, s32[6,128]{1,0:T(8,128)} %bitcast.8, s32[6,128]{1,0:T(8,128)} %bitcast.9, s32[1]{0:T(128)S(6)} %copy.14.live_ref), custom_call_target="tpu_custom_call" | custom-call | tf_op jit(solution)/shard_map/pack_domain/pallas_call | solution.py:634
  2.1 0.0 copy-start
  2.1 3.9 %collective-permute-start = (f32[48,128]{1,0:T(8,128)S(1)}, f32[48,128]{1,0:T(8,128)S(1)}, u32[]{:S(2)}, u32[]{:S(2)}) collective-permute-start(f32[48,128]{1,0:T(8,128)S(1)} %pack_domain.1.own_ref.raw_ref), channel_id=1, source_target_pairs={{0,64},{1,65},{2,66},{3,67},{4,68},{5,69},{6,70},{7,71},{8,72},{9,... | collective-permute-start | bytes 73736 | tf_op jit(solution)/shard_map/ppermute | solution.py:36
  6.1 1.3 %collective-permute-start.1 = (f32[48,128]{1,0:T(8,128)S(1)}, f32[48,128]{1,0:T(8,128)S(1)}, u32[]{:S(2)}, u32[]{:S(2)}) collective-permute-start(f32[48,128]{1,0:T(8,128)S(1)} %pack_domain.1.own_ref.raw_ref), channel_id=1, source_target_pairs={{64,448},{65,449},{66,450},{67,451},{68,452},{69,453},{70,454},{71... | collective-permute-start | bytes 73736 | tf_op jit(solution)/shard_map/ppermute | solution.py:36
  7.4 10.4 %collective-permute-start.2 = (f32[48,128]{1,0:T(8,128)S(1)}, f32[48,128]{1,0:T(8,128)S(1)}, u32[]{:S(2)}, u32[]{:S(2)}) collective-permute-start(f32[48,128]{1,0:T(8,128)S(1)} %pack_domain.1.own_ref.raw_ref), channel_id=1, source_target_pairs={{0,448},{1,449},{2,450},{3,451},{4,452},{5,453},{6,454},{7,455},{8... | collective-permute-start | bytes 73736 | tf_op jit(solution)/shard_map/ppermute | solution.py:36
  17.8 0.7 %collective-permute-start.3 = (f32[48,128]{1,0:T(8,128)S(1)}, f32[48,128]{1,0:T(8,128)S(1)}, u32[]{:S(2)}, u32[]{:S(2)}) collective-permute-start(f32[48,128]{1,0:T(8,128)S(1)} %pack_domain.1.own_ref.raw_ref), channel_id=1, source_target_pairs={{256,320},{257,321},{258,322},{259,323},{260,324},{261,325},{262,3... | collective-permute-start | bytes 73736 | tf_op jit(solution)/shard_map/ppermute | solution.py:36
  18.4 0.0 copy-start.2
  18.4 0.0 copy-done.1
  18.4 0.0 copy-done
  18.5 0.6 %copy-done.2 = bf16[128]{0:T(256)(128)(2,1)S(1)} copy-done((bf16[128]{0:T(256)(128)(2,1)S(1)}, bf16[128]{0:T(256)(128)(2,1)}, u32[]{:S(2)}) %copy-start.2) | copy-done | bytes 280
  19.1 1.0 %place_weights.1 = (bf16[64,128]{1,0:T(8,128)(2,1)S(1)}, bf16[192,128]{1,0:T(8,128)(2,1)S(1)}, bf16[320,128]{1,0:T(8,128)(2,1)S(1)}, bf16[16,128]{1,0:T(8,128)(2,1)S(1)}) custom-call(f32[8,128]{1,0:T(8,128)} %w_rad_hbm.1, bf16[192,128]{1,0:T(8,128)(2,1)} %bitcast.7, bf16[320,128]{1,0:T(8,128)(2,1)} %w_lat_hbm.1, bf16[7,128]{1,0:T(8,128)(2,1)S(1)} %copy-done, ...), custom_call_target="tpu_custom_call" | custom-call | bytes 4000000 | tf_op jit(solution)/shard_map/place_weights/pallas_call | solution.py:662
  20.1 0.0 collective-permute-done.first_ref
  20.1 0.0 collective-permute-done.1.border_ref
  20.1 0.0 collective-permute-done.2.cross_ref
  20.1 0.0 collective-permute-done.3.last_ref
  20.1 0.3 gather_sends.1
  20.4 3.9 %collective-permute-start.4 = (f32[48,128]{1,0:T(8,128)S(1)}, f32[48,128]{1,0:T(8,128)S(1)}, u32[]{:S(2)}, u32[]{:S(2)}) collective-permute-start(f32[48,128]{1,0:T(8,128)S(1)} %get-tuple-element.24), channel_id=1, source_target_pairs={{0,63},{1,2},{2,1},{3,4},{4,3},{5,6},{6,5},{7,8},{8,7},{9,10},{10,... | collective-permute-start | bytes 73736 | tf_op jit(solution)/shard_map/ppermute | solution.py:36
  24.4 6.7 %collective-permute-start.5 = (f32[48,128]{1,0:T(8,128)S(1)}, f32[48,128]{1,0:T(8,128)S(1)}, u32[]{:S(2)}, u32[]{:S(2)}) collective-permute-start(f32[48,128]{1,0:T(8,128)S(1)} %get-tuple-element.25), channel_id=1, source_target_pairs={{0,1},{1,0},{2,3},{3,2},{4,5},{5,4},{6,7},{7,6},{8,9},{9,8},{10,11... | collective-permute-start | bytes 73736 | tf_op jit(solution)/shard_map/ppermute | solution.py:36
  31.1 0.4 pair_columns.1
  31.5 0.0 collective-permute-done.4.refs_2_
  31.5 0.5 collective-permute-done.5.refs_3_
  31.9 5.8 %pair_terms.1 = (f32[16,128]{1,0:T(8,128)S(1)}, f32[8,128]{1,0:T(8,128)S(1)}, f32[8,128]{1,0:T(8,128)S(1)}, f32[24,128]{1,0:T(8,128)S(1)}, f32[24,128]{1,0:T(8,128)S(1)}) custom-call(f32[2,48,128]{2,1,0:T(8,128)S(1)} %get-tuple-element.22.raw_ref.refs_0_, f32[32,128]{1,0:T(8,128)S(1)} %get-tuple-element.23.refs_1_, ...), custom_call_target="tpu_custom_call" | custom-call | tf_op jit(solution)/shard_map/pair_terms/pallas_call | solution.py:715
  37.8 1.9 %collective-permute-start.6 = (f32[24,128]{1,0:T(8,128)S(1)}, f32[24,128]{1,0:T(8,128)S(1)}, u32[]{:S(2)}, u32[]{:S(2)}) collective-permute-start(f32[24,128]{1,0:T(8,128)S(1)} %get-tuple-element.32), channel_id=1, source_target_pairs={{0,63},{1,2},{2,1},{3,4},{4,3},{5,6},{6,5},{7,8},{8,7},{9,10},{10,... | collective-permute-start | bytes 36872 | tf_op jit(solution)/shard_map/ppermute | solution.py:36
  39.7 6.3 %collective-permute-start.7 = (f32[24,128]{1,0:T(8,128)S(1)}, f32[24,128]{1,0:T(8,128)S(1)}, u32[]{:S(2)}, u32[]{:S(2)}) collective-permute-start(f32[24,128]{1,0:T(8,128)S(1)} %get-tuple-element.33), channel_id=1, source_target_pairs={{0,1},{1,0},{2,3},{3,2},{4,5},{5,4},{6,7},{7,6},{8,9},{9,8},{10,11... | collective-permute-start | bytes 36872 | tf_op jit(solution)/shard_map/ppermute | solution.py:36
  46.0 0.0 collective-permute-done.6.up_ref
  46.0 0.8 %collective-permute-done.7.low_ref = f32[24,128]{1,0:T(8,128)S(1)} collective-permute-done((f32[24,128]{1,0:T(8,128)S(1)}, f32[24,128]{1,0:T(8,128)S(1)}, u32[]{:S(2)}, u32[]{:S(2)}) %collective-permute-start.7) | collective-permute-done | bytes 12320 | tf_op jit(solution)/shard_map/ppermute | solution.py:36
  46.8 0.7 %collective-permute-start.9 = (f32[24,128]{1,0:T(8,128)S(1)}, f32[24,128]{1,0:T(8,128)S(1)}, u32[]{:S(2)}, u32[]{:S(2)}) collective-permute-start(f32[24,128]{1,0:T(8,128)S(1)} %pad_maximum_fusion.1), channel_id=1, source_target_pairs={{64,128},{65,129},{66,130},{67,131},{68,132},{69,133},{70,134},{71... | collective-permute-start | bytes 36872 | tf_op jit(solution)/shard_map/ppermute | solution.py:36
  47.5 3.2 %collective-permute-start.8 = (f32[24,128]{1,0:T(8,128)S(1)}, f32[24,128]{1,0:T(8,128)S(1)}, u32[]{:S(2)}, u32[]{:S(2)}) collective-permute-start(f32[24,128]{1,0:T(8,128)S(1)} %pad_maximum_fusion), channel_id=1, source_target_pairs={{0,64},{1,65},{2,66},{3,67},{4,68},{5,69},{6,70},{7,71},{8,72},{9,... | collective-permute-start | bytes 36872 | tf_op jit(solution)/shard_map/ppermute | solution.py:36
  50.7 0.2 begin_terms.1
  50.9 0.0 collective-permute-done.9.inside_ref
  50.9 1.0 %collective-permute-done.8.beside_ref = f32[24,128]{1,0:T(8,128)S(1)} collective-permute-done((f32[24,128]{1,0:T(8,128)S(1)}, f32[24,128]{1,0:T(8,128)S(1)}, u32[]{:S(2)}, u32[]{:S(2)}) %collective-permute-start.8) | collective-permute-done | bytes 12320 | tf_op jit(solution)/shard_map/ppermute | solution.py:36
  52.0 0.8 %collect_terms.1 = (f32[3,512]{1,0:T(4,128)}, f32[1,512]{1,0:T(1,128)}) custom-call(f32[16,128]{1,0:T(8,128)S(1)} %get-tuple-element.34.total_ref, bf16[1536,128]{1,0:T(8,128)(2,1)S(1)} %get-tuple-element.35.hot_ref, f32[48,128]{1,0:T(8,128)S(1)} %pack_domain.1.own_ref.raw_ref, f32[24,128]{1,0:T(8,128)S(1)} %collective-permute-done.6.up_ref, ...), custom_call_target="tpu_custom_call" | custom-call | tf_op jit(solution)/shard_map/collect_terms/pallas_call | solution.py:743
  (4 shorter events, 0.0 us)
Async XLA Ops:
  1.3 17.2 %copy-start.1 = (bf16[7,128]{1,0:T(8,128)(2,1)S(1)}, bf16[7,128]{1,0:T(8,128)(2,1)}, u32[]{:S(2)}) copy-start(bf16[7,128]{1,0:T(8,128)(2,1)} %emb_neigh_ref.1) | copy-start | bytes 5380
  2.1 16.3 %copy-start = (bf16[7,128]{1,0:T(8,128)(2,1)S(1)}, bf16[7,128]{1,0:T(8,128)(2,1)}, u32[]{:S(2)}) copy-start(bf16[7,128]{1,0:T(8,128)(2,1)} %emb_center_ref.1) | copy-start | bytes 5380
  2.1 17.9 %collective-permute-start = (f32[48,128]{1,0:T(8,128)S(1)}, f32[48,128]{1,0:T(8,128)S(1)}, u32[]{:S(2)}, u32[]{:S(2)}) collective-permute-start(f32[48,128]{1,0:T(8,128)S(1)} %pack_domain.1.own_ref.raw_ref), channel_id=1, source_target_pairs={{0,64},{1,65},{2,66},{3,67},{4,68},{5,69},{6,70},{7,71},{8,72},{9,... | collective-permute-start | bytes 73736 | tf_op jit(solution)/shard_map/ppermute | solution.py:36
  6.1 14.0 %collective-permute-start.1 = (f32[48,128]{1,0:T(8,128)S(1)}, f32[48,128]{1,0:T(8,128)S(1)}, u32[]{:S(2)}, u32[]{:S(2)}) collective-permute-start(f32[48,128]{1,0:T(8,128)S(1)} %pack_domain.1.own_ref.raw_ref), channel_id=1, source_target_pairs={{64,448},{65,449},{66,450},{67,451},{68,452},{69,453},{70,454},{71... | collective-permute-start | bytes 73736 | tf_op jit(solution)/shard_map/ppermute | solution.py:36
  7.4 12.7 %collective-permute-start.2 = (f32[48,128]{1,0:T(8,128)S(1)}, f32[48,128]{1,0:T(8,128)S(1)}, u32[]{:S(2)}, u32[]{:S(2)}) collective-permute-start(f32[48,128]{1,0:T(8,128)S(1)} %pack_domain.1.own_ref.raw_ref), channel_id=1, source_target_pairs={{0,448},{1,449},{2,450},{3,451},{4,452},{5,453},{6,454},{7,455},{8... | collective-permute-start | bytes 73736 | tf_op jit(solution)/shard_map/ppermute | solution.py:36
  17.8 2.3 %collective-permute-start.3 = (f32[48,128]{1,0:T(8,128)S(1)}, f32[48,128]{1,0:T(8,128)S(1)}, u32[]{:S(2)}, u32[]{:S(2)}) collective-permute-start(f32[48,128]{1,0:T(8,128)S(1)} %pack_domain.1.own_ref.raw_ref), channel_id=1, source_target_pairs={{256,320},{257,321},{258,322},{259,323},{260,324},{261,325},{262,3... | collective-permute-start | bytes 73736 | tf_op jit(solution)/shard_map/ppermute | solution.py:36
  18.4 0.7 %copy-start.2 = (bf16[128]{0:T(256)(128)(2,1)S(1)}, bf16[128]{0:T(256)(128)(2,1)}, u32[]{:S(2)}) copy-start(bf16[128]{0:T(256)(128)(2,1)} %param.23) | copy-start | bytes 772
  20.4 11.1 %collective-permute-start.4 = (f32[48,128]{1,0:T(8,128)S(1)}, f32[48,128]{1,0:T(8,128)S(1)}, u32[]{:S(2)}, u32[]{:S(2)}) collective-permute-start(f32[48,128]{1,0:T(8,128)S(1)} %get-tuple-element.24), channel_id=1, source_target_pairs={{0,63},{1,2},{2,1},{3,4},{4,3},{5,6},{6,5},{7,8},{8,7},{9,10},{10,... | collective-permute-start | bytes 73736 | tf_op jit(solution)/shard_map/ppermute | solution.py:36
  24.4 7.6 %collective-permute-start.5 = (f32[48,128]{1,0:T(8,128)S(1)}, f32[48,128]{1,0:T(8,128)S(1)}, u32[]{:S(2)}, u32[]{:S(2)}) collective-permute-start(f32[48,128]{1,0:T(8,128)S(1)} %get-tuple-element.25), channel_id=1, source_target_pairs={{0,1},{1,0},{2,3},{3,2},{4,5},{5,4},{6,7},{7,6},{8,9},{9,8},{10,11... | collective-permute-start | bytes 73736 | tf_op jit(solution)/shard_map/ppermute | solution.py:36
  37.8 8.2 %collective-permute-start.6 = (f32[24,128]{1,0:T(8,128)S(1)}, f32[24,128]{1,0:T(8,128)S(1)}, u32[]{:S(2)}, u32[]{:S(2)}) collective-permute-start(f32[24,128]{1,0:T(8,128)S(1)} %get-tuple-element.32), channel_id=1, source_target_pairs={{0,63},{1,2},{2,1},{3,4},{4,3},{5,6},{6,5},{7,8},{8,7},{9,10},{10,... | collective-permute-start | bytes 36872 | tf_op jit(solution)/shard_map/ppermute | solution.py:36
  39.7 7.1 %collective-permute-start.7 = (f32[24,128]{1,0:T(8,128)S(1)}, f32[24,128]{1,0:T(8,128)S(1)}, u32[]{:S(2)}, u32[]{:S(2)}) collective-permute-start(f32[24,128]{1,0:T(8,128)S(1)} %get-tuple-element.33), channel_id=1, source_target_pairs={{0,1},{1,0},{2,3},{3,2},{4,5},{5,4},{6,7},{7,6},{8,9},{9,8},{10,11... | collective-permute-start | bytes 36872 | tf_op jit(solution)/shard_map/ppermute | solution.py:36
  46.8 4.1 %collective-permute-start.9 = (f32[24,128]{1,0:T(8,128)S(1)}, f32[24,128]{1,0:T(8,128)S(1)}, u32[]{:S(2)}, u32[]{:S(2)}) collective-permute-start(f32[24,128]{1,0:T(8,128)S(1)} %pad_maximum_fusion.1), channel_id=1, source_target_pairs={{64,128},{65,129},{66,130},{67,131},{68,132},{69,133},{70,134},{71... | collective-permute-start | bytes 36872 | tf_op jit(solution)/shard_map/ppermute | solution.py:36
  47.5 4.4 %collective-permute-start.8 = (f32[24,128]{1,0:T(8,128)S(1)}, f32[24,128]{1,0:T(8,128)S(1)}, u32[]{:S(2)}, u32[]{:S(2)}) collective-permute-start(f32[24,128]{1,0:T(8,128)S(1)} %pad_maximum_fusion), channel_id=1, source_target_pairs={{0,64},{1,65},{2,66},{3,67},{4,68},{5,69},{6,70},{7,71},{8,72},{9,... | collective-permute-start | bytes 36872 | tf_op jit(solution)/shard_map/ppermute | solution.py:36

commit v10 on v9

--- a/solution.py
+++ b/solution.py
@@ -196,45 +196,65 @@
     return 8 * (3 * extra + 1 - side)
 
 
+def tiles_of(raw, sides):
+    odd = lax.axis_index("outer") % 2 == 1
+    rows = lax.broadcasted_iota(jnp.int32, (8, LANES), 0)
+    halves = [raw[LISTS + 8 * i : LISTS + 8 * i + 8].astype(jnp.int32) for i in range(2)]
+    names, ids = [], []
+    for side in sides:
+        if side == 0:
+            picked = [half[3:5] for half in halves]
+            names += [(0, -1), (0, 1)]
+        else:
+            upper = odd if side > 0 else jnp.logical_not(odd)
+            picked = [jnp.where(upper, half[5:8], half[0:3]) for half in halves]
+            names += [(side, dy) for dy in (-1, 0, 1)]
+        for i in range(picked[0].shape[0]):
+            ids += [picked[0][i : i + 1], picked[1][i : i + 1]]
+    ids = jnp.concatenate(ids, 1)
+    taken = gather(raw[TABLE : TABLE + 16], onehot_low(ids & 127), ids >> 7)
+    tiles = {}
+    for j, name in enumerate(names):
+        at = 2 * j * LANES
+        tiles[name] = jnp.where(
+            rows < 4, taken[:, at : at + LANES], taken[:, at + LANES : at + 2 * LANES]
+        )
+    return tiles
+
+
+def names_of(sides):
+    return [(side, dy) for side in sides for dy in ((-1, 1) if side == 0 else (-1, 0, 1))]
+
+
+def early_kernel(own_ref, first_ref, border_ref, _, early_ref):
+    at = 0
+    for raw, sides in ((own_ref[...], (1, 0)), (first_ref[...], (1,)), (border_ref[...], (-1,))):
+        tiles = tiles_of(raw, sides)
+        for name in names_of(sides):
+            early_ref[at : at + 8] = tiles[name]
+            at += 8
+
+
 def sends_kernel(
-    own_ref, first_ref, border_ref, cross_ref, last_ref, _, far_ref, near_ref, mid_ref, raw_ref
+    early_ref, own_ref, cross_ref, last_ref, far_ref, near_ref, mid_ref, raw_ref
 ):
     even_n = lax.axis_index("inner") % 2 == 0
-    odd = lax.axis_index("outer") % 2 == 1
+    cross = cross_ref[...]
+    raw_ref[0] = own_ref[...]
+    raw_ref[1] = cross
+    made = []
+    at = 0
+    for sides in ((1, 0), (1,), (-1,)):
+        tiles = {}
+        for name in names_of(sides):
+            tiles[name] = early_ref[at : at + 8]
+            at += 8
+        made.append(tiles)
+    by_own, by_beside, by_border = made
+    by_cross = tiles_of(cross, (0, -1))
+    by_last = tiles_of(last_ref[...], (1,))
     low_half, _ = row_kind()
-    rows = lax.broadcasted_iota(jnp.int32, (8, LANES), 0)
-    own, cross = own_ref[...], cross_ref[...]
-    beside = jnp.where(low_half, first_ref[...], last_ref[...])
-    raw_ref[0] = own
-    raw_ref[1] = cross
-
-    def tiles_of(raw, sides):
-        halves = [raw[LISTS + 8 * i : LISTS + 8 * i + 8].astype(jnp.int32) for i in range(2)]
-        names, ids = [], []
-        for side in sides:
-            if side == 0:
-                picked = [half[3:5] for half in halves]
-                names += [(0, -1), (0, 1)]
-            else:
-                upper = odd if side > 0 else jnp.logical_not(odd)
-                picked = [jnp.where(upper, half[5:8], half[0:3]) for half in halves]
-                names += [(side, dy) for dy in (-1, 0, 1)]
-            for i in range(picked[0].shape[0]):
-                ids += [picked[0][i : i + 1], picked[1][i : i + 1]]
-        ids = jnp.concatenate(ids, 1)
-        taken = gather(raw[TABLE : TABLE + 16], onehot_low(ids & 127), ids >> 7)
-        tiles = {}
-        for j, name in enumerate(names):
-            at = 2 * j * LANES
-            tiles[name] = jnp.where(
-                rows < 4, taken[:, at : at + LANES], taken[:, at + LANES : at + 2 * LANES]
-            )
-        return tiles
-
-    by_own = tiles_of(own, (1, 0))
-    by_cross = tiles_of(cross, (0, -1))
-    by_beside = tiles_of(beside, (1,))
-    by_border = tiles_of(border_ref[...], (-1,))
+    by_beside = {n: jnp.where(low_half, by_beside[n], by_last[n]) for n in by_last}
     sources = ({1: by_beside, 0: by_own, -1: by_cross}, {1: by_own, 0: by_cross, -1: by_border})
     for extra in range(2):
         for side in (1, 0, -1):
@@ -689,6 +709,12 @@
     border = copy_rows(packed, {1: high, low - 1: half, half + 1: low, high - 1: 0})
     cross = swap_outer(packed, 1, range(count))
     last = swap_outer(packed, 0, range(half, count))
+    early = pl.pallas_call(
+        early_kernel,
+        out_shape=rows(88),
+        compiler_params=SMALL,
+        name="gather_early",
+    )(packed, first, border, weights[3])
     far, near, mid, raw = pl.pallas_call(
         sends_kernel,
         out_shape=[
@@ -699,7 +725,7 @@
         ],
         compiler_params=SMALL,
         name="gather_sends",
-    )(packed, first, border, cross, last, weights[3])
+    )(early, packed, cross, last)
     up = swap_inner(far, 1)
     low = swap_inner(near, 0)
     down, hot_t = pl.pallas_call(

time: 53.5 us -> 53.7 us (level)
  no operation moved by 1% of the time
where the time goes in v10:
time: 53.7 us; the launch traced here: 52.7 us
  starting transfers between devices  39 us (73%)
  Pallas kernels  9.48 us (18%)
  waiting for transfers between devices  2.09 us (4%)
  between operations  1.52 us (3%)
  local copies, waits for them, and re-layouts  0.65 us (1%)
    ppermute x10, starting transfers between devices, permute(): return lax.ppermute(block, AXES, route)  39 us
    pallas_call x1, Pallas kernels, on_device(): pl.pallas_call(lambda *refs: pair_kernel(feat, pair_len, *refs), out_shap...  5.84 us
    ppermute x10, waiting for transfers between devices, permute(): return lax.ppermute(block, AXES, route)  2.09 us
  transfers between devices with their start and end apart: 10, of which 3 were waited for; matrix products, arithmetic and copies ran while one was open for 0% of the time, Pallas kernels for 3%

profile of v10, /device:TPU:1, one launch (start us, length us, event | category | flops | bytes accessed | tf_op | source)
XLA Modules:
  0.0 52.7 jit_solution(11937090081003327885)
XLA Ops:
  1.3 0.0 copy-start.1
  1.3 0.8 %pack_domain.1.own_ref.raw_ref = f32[48,128]{1,0:T(8,128)S(1)} custom-call(f32[3,512]{1,0:T(4,128)} %pos_hbm.1, s32[1,512]{1,0:T(1,128)} %bitcast.10, s32[8,176]{1,0:T(8,128)} %lists_hbm.1, s32[6,128]{1,0:T(8,128)} %bitcast.8, s32[6,128]{1,0:T(8,128)} %bitcast.9, s32[1]{0:T(128)S(6)} %copy.14.live_ref), custom_call_target="tpu_custom_call" | custom-call | tf_op jit(solution)/shard_map/pack_domain/pallas_call | solution.py:654
  2.1 0.0 copy-start
  2.1 3.9 %collective-permute-start = (f32[48,128]{1,0:T(8,128)S(1)}, f32[48,128]{1,0:T(8,128)S(1)}, u32[]{:S(2)}, u32[]{:S(2)}) collective-permute-start(f32[48,128]{1,0:T(8,128)S(1)} %pack_domain.1.own_ref.raw_ref), channel_id=1, source_target_pairs={{0,64},{1,65},{2,66},{3,67},{4,68},{5,69},{6,70},{7,71},{8,72},{9,... | collective-permute-start | bytes 73736 | tf_op jit(solution)/shard_map/ppermute | solution.py:36
  6.1 1.3 %collective-permute-start.1 = (f32[48,128]{1,0:T(8,128)S(1)}, f32[48,128]{1,0:T(8,128)S(1)}, u32[]{:S(2)}, u32[]{:S(2)}) collective-permute-start(f32[48,128]{1,0:T(8,128)S(1)} %pack_domain.1.own_ref.raw_ref), channel_id=1, source_target_pairs={{64,448},{65,449},{66,450},{67,451},{68,452},{69,453},{70,454},{71... | collective-permute-start | bytes 73736 | tf_op jit(solution)/shard_map/ppermute | solution.py:36
  7.4 10.4 %collective-permute-start.2 = (f32[48,128]{1,0:T(8,128)S(1)}, f32[48,128]{1,0:T(8,128)S(1)}, u32[]{:S(2)}, u32[]{:S(2)}) collective-permute-start(f32[48,128]{1,0:T(8,128)S(1)} %pack_domain.1.own_ref.raw_ref), channel_id=1, source_target_pairs={{0,448},{1,449},{2,450},{3,451},{4,452},{5,453},{6,454},{7,455},{8... | collective-permute-start | bytes 73736 | tf_op jit(solution)/shard_map/ppermute | solution.py:36
  17.8 0.7 %collective-permute-start.3 = (f32[48,128]{1,0:T(8,128)S(1)}, f32[48,128]{1,0:T(8,128)S(1)}, u32[]{:S(2)}, u32[]{:S(2)}) collective-permute-start(f32[48,128]{1,0:T(8,128)S(1)} %pack_domain.1.own_ref.raw_ref), channel_id=1, source_target_pairs={{256,320},{257,321},{258,322},{259,323},{260,324},{261,325},{262,3... | collective-permute-start | bytes 73736 | tf_op jit(solution)/shard_map/ppermute | solution.py:36
  18.4 0.0 copy-start.2
  18.4 0.0 copy-done.1
  18.4 0.0 copy-done
  18.5 0.6 %copy-done.2 = bf16[128]{0:T(256)(128)(2,1)S(1)} copy-done((bf16[128]{0:T(256)(128)(2,1)S(1)}, bf16[128]{0:T(256)(128)(2,1)}, u32[]{:S(2)}) %copy-start.2) | copy-done | bytes 280
  19.1 1.0 %place_weights.1 = (bf16[64,128]{1,0:T(8,128)(2,1)S(1)}, bf16[192,128]{1,0:T(8,128)(2,1)S(1)}, bf16[320,128]{1,0:T(8,128)(2,1)S(1)}, bf16[16,128]{1,0:T(8,128)(2,1)S(1)}) custom-call(f32[8,128]{1,0:T(8,128)} %w_rad_hbm.1, bf16[192,128]{1,0:T(8,128)(2,1)} %bitcast.7, bf16[320,128]{1,0:T(8,128)(2,1)} %w_lat_hbm.1, bf16[7,128]{1,0:T(8,128)(2,1)S(1)} %copy-done, ...), custom_call_target="tpu_custom_call" | custom-call | bytes 4000000 | tf_op jit(solution)/shard_map/place_weights/pallas_call | solution.py:682
  20.1 0.0 collective-permute-done.first_ref
  20.1 0.0 collective-permute-done.1.border_ref
  20.1 0.3 gather_early.1.early_ref
  20.4 0.0 collective-permute-done.2.cross_ref
  20.4 0.0 collective-permute-done.3.last_ref
  20.4 0.2 gather_sends.1
  20.6 3.9 %collective-permute-start.4 = (f32[48,128]{1,0:T(8,128)S(1)}, f32[48,128]{1,0:T(8,128)S(1)}, u32[]{:S(2)}, u32[]{:S(2)}) collective-permute-start(f32[48,128]{1,0:T(8,128)S(1)} %get-tuple-element.24), channel_id=1, source_target_pairs={{0,63},{1,2},{2,1},{3,4},{4,3},{5,6},{6,5},{7,8},{8,7},{9,10},{10,... | collective-permute-start | bytes 73736 | tf_op jit(solution)/shard_map/ppermute | solution.py:36
  24.5 6.5 %collective-permute-start.5 = (f32[48,128]{1,0:T(8,128)S(1)}, f32[48,128]{1,0:T(8,128)S(1)}, u32[]{:S(2)}, u32[]{:S(2)}) collective-permute-start(f32[48,128]{1,0:T(8,128)S(1)} %get-tuple-element.25), channel_id=1, source_target_pairs={{0,1},{1,0},{2,3},{3,2},{4,5},{5,4},{6,7},{7,6},{8,9},{9,8},{10,11... | collective-permute-start | bytes 73736 | tf_op jit(solution)/shard_map/ppermute | solution.py:36
  31.0 0.4 pair_columns.1
  31.4 0.0 collective-permute-done.4.refs_2_
  31.4 0.5 collective-permute-done.5.refs_3_
  31.9 5.8 %pair_terms.1 = (f32[16,128]{1,0:T(8,128)S(1)}, f32[8,128]{1,0:T(8,128)S(1)}, f32[8,128]{1,0:T(8,128)S(1)}, f32[24,128]{1,0:T(8,128)S(1)}, f32[24,128]{1,0:T(8,128)S(1)}) custom-call(f32[2,48,128]{2,1,0:T(8,128)S(1)} %get-tuple-element.22.raw_ref.refs_0_, f32[32,128]{1,0:T(8,128)S(1)} %get-tuple-element.23.refs_1_, ...), custom_call_target="tpu_custom_call" | custom-call | tf_op jit(solution)/shard_map/pair_terms/pallas_call | solution.py:741
  37.7 1.9 %collective-permute-start.6 = (f32[24,128]{1,0:T(8,128)S(1)}, f32[24,128]{1,0:T(8,128)S(1)}, u32[]{:S(2)}, u32[]{:S(2)}) collective-permute-start(f32[24,128]{1,0:T(8,128)S(1)} %get-tuple-element.32), channel_id=1, source_target_pairs={{0,63},{1,2},{2,1},{3,4},{4,3},{5,6},{6,5},{7,8},{8,7},{9,10},{10,... | collective-permute-start | bytes 36872 | tf_op jit(solution)/shard_map/ppermute | solution.py:36
  39.6 6.3 %collective-permute-start.7 = (f32[24,128]{1,0:T(8,128)S(1)}, f32[24,128]{1,0:T(8,128)S(1)}, u32[]{:S(2)}, u32[]{:S(2)}) collective-permute-start(f32[24,128]{1,0:T(8,128)S(1)} %get-tuple-element.33), channel_id=1, source_target_pairs={{0,1},{1,0},{2,3},{3,2},{4,5},{5,4},{6,7},{7,6},{8,9},{9,8},{10,11... | collective-permute-start | bytes 36872 | tf_op jit(solution)/shard_map/ppermute | solution.py:36
  45.9 0.0 collective-permute-done.6.up_ref
  46.0 0.8 %collective-permute-done.7.low_ref = f32[24,128]{1,0:T(8,128)S(1)} collective-permute-done((f32[24,128]{1,0:T(8,128)S(1)}, f32[24,128]{1,0:T(8,128)S(1)}, u32[]{:S(2)}, u32[]{:S(2)}) %collective-permute-start.7) | collective-permute-done | bytes 12320 | tf_op jit(solution)/shard_map/ppermute | solution.py:36
  46.8 0.7 %collective-permute-start.9 = (f32[24,128]{1,0:T(8,128)S(1)}, f32[24,128]{1,0:T(8,128)S(1)}, u32[]{:S(2)}, u32[]{:S(2)}) collective-permute-start(f32[24,128]{1,0:T(8,128)S(1)} %pad_maximum_fusion.1), channel_id=1, source_target_pairs={{64,128},{65,129},{66,130},{67,131},{68,132},{69,133},{70,134},{71... | collective-permute-start | bytes 36872 | tf_op jit(solution)/shard_map/ppermute | solution.py:36
  47.4 3.4 %collective-permute-start.8 = (f32[24,128]{1,0:T(8,128)S(1)}, f32[24,128]{1,0:T(8,128)S(1)}, u32[]{:S(2)}, u32[]{:S(2)}) collective-permute-start(f32[24,128]{1,0:T(8,128)S(1)} %pad_maximum_fusion), channel_id=1, source_target_pairs={{0,64},{1,65},{2,66},{3,67},{4,68},{5,69},{6,70},{7,71},{8,72},{9,... | collective-permute-start | bytes 36872 | tf_op jit(solution)/shard_map/ppermute | solution.py:36
  50.9 0.2 begin_terms.1
  51.1 0.0 collective-permute-done.9.inside_ref
  51.1 0.8 %collective-permute-done.8.beside_ref = f32[24,128]{1,0:T(8,128)S(1)} collective-permute-done((f32[24,128]{1,0:T(8,128)S(1)}, f32[24,128]{1,0:T(8,128)S(1)}, u32[]{:S(2)}, u32[]{:S(2)}) %collective-permute-start.8) | collective-permute-done | bytes 12320 | tf_op jit(solution)/shard_map/ppermute | solution.py:36
  52.0 0.8 %collect_terms.1 = (f32[3,512]{1,0:T(4,128)}, f32[1,512]{1,0:T(1,128)}) custom-call(f32[16,128]{1,0:T(8,128)S(1)} %get-tuple-element.34.total_ref, bf16[1536,128]{1,0:T(8,128)(2,1)S(1)} %get-tuple-element.35.hot_ref, f32[48,128]{1,0:T(8,128)S(1)} %pack_domain.1.own_ref.raw_ref, f32[24,128]{1,0:T(8,128)S(1)} %collective-permute-done.6.up_ref, ...), custom_call_target="tpu_custom_call" | custom-call | tf_op jit(solution)/shard_map/collect_terms/pallas_call | solution.py:769
  (4 shorter events, 0.0 us)
Async XLA Ops:
  1.3 17.2 %copy-start.1 = (bf16[7,128]{1,0:T(8,128)(2,1)S(1)}, bf16[7,128]{1,0:T(8,128)(2,1)}, u32[]{:S(2)}) copy-start(bf16[7,128]{1,0:T(8,128)(2,1)} %emb_neigh_ref.1) | copy-start | bytes 5380
  2.1 16.3 %copy-start = (bf16[7,128]{1,0:T(8,128)(2,1)S(1)}, bf16[7,128]{1,0:T(8,128)(2,1)}, u32[]{:S(2)}) copy-start(bf16[7,128]{1,0:T(8,128)(2,1)} %emb_center_ref.1) | copy-start | bytes 5380
  2.1 17.9 %collective-permute-start = (f32[48,128]{1,0:T(8,128)S(1)}, f32[48,128]{1,0:T(8,128)S(1)}, u32[]{:S(2)}, u32[]{:S(2)}) collective-permute-start(f32[48,128]{1,0:T(8,128)S(1)} %pack_domain.1.own_ref.raw_ref), channel_id=1, source_target_pairs={{0,64},{1,65},{2,66},{3,67},{4,68},{5,69},{6,70},{7,71},{8,72},{9,... | collective-permute-start | bytes 73736 | tf_op jit(solution)/shard_map/ppermute | solution.py:36
  6.1 14.0 %collective-permute-start.1 = (f32[48,128]{1,0:T(8,128)S(1)}, f32[48,128]{1,0:T(8,128)S(1)}, u32[]{:S(2)}, u32[]{:S(2)}) collective-permute-start(f32[48,128]{1,0:T(8,128)S(1)} %pack_domain.1.own_ref.raw_ref), channel_id=1, source_target_pairs={{64,448},{65,449},{66,450},{67,451},{68,452},{69,453},{70,454},{71... | collective-permute-start | bytes 73736 | tf_op jit(solution)/shard_map/ppermute | solution.py:36
  7.4 13.0 %collective-permute-start.2 = (f32[48,128]{1,0:T(8,128)S(1)}, f32[48,128]{1,0:T(8,128)S(1)}, u32[]{:S(2)}, u32[]{:S(2)}) collective-permute-start(f32[48,128]{1,0:T(8,128)S(1)} %pack_domain.1.own_ref.raw_ref), channel_id=1, source_target_pairs={{0,448},{1,449},{2,450},{3,451},{4,452},{5,453},{6,454},{7,455},{8... | collective-permute-start | bytes 73736 | tf_op jit(solution)/shard_map/ppermute | solution.py:36
  17.8 2.6 %collective-permute-start.3 = (f32[48,128]{1,0:T(8,128)S(1)}, f32[48,128]{1,0:T(8,128)S(1)}, u32[]{:S(2)}, u32[]{:S(2)}) collective-permute-start(f32[48,128]{1,0:T(8,128)S(1)} %pack_domain.1.own_ref.raw_ref), channel_id=1, source_target_pairs={{256,320},{257,321},{258,322},{259,323},{260,324},{261,325},{262,3... | collective-permute-start | bytes 73736 | tf_op jit(solution)/shard_map/ppermute | solution.py:36
  18.4 0.7 %copy-start.2 = (bf16[128]{0:T(256)(128)(2,1)S(1)}, bf16[128]{0:T(256)(128)(2,1)}, u32[]{:S(2)}) copy-start(bf16[128]{0:T(256)(128)(2,1)} %param.23) | copy-start | bytes 772
  20.6 10.8 %collective-permute-start.4 = (f32[48,128]{1,0:T(8,128)S(1)}, f32[48,128]{1,0:T(8,128)S(1)}, u32[]{:S(2)}, u32[]{:S(2)}) collective-permute-start(f32[48,128]{1,0:T(8,128)S(1)} %get-tuple-element.24), channel_id=1, source_target_pairs={{0,63},{1,2},{2,1},{3,4},{4,3},{5,6},{6,5},{7,8},{8,7},{9,10},{10,... | collective-permute-start | bytes 73736 | tf_op jit(solution)/shard_map/ppermute | solution.py:36
  24.5 7.3 %collective-permute-start.5 = (f32[48,128]{1,0:T(8,128)S(1)}, f32[48,128]{1,0:T(8,128)S(1)}, u32[]{:S(2)}, u32[]{:S(2)}) collective-permute-start(f32[48,128]{1,0:T(8,128)S(1)} %get-tuple-element.25), channel_id=1, source_target_pairs={{0,1},{1,0},{2,3},{3,2},{4,5},{5,4},{6,7},{7,6},{8,9},{9,8},{10,11... | collective-permute-start | bytes 73736 | tf_op jit(solution)/shard_map/ppermute | solution.py:36
  37.7 8.2 %collective-permute-start.6 = (f32[24,128]{1,0:T(8,128)S(1)}, f32[24,128]{1,0:T(8,128)S(1)}, u32[]{:S(2)}, u32[]{:S(2)}) collective-permute-start(f32[24,128]{1,0:T(8,128)S(1)} %get-tuple-element.32), channel_id=1, source_target_pairs={{0,63},{1,2},{2,1},{3,4},{4,3},{5,6},{6,5},{7,8},{8,7},{9,10},{10,... | collective-permute-start | bytes 36872 | tf_op jit(solution)/shard_map/ppermute | solution.py:36
  39.6 7.1 %collective-permute-start.7 = (f32[24,128]{1,0:T(8,128)S(1)}, f32[24,128]{1,0:T(8,128)S(1)}, u32[]{:S(2)}, u32[]{:S(2)}) collective-permute-start(f32[24,128]{1,0:T(8,128)S(1)} %get-tuple-element.33), channel_id=1, source_target_pairs={{0,1},{1,0},{2,3},{3,2},{4,5},{5,4},{6,7},{7,6},{8,9},{9,8},{10,11... | collective-permute-start | bytes 36872 | tf_op jit(solution)/shard_map/ppermute | solution.py:36
  46.8 4.4 %collective-permute-start.9 = (f32[24,128]{1,0:T(8,128)S(1)}, f32[24,128]{1,0:T(8,128)S(1)}, u32[]{:S(2)}, u32[]{:S(2)}) collective-permute-start(f32[24,128]{1,0:T(8,128)S(1)} %pad_maximum_fusion.1), channel_id=1, source_target_pairs={{64,128},{65,129},{66,130},{67,131},{68,132},{69,133},{70,134},{71... | collective-permute-start | bytes 36872 | tf_op jit(solution)/shard_map/ppermute | solution.py:36
  47.4 4.5 %collective-permute-start.8 = (f32[24,128]{1,0:T(8,128)S(1)}, f32[24,128]{1,0:T(8,128)S(1)}, u32[]{:S(2)}, u32[]{:S(2)}) collective-permute-start(f32[24,128]{1,0:T(8,128)S(1)} %pad_maximum_fusion), channel_id=1, source_target_pairs={{0,64},{1,65},{2,66},{3,67},{4,68},{5,69},{6,70},{7,71},{8,72},{9,... | collective-permute-start | bytes 36872 | tf_op jit(solution)/shard_map/ppermute | solution.py:36

commit v11 on v9

--- a/solution.py
+++ b/solution.py
@@ -424,10 +424,10 @@
 
     def spread_same(d, value, out_ref):
         at = domain(d)
-        value = value[:, at]
+        value = value[:, at].astype(BF16)
         for k in range(9):
             rows = of_order(value, k)
-            contrib_ref[d, feat_rows(k)] = (rows if k == 0 else rows * shape[k][:, at]).astype(BF16)
+            contrib_ref[d, feat_rows(k)] = rows if k == 0 else rows * shape_half[k][:, at]
         out_ref[d] = dot(contrib_ref[d], same_ref[d])
 
     def gathered_sums(d, in_ref):

time: 53.5 us -> 53.5 us (level)
  no operation moved by 1% of the time
where the time goes in v11:
time: 53.5 us; the launch traced here: 52.8 us
  starting transfers between devices  38.9 us (73%)
  Pallas kernels  9.37 us (18%)
  waiting for transfers between devices  2.34 us (4%)
  between operations  1.51 us (3%)
  local copies, waits for them, and re-layouts  0.65 us (1%)
    ppermute x10, starting transfers between devices, permute(): return lax.ppermute(block, AXES, route)  38.9 us
    pallas_call x1, Pallas kernels, on_device(): pl.pallas_call(lambda *refs: pair_kernel(feat, pair_len, *refs), out_shap...  5.91 us
    ppermute x10, waiting for transfers between devices, permute(): return lax.ppermute(block, AXES, route)  2.34 us
  transfers between devices with their start and end apart: 10, of which 3 were waited for; matrix products, arithmetic and copies ran while one was open for 0% of the time, Pallas kernels for 3%

profile of v11, /device:TPU:1, one launch (start us, length us, event | category | flops | bytes accessed | tf_op | source)
XLA Modules:
  0.0 52.8 jit_solution(11850530462923969944)
XLA Ops:
  1.3 0.0 copy-start.1
  1.3 0.8 %pack_domain.1.own_ref.raw_ref = f32[48,128]{1,0:T(8,128)S(1)} custom-call(f32[3,512]{1,0:T(4,128)} %pos_hbm.1, s32[1,512]{1,0:T(1,128)} %bitcast.10, s32[8,176]{1,0:T(8,128)} %lists_hbm.1, s32[6,128]{1,0:T(8,128)} %bitcast.8, s32[6,128]{1,0:T(8,128)} %bitcast.9, s32[1]{0:T(128)S(6)} %copy.14.live_ref), custom_call_target="tpu_custom_call" | custom-call | tf_op jit(solution)/shard_map/pack_domain/pallas_call | solution.py:634
  2.1 0.0 copy-start
  2.1 3.9 %collective-permute-start = (f32[48,128]{1,0:T(8,128)S(1)}, f32[48,128]{1,0:T(8,128)S(1)}, u32[]{:S(2)}, u32[]{:S(2)}) collective-permute-start(f32[48,128]{1,0:T(8,128)S(1)} %pack_domain.1.own_ref.raw_ref), channel_id=1, source_target_pairs={{0,64},{1,65},{2,66},{3,67},{4,68},{5,69},{6,70},{7,71},{8,72},{9,... | collective-permute-start | bytes 73736 | tf_op jit(solution)/shard_map/ppermute | solution.py:36
  6.1 1.3 %collective-permute-start.1 = (f32[48,128]{1,0:T(8,128)S(1)}, f32[48,128]{1,0:T(8,128)S(1)}, u32[]{:S(2)}, u32[]{:S(2)}) collective-permute-start(f32[48,128]{1,0:T(8,128)S(1)} %pack_domain.1.own_ref.raw_ref), channel_id=1, source_target_pairs={{64,448},{65,449},{66,450},{67,451},{68,452},{69,453},{70,454},{71... | collective-permute-start | bytes 73736 | tf_op jit(solution)/shard_map/ppermute | solution.py:36
  7.4 10.4 %collective-permute-start.2 = (f32[48,128]{1,0:T(8,128)S(1)}, f32[48,128]{1,0:T(8,128)S(1)}, u32[]{:S(2)}, u32[]{:S(2)}) collective-permute-start(f32[48,128]{1,0:T(8,128)S(1)} %pack_domain.1.own_ref.raw_ref), channel_id=1, source_target_pairs={{0,448},{1,449},{2,450},{3,451},{4,452},{5,453},{6,454},{7,455},{8... | collective-permute-start | bytes 73736 | tf_op jit(solution)/shard_map/ppermute | solution.py:36
  17.8 0.7 %collective-permute-start.3 = (f32[48,128]{1,0:T(8,128)S(1)}, f32[48,128]{1,0:T(8,128)S(1)}, u32[]{:S(2)}, u32[]{:S(2)}) collective-permute-start(f32[48,128]{1,0:T(8,128)S(1)} %pack_domain.1.own_ref.raw_ref), channel_id=1, source_target_pairs={{256,320},{257,321},{258,322},{259,323},{260,324},{261,325},{262,3... | collective-permute-start | bytes 73736 | tf_op jit(solution)/shard_map/ppermute | solution.py:36
  18.4 0.0 copy-start.2
  18.4 0.0 copy-done.1
  18.4 0.0 copy-done
  18.5 0.6 %copy-done.2 = bf16[128]{0:T(256)(128)(2,1)S(1)} copy-done((bf16[128]{0:T(256)(128)(2,1)S(1)}, bf16[128]{0:T(256)(128)(2,1)}, u32[]{:S(2)}) %copy-start.2) | copy-done | bytes 280
  19.1 1.0 %place_weights.1 = (bf16[64,128]{1,0:T(8,128)(2,1)S(1)}, bf16[192,128]{1,0:T(8,128)(2,1)S(1)}, bf16[320,128]{1,0:T(8,128)(2,1)S(1)}, bf16[16,128]{1,0:T(8,128)(2,1)S(1)}) custom-call(f32[8,128]{1,0:T(8,128)} %w_rad_hbm.1, bf16[192,128]{1,0:T(8,128)(2,1)} %bitcast.7, bf16[320,128]{1,0:T(8,128)(2,1)} %w_lat_hbm.1, bf16[7,128]{1,0:T(8,128)(2,1)S(1)} %copy-done, ...), custom_call_target="tpu_custom_call" | custom-call | bytes 4000000 | tf_op jit(solution)/shard_map/place_weights/pallas_call | solution.py:662
  20.1 0.0 collective-permute-done.first_ref
  20.1 0.0 collective-permute-done.1.border_ref
  20.1 0.0 collective-permute-done.2.cross_ref
  20.1 0.0 collective-permute-done.3.last_ref
  20.1 0.3 gather_sends.1
  20.4 3.9 %collective-permute-start.4 = (f32[48,128]{1,0:T(8,128)S(1)}, f32[48,128]{1,0:T(8,128)S(1)}, u32[]{:S(2)}, u32[]{:S(2)}) collective-permute-start(f32[48,128]{1,0:T(8,128)S(1)} %get-tuple-element.24), channel_id=1, source_target_pairs={{0,63},{1,2},{2,1},{3,4},{4,3},{5,6},{6,5},{7,8},{8,7},{9,10},{10,... | collective-permute-start | bytes 73736 | tf_op jit(solution)/shard_map/ppermute | solution.py:36
  24.4 6.7 %collective-permute-start.5 = (f32[48,128]{1,0:T(8,128)S(1)}, f32[48,128]{1,0:T(8,128)S(1)}, u32[]{:S(2)}, u32[]{:S(2)}) collective-permute-start(f32[48,128]{1,0:T(8,128)S(1)} %get-tuple-element.25), channel_id=1, source_target_pairs={{0,1},{1,0},{2,3},{3,2},{4,5},{5,4},{6,7},{7,6},{8,9},{9,8},{10,11... | collective-permute-start | bytes 73736 | tf_op jit(solution)/shard_map/ppermute | solution.py:36
  31.1 0.4 pair_columns.1
  31.5 0.0 collective-permute-done.4.refs_2_
  31.5 0.5 collective-permute-done.5.refs_3_
  31.9 5.9 %pair_terms.1 = (f32[16,128]{1,0:T(8,128)S(1)}, f32[8,128]{1,0:T(8,128)S(1)}, f32[8,128]{1,0:T(8,128)S(1)}, f32[24,128]{1,0:T(8,128)S(1)}, f32[24,128]{1,0:T(8,128)S(1)}) custom-call(f32[2,48,128]{2,1,0:T(8,128)S(1)} %get-tuple-element.22.raw_ref.refs_0_, f32[32,128]{1,0:T(8,128)S(1)} %get-tuple-element.23.refs_1_, ...), custom_call_target="tpu_custom_call" | custom-call | tf_op jit(solution)/shard_map/pair_terms/pallas_call | solution.py:715
  37.9 1.9 %collective-permute-start.6 = (f32[24,128]{1,0:T(8,128)S(1)}, f32[24,128]{1,0:T(8,128)S(1)}, u32[]{:S(2)}, u32[]{:S(2)}) collective-permute-start(f32[24,128]{1,0:T(8,128)S(1)} %get-tuple-element.32), channel_id=1, source_target_pairs={{0,63},{1,2},{2,1},{3,4},{4,3},{5,6},{6,5},{7,8},{8,7},{9,10},{10,... | collective-permute-start | bytes 36872 | tf_op jit(solution)/shard_map/ppermute | solution.py:36
  39.8 6.3 %collective-permute-start.7 = (f32[24,128]{1,0:T(8,128)S(1)}, f32[24,128]{1,0:T(8,128)S(1)}, u32[]{:S(2)}, u32[]{:S(2)}) collective-permute-start(f32[24,128]{1,0:T(8,128)S(1)} %get-tuple-element.33), channel_id=1, source_target_pairs={{0,1},{1,0},{2,3},{3,2},{4,5},{5,4},{6,7},{7,6},{8,9},{9,8},{10,11... | collective-permute-start | bytes 36872 | tf_op jit(solution)/shard_map/ppermute | solution.py:36
  46.1 0.0 collective-permute-done.6.up_ref
  46.1 0.8 %collective-permute-done.7.low_ref = f32[24,128]{1,0:T(8,128)S(1)} collective-permute-done((f32[24,128]{1,0:T(8,128)S(1)}, f32[24,128]{1,0:T(8,128)S(1)}, u32[]{:S(2)}, u32[]{:S(2)}) %collective-permute-start.7) | collective-permute-done | bytes 12320 | tf_op jit(solution)/shard_map/ppermute | solution.py:36
  46.9 0.7 %collective-permute-start.9 = (f32[24,128]{1,0:T(8,128)S(1)}, f32[24,128]{1,0:T(8,128)S(1)}, u32[]{:S(2)}, u32[]{:S(2)}) collective-permute-start(f32[24,128]{1,0:T(8,128)S(1)} %pad_maximum_fusion.1), channel_id=1, source_target_pairs={{64,128},{65,129},{66,130},{67,131},{68,132},{69,133},{70,134},{71... | collective-permute-start | bytes 36872 | tf_op jit(solution)/shard_map/ppermute | solution.py:36
  47.6 3.1 %collective-permute-start.8 = (f32[24,128]{1,0:T(8,128)S(1)}, f32[24,128]{1,0:T(8,128)S(1)}, u32[]{:S(2)}, u32[]{:S(2)}) collective-permute-start(f32[24,128]{1,0:T(8,128)S(1)} %pad_maximum_fusion), channel_id=1, source_target_pairs={{0,64},{1,65},{2,66},{3,67},{4,68},{5,69},{6,70},{7,71},{8,72},{9,... | collective-permute-start | bytes 36872 | tf_op jit(solution)/shard_map/ppermute | solution.py:36
  50.7 0.2 begin_terms.1
  51.0 0.0 collective-permute-done.9.inside_ref
  51.0 1.1 %collective-permute-done.8.beside_ref = f32[24,128]{1,0:T(8,128)S(1)} collective-permute-done((f32[24,128]{1,0:T(8,128)S(1)}, f32[24,128]{1,0:T(8,128)S(1)}, u32[]{:S(2)}, u32[]{:S(2)}) %collective-permute-start.8) | collective-permute-done | bytes 12320 | tf_op jit(solution)/shard_map/ppermute | solution.py:36
  52.0 0.8 %collect_terms.1 = (f32[3,512]{1,0:T(4,128)}, f32[1,512]{1,0:T(1,128)}) custom-call(f32[16,128]{1,0:T(8,128)S(1)} %get-tuple-element.34.total_ref, bf16[1536,128]{1,0:T(8,128)(2,1)S(1)} %get-tuple-element.35.hot_ref, f32[48,128]{1,0:T(8,128)S(1)} %pack_domain.1.own_ref.raw_ref, f32[24,128]{1,0:T(8,128)S(1)} %collective-permute-done.6.up_ref, ...), custom_call_target="tpu_custom_call" | custom-call | tf_op jit(solution)/shard_map/collect_terms/pallas_call | solution.py:743
  (4 shorter events, 0.0 us)
Async XLA Ops:
  1.3 17.2 %copy-start.1 = (bf16[7,128]{1,0:T(8,128)(2,1)S(1)}, bf16[7,128]{1,0:T(8,128)(2,1)}, u32[]{:S(2)}) copy-start(bf16[7,128]{1,0:T(8,128)(2,1)} %emb_neigh_ref.1) | copy-start | bytes 5380
  2.1 16.3 %copy-start = (bf16[7,128]{1,0:T(8,128)(2,1)S(1)}, bf16[7,128]{1,0:T(8,128)(2,1)}, u32[]{:S(2)}) copy-start(bf16[7,128]{1,0:T(8,128)(2,1)} %emb_center_ref.1) | copy-start | bytes 5380
  2.1 17.9 %collective-permute-start = (f32[48,128]{1,0:T(8,128)S(1)}, f32[48,128]{1,0:T(8,128)S(1)}, u32[]{:S(2)}, u32[]{:S(2)}) collective-permute-start(f32[48,128]{1,0:T(8,128)S(1)} %pack_domain.1.own_ref.raw_ref), channel_id=1, source_target_pairs={{0,64},{1,65},{2,66},{3,67},{4,68},{5,69},{6,70},{7,71},{8,72},{9,... | collective-permute-start | bytes 73736 | tf_op jit(solution)/shard_map/ppermute | solution.py:36
  6.1 14.0 %collective-permute-start.1 = (f32[48,128]{1,0:T(8,128)S(1)}, f32[48,128]{1,0:T(8,128)S(1)}, u32[]{:S(2)}, u32[]{:S(2)}) collective-permute-start(f32[48,128]{1,0:T(8,128)S(1)} %pack_domain.1.own_ref.raw_ref), channel_id=1, source_target_pairs={{64,448},{65,449},{66,450},{67,451},{68,452},{69,453},{70,454},{71... | collective-permute-start | bytes 73736 | tf_op jit(solution)/shard_map/ppermute | solution.py:36
  7.4 12.7 %collective-permute-start.2 = (f32[48,128]{1,0:T(8,128)S(1)}, f32[48,128]{1,0:T(8,128)S(1)}, u32[]{:S(2)}, u32[]{:S(2)}) collective-permute-start(f32[48,128]{1,0:T(8,128)S(1)} %pack_domain.1.own_ref.raw_ref), channel_id=1, source_target_pairs={{0,448},{1,449},{2,450},{3,451},{4,452},{5,453},{6,454},{7,455},{8... | collective-permute-start | bytes 73736 | tf_op jit(solution)/shard_map/ppermute | solution.py:36
  17.8 2.3 %collective-permute-start.3 = (f32[48,128]{1,0:T(8,128)S(1)}, f32[48,128]{1,0:T(8,128)S(1)}, u32[]{:S(2)}, u32[]{:S(2)}) collective-permute-start(f32[48,128]{1,0:T(8,128)S(1)} %pack_domain.1.own_ref.raw_ref), channel_id=1, source_target_pairs={{256,320},{257,321},{258,322},{259,323},{260,324},{261,325},{262,3... | collective-permute-start | bytes 73736 | tf_op jit(solution)/shard_map/ppermute | solution.py:36
  18.4 0.7 %copy-start.2 = (bf16[128]{0:T(256)(128)(2,1)S(1)}, bf16[128]{0:T(256)(128)(2,1)}, u32[]{:S(2)}) copy-start(bf16[128]{0:T(256)(128)(2,1)} %param.23) | copy-start | bytes 772
  20.4 11.1 %collective-permute-start.4 = (f32[48,128]{1,0:T(8,128)S(1)}, f32[48,128]{1,0:T(8,128)S(1)}, u32[]{:S(2)}, u32[]{:S(2)}) collective-permute-start(f32[48,128]{1,0:T(8,128)S(1)} %get-tuple-element.24), channel_id=1, source_target_pairs={{0,63},{1,2},{2,1},{3,4},{4,3},{5,6},{6,5},{7,8},{8,7},{9,10},{10,... | collective-permute-start | bytes 73736 | tf_op jit(solution)/shard_map/ppermute | solution.py:36
  24.4 7.6 %collective-permute-start.5 = (f32[48,128]{1,0:T(8,128)S(1)}, f32[48,128]{1,0:T(8,128)S(1)}, u32[]{:S(2)}, u32[]{:S(2)}) collective-permute-start(f32[48,128]{1,0:T(8,128)S(1)} %get-tuple-element.25), channel_id=1, source_target_pairs={{0,1},{1,0},{2,3},{3,2},{4,5},{5,4},{6,7},{7,6},{8,9},{9,8},{10,11... | collective-permute-start | bytes 73736 | tf_op jit(solution)/shard_map/ppermute | solution.py:36
  37.9 8.2 %collective-permute-start.6 = (f32[24,128]{1,0:T(8,128)S(1)}, f32[24,128]{1,0:T(8,128)S(1)}, u32[]{:S(2)}, u32[]{:S(2)}) collective-permute-start(f32[24,128]{1,0:T(8,128)S(1)} %get-tuple-element.32), channel_id=1, source_target_pairs={{0,63},{1,2},{2,1},{3,4},{4,3},{5,6},{6,5},{7,8},{8,7},{9,10},{10,... | collective-permute-start | bytes 36872 | tf_op jit(solution)/shard_map/ppermute | solution.py:36
  39.8 7.1 %collective-permute-start.7 = (f32[24,128]{1,0:T(8,128)S(1)}, f32[24,128]{1,0:T(8,128)S(1)}, u32[]{:S(2)}, u32[]{:S(2)}) collective-permute-start(f32[24,128]{1,0:T(8,128)S(1)} %get-tuple-element.33), channel_id=1, source_target_pairs={{0,1},{1,0},{2,3},{3,2},{4,5},{5,4},{6,7},{7,6},{8,9},{9,8},{10,11... | collective-permute-start | bytes 36872 | tf_op jit(solution)/shard_map/ppermute | solution.py:36
  46.9 4.0 %collective-permute-start.9 = (f32[24,128]{1,0:T(8,128)S(1)}, f32[24,128]{1,0:T(8,128)S(1)}, u32[]{:S(2)}, u32[]{:S(2)}) collective-permute-start(f32[24,128]{1,0:T(8,128)S(1)} %pad_maximum_fusion.1), channel_id=1, source_target_pairs={{64,128},{65,129},{66,130},{67,131},{68,132},{69,133},{70,134},{71... | collective-permute-start | bytes 36872 | tf_op jit(solution)/shard_map/ppermute | solution.py:36
  47.6 4.4 %collective-permute-start.8 = (f32[24,128]{1,0:T(8,128)S(1)}, f32[24,128]{1,0:T(8,128)S(1)}, u32[]{:S(2)}, u32[]{:S(2)}) collective-permute-start(f32[24,128]{1,0:T(8,128)S(1)} %pad_maximum_fusion), channel_id=1, source_target_pairs={{0,64},{1,65},{2,66},{3,67},{4,68},{5,69},{6,70},{7,71},{8,72},{9,... | collective-permute-start | bytes 36872 | tf_op jit(solution)/shard_map/ppermute | solution.py:36
